TPU v7x, 32 devices: a whole 2x2x4 slice. The times are simulated.
32 devices in a mesh: roi: 8 (over z, x), col: 4 (over y, core).
Axes of the slice: x: 2, y: 2, z: 4, core: 2. Of those that a mesh axis runs over, the one named last changes fastest.
Arguments:
- p2: bfloat16 [8, 256, 65536], P('roi', 'col'), may hold values from -120 to 120
- p3: bfloat16 [8, 256, 16384], P('roi', 'col'), may hold values from -120 to 120
- p4: bfloat16 [8, 256, 4096], P('roi', 'col'), may hold values from -120 to 120
- p5: bfloat16 [8, 256, 1024], P('roi', 'col'), may hold values from -120 to 120
- norm_gain: float32 [256], P('col'), may hold values from 0.5 to 1.5
- norm_bias: float32 [256], P('col'), may hold values from -3 to 3
- fc6_weight: bfloat16 [12544, 1024], P('roi', 'col'), may hold values from -0.0546875 to 0.0546875
- fc6_bias: float32 [1024], P('col'), may hold values from -3 to 3
- fc7_weight: bfloat16 [1024, 1024], P('roi', 'col'), may hold values from -0.1875 to 0.1875
- fc7_bias: bfloat16 [1024], P(('roi', 'col')), may hold values from -3 to 3
- cls_weight: bfloat16 [1024, 81], P(('roi', 'col')), may hold values from -0.59765625 to 0.59765625
- cls_bias: float32 [81], replicated, may hold values from -4 to 4
- box_weight: bfloat16 [1024, 4], P(('roi', 'col')), may hold values from -0.1875 to 0.1875
- box_bias: float32 [4], replicated, may hold values from -3 to 3
- roi_boxes: int32 [4, 3072], P(None, 'roi'), may hold values from 0 to 512, as said below
- roi_level: int32 [3072], P('roi'), may hold values from 0 to 3
- roi_image: int32 [3072], P('roi'), may hold values from 0 to 3
- canvas_offsets: int32 [2, 32], P(None, 'roi'), may hold values from 0 to 544, as said below
- labels: int32 [3072], P('roi'), may hold values from 0 to 80
- target_boxes: int32 [4, 3072], P(None, 'roi'), may hold values from -128 to 640, as said below
- valid: int32 [3072], P('roi'), may hold values from 0 to 1, as said below
Outputs:
- cls_loss: float32 [], replicated
- box_loss: float32 [], replicated
- decoded_boxes: float32 [4, 3072], P(None, ('roi', 'col'))
- p2_grad: float32 [8, 256, 65536], P('roi', 'col')
- p3_grad: float32 [8, 256, 16384], P('roi', 'col')
- p4_grad: float32 [8, 256, 4096], P('roi', 'col')
- p5_grad: float32 [8, 256, 1024], P('roi', 'col')
- norm_gain_grad: float32 [256], P('col')
- norm_bias_grad: float32 [256], P('col')
- fc6_weight_grad: float32 [12544, 1024], P('roi', 'col')
- fc6_bias_grad: float32 [1024], P('col')
- fc7_weight_grad: float32 [1024, 1024], P('roi', 'col')
- fc7_bias_grad: float32 [1024], P(('roi', 'col'))
- cls_weight_grad: float32 [1024, 81], P(('roi', 'col'))
- cls_bias_grad: float32 [81], replicated
- box_weight_grad: float32 [1024, 4], P(('roi', 'col'))
- box_bias_grad: float32 [4], replicated
Inputs may be any that keep to these rules, and one draw needn't show every extreme that they name: `roi_boxes`: each box has positive width and height and lies inside its image, whose content spans 480 pixels; the box side grows with the level. `canvas_offsets`: image g sits in quadrant g mod 4 of its canvas. `target_boxes`: each target box has positive width and height. The first region of each canvas is valid.
All inputs are finite; a program needn't handle non-finite values.
Results may differ from a plain program's by a relative error of at most 0.018.
Values may be sent and summed in bfloat16 or wider, within the bound.
A program may use at most 256 MiB of HBM per device.

v0:
```python
import math

import jax
import jax.numpy as jnp
from jax import lax
from jax.sharding import PartitionSpec as P

CANVAS = 1024


EPSILON = 1e-05


def axis_weights(begin_at, end_at, step_size, cell_count):
    anchor = begin_at / step_size - 0.5
    extent = (end_at - begin_at) / step_size
    fractions = (jnp.arange(14, dtype=jnp.float32) + 0.5) / 14.0
    samples = anchor[:, None] + extent[:, None] * fractions[None, :]
    grid_points = jnp.arange(cell_count, dtype=jnp.float32)
    tent_value = jnp.maximum(1.0 - jnp.abs(samples[:, :, None] - grid_points[None, None, :]), 0.0)
    return 0.5 * (tent_value[:, 0::2, :] + tent_value[:, 1::2, :])


def level_weights(region, level_idx):
    left_b, top_b, right_b, bottom_b, level_ids = region
    step_size = 4.0 * 2**level_idx
    cell_count = CANVAS // (4 * 2**level_idx)
    chosen = (level_ids == level_idx).astype(jnp.float32)
    rows_w = (axis_weights(top_b, bottom_b, step_size, cell_count) * chosen[:, None, None]).astype(
        jnp.bfloat16
    )
    cols_w = axis_weights(left_b, right_b, step_size, cell_count).astype(jnp.bfloat16)
    return (rows_w, cols_w)


def silu_slope(values):
    sigma = jax.nn.sigmoid(values)
    return sigma * (1.0 + values * (1.0 - sigma))


def contract_first(left_m, right_m):
    return lax.dot_general(
        left_m, right_m, (((0,), (0,)), ((), ())), preferred_element_type=jnp.float32
    )


def contract_last(left_m, right_m):
    return lax.dot_general(
        left_m, right_m, (((1,), (1,)), ((), ())), preferred_element_type=jnp.float32
    )


def local(
    p2,
    p3,
    p4,
    p5,
    norm_gain,
    norm_bias,
    fc6_weight,
    fc6_bias,
    fc7_weight,
    fc7_bias,
    cls_weight,
    cls_bias,
    box_weight,
    box_bias,
    roi_boxes,
    roi_level,
    roi_image,
    canvas_offsets,
    labels,
    target_boxes,
    valid,
):
    channels = p2.shape[1]
    rois = roi_level.shape[0]
    col_count = lax.axis_size("col")
    roi_count = lax.axis_size("roi")
    sides = [CANVAS // (4 * 2**level_idx) for level_idx in range(4)]
    values = [plane[0].astype(jnp.float32) for plane in (p2, p3, p4, p5)]
    pixel_total = roi_count * sum((plane.shape[1] for plane in values))
    first_sum = sum((jnp.sum(plane, axis=1) for plane in values))
    second_sum = sum((jnp.sum(plane * plane, axis=1) for plane in values))
    local_valid = jnp.sum(valid.astype(jnp.float32))
    first_sum, second_sum, valid_total = lax.psum((first_sum, second_sum, local_valid), "roi")
    mean_value = first_sum / pixel_total
    variance = second_sum / pixel_total - mean_value * mean_value
    inv_std = lax.rsqrt(variance + EPSILON)
    centred = [(plane - mean_value[:, None]) * inv_std[:, None] for plane in values]
    normed = [
        (item * norm_gain[:, None] + norm_bias[:, None])
        .astype(jnp.bfloat16)
        .reshape(channels, side, side)
        for item, side in zip(centred, sides)
    ]
    picks = roi_image[None, :] == jnp.arange(4, dtype=jnp.int32)[:, None]
    shift_x = jnp.sum(jnp.where(picks, canvas_offsets[0][:, None], 0), axis=0)
    shift_y = jnp.sum(jnp.where(picks, canvas_offsets[1][:, None], 0), axis=0)
    left_edge = (roi_boxes[0] + shift_x).astype(jnp.float32)
    top_edge = (roi_boxes[1] + shift_y).astype(jnp.float32)
    right_edge = (roi_boxes[2] + shift_x).astype(jnp.float32)
    bottom_edge = (roi_boxes[3] + shift_y).astype(jnp.float32)
    block_rows = math.gcd(rois, 64)
    block_count = rois // block_rows
    regions = tuple(
        (
            item.reshape(block_count, block_rows)
            for item in (left_edge, top_edge, right_edge, bottom_edge, roi_level)
        )
    )

    def pool_step(unused_carry, region):
        summed = jnp.zeros((block_rows, channels, 7, 7), jnp.float32)
        for level_idx in range(4):
            rows_w, cols_w = level_weights(region, level_idx)
            inner_rows = jnp.einsum(
                "riy,cyx->rixc", rows_w, normed[level_idx], preferred_element_type=jnp.float32
            ).astype(jnp.bfloat16)
            summed = summed + jnp.einsum(
                "rjx,rixc->rcij", cols_w, inner_rows, preferred_element_type=jnp.float32
            )
        return (unused_carry, summed.astype(jnp.bfloat16))

    unused_carry, pooled = lax.scan(pool_step, jnp.zeros((), jnp.int32), regions)
    pooled = pooled.reshape(rois, channels, 49)
    pooled_all = lax.all_gather(pooled, "col", axis=1, tiled=True).reshape(
        rois, channels * col_count * 49
    )
    wide_rows, deep_rows = (
        lax.all_gather(fc6_weight, "roi", axis=0, tiled=True),
        lax.all_gather(fc7_weight, "roi", axis=0, tiled=True),
    )
    pre_six = jnp.dot(pooled_all, wide_rows, preferred_element_type=jnp.float32) + fc6_bias
    hidden_six = jax.nn.silu(pre_six).astype(jnp.bfloat16)
    partial_seven = contract_last(hidden_six, deep_rows)
    sums_seven = lax.psum_scatter(
        partial_seven.astype(jnp.bfloat16), "col", scatter_dimension=0, tiled=True
    ).astype(jnp.float32)
    head_cls, head_box, bias_seven = (
        lax.all_gather(cls_weight, ("roi", "col"), axis=0, tiled=True),
        lax.all_gather(box_weight, ("roi", "col"), axis=0, tiled=True),
        lax.all_gather(fc7_bias, ("roi", "col"), axis=0, tiled=True),
    )
    pre_seven = sums_seven + bias_seven.astype(jnp.float32)
    hidden_seven = jax.nn.silu(pre_seven).astype(jnp.bfloat16)
    logits = jnp.dot(hidden_seven, head_cls, preferred_element_type=jnp.float32) + cls_bias
    deltas = jnp.dot(hidden_seven, head_box, preferred_element_type=jnp.float32) + box_bias
    quarter = rois // col_count
    first_row = lax.axis_index("col") * quarter
    mine_labels = lax.dynamic_slice_in_dim(labels, first_row, quarter)
    mine_valid = lax.dynamic_slice_in_dim(valid, first_row, quarter).astype(jnp.float32)
    mine_boxes = lax.dynamic_slice_in_dim(roi_boxes, first_row, quarter, axis=1).astype(jnp.float32)
    mine_goals = lax.dynamic_slice_in_dim(target_boxes, first_row, quarter, axis=1).astype(
        jnp.float32
    )
    prop_width = mine_boxes[2] - mine_boxes[0]
    prop_height = mine_boxes[3] - mine_boxes[1]
    prop_cx = mine_boxes[0] + 0.5 * prop_width
    prop_cy = mine_boxes[1] + 0.5 * prop_height
    goal_width = mine_goals[2] - mine_goals[0]
    goal_height = mine_goals[3] - mine_goals[1]
    goal_cx = mine_goals[0] + 0.5 * goal_width
    goal_cy = mine_goals[1] + 0.5 * goal_height
    targets = jnp.stack(
        [
            10.0 * (goal_cx - prop_cx) / prop_width,
            10.0 * (goal_cy - prop_cy) / prop_height,
            5.0 * jnp.log(goal_width / prop_width),
            5.0 * jnp.log(goal_height / prop_height),
        ],
        axis=1,
    )
    foreground = mine_valid * (mine_labels > 0).astype(jnp.float32)
    top_logit = jnp.max(logits, axis=1, keepdims=True)
    log_total = top_logit[:, 0] + jnp.log(jnp.sum(jnp.exp(logits - top_logit), axis=1))
    onehot = (mine_labels[:, None] == jnp.arange(logits.shape[1], dtype=jnp.int32)[None, :]).astype(
        jnp.float32
    )
    picked = jnp.sum(onehot * logits, axis=1)
    misfit = deltas - targets
    huber_terms = jnp.where(jnp.abs(misfit) < 1.0, 0.5 * misfit * misfit, jnp.abs(misfit) - 0.5)
    class_part = jnp.sum(mine_valid * (log_total - picked))
    box_part = jnp.sum(foreground * jnp.sum(huber_terms, axis=1))
    centre_x = prop_cx + deltas[:, 0] / 10.0 * prop_width
    centre_y = prop_cy + deltas[:, 1] / 10.0 * prop_height
    new_width = prop_width * jnp.exp(deltas[:, 2] / 5.0)
    new_height = prop_height * jnp.exp(deltas[:, 3] / 5.0)
    decoded = jnp.stack(
        [
            centre_x - 0.5 * new_width,
            centre_y - 0.5 * new_height,
            centre_x + 0.5 * new_width,
            centre_y + 0.5 * new_height,
        ]
    ) / (CANVAS // 2)
    loss_scale = rois * roi_count / valid_total
    softmax = jnp.exp(logits - log_total[:, None])
    logit_grads = (loss_scale * mine_valid[:, None] * (softmax - onehot)).astype(jnp.bfloat16)
    delta_grads = (loss_scale * foreground[:, None] * jnp.clip(misfit, -1.0, 1.0)).astype(
        jnp.bfloat16
    )
    class_bias_grad, box_bias_grad, class_sum, box_sum = lax.psum(
        (
            jnp.sum(logit_grads.astype(jnp.float32), axis=0),
            jnp.sum(delta_grads.astype(jnp.float32), axis=0),
            class_part,
            box_part,
        ),
        ("roi", "col"),
    )
    cls_loss = class_sum / valid_total
    box_loss = box_sum / valid_total
    cls_term = contract_first(hidden_seven, logit_grads)
    box_term = contract_first(hidden_seven, delta_grads)
    hidden_grads = contract_last(logit_grads, head_cls) + contract_last(delta_grads, head_box)
    pre_seven_grads = (hidden_grads * silu_slope(pre_seven)).astype(jnp.bfloat16)
    seven_bias_term = jnp.sum(pre_seven_grads.astype(jnp.float32), axis=0)
    cls_weight_grad, box_weight_grad, fc7_bias_grad = (
        lax.psum_scatter(cls_term, ("roi", "col"), scatter_dimension=0, tiled=True),
        lax.psum_scatter(box_term, ("roi", "col"), scatter_dimension=0, tiled=True),
        lax.psum_scatter(seven_bias_term, ("roi", "col"), scatter_dimension=0, tiled=True),
    )
    seven_grads_all = lax.all_gather(pre_seven_grads, "col", axis=0, tiled=True)
    deep_term = contract_first(seven_grads_all, hidden_six)
    six_hidden_grads = jnp.dot(seven_grads_all, deep_rows, preferred_element_type=jnp.float32)
    pre_six_grads = (six_hidden_grads * silu_slope(pre_six)).astype(jnp.bfloat16)
    wide_term = contract_first(pooled_all, pre_six_grads)
    fc6_weight_grad, fc7_weight_grad = (
        lax.psum_scatter(wide_term, "roi", scatter_dimension=0, tiled=True),
        lax.psum_scatter(deep_term, "roi", scatter_dimension=0, tiled=True),
    )
    partial_pool = contract_last(pre_six_grads, wide_rows).reshape(rois, channels * col_count, 49)
    pool_grads = lax.psum_scatter(
        partial_pool.astype(jnp.bfloat16), "col", scatter_dimension=1, tiled=True
    ).astype(jnp.float32)
    pool_grads = pool_grads.astype(jnp.bfloat16).reshape(block_count, block_rows, channels, 7, 7)

    def unpool_step(map_grads, item):
        region, block_grads = item
        updated = []
        for level_idx in range(4):
            rows_w, cols_w = level_weights(region, level_idx)
            inner_grads = jnp.einsum(
                "rcij,rjx->rixc", block_grads, cols_w, preferred_element_type=jnp.float32
            ).astype(jnp.bfloat16)
            updated.append(
                map_grads[level_idx]
                + jnp.einsum(
                    "riy,rixc->cyx", rows_w, inner_grads, preferred_element_type=jnp.float32
                )
            )
        return (tuple(updated), None)

    start_grads = tuple((jnp.zeros((channels, side, side), jnp.float32) for side in sides))
    map_grads, unused_rows = lax.scan(unpool_step, start_grads, (regions, pool_grads))
    flat_grads = [
        grad_map.reshape(channels, side * side) for grad_map, side in zip(map_grads, sides)
    ]
    gain_part = sum(
        (jnp.sum(grad_map * item, axis=1) for grad_map, item in zip(flat_grads, centred))
    )
    shift_part = sum((jnp.sum(grad_map, axis=1) for grad_map in flat_grads))
    six_bias_part = jnp.sum(pre_six_grads.astype(jnp.float32), axis=0)
    norm_gain_grad, norm_bias_grad, fc6_bias_grad = lax.psum(
        (gain_part, shift_part, six_bias_part), "roi"
    )
    scale_col = (norm_gain * inv_std)[:, None]
    input_grads = [
        (
            scale_col
            * (
                grad_map
                - (norm_bias_grad / pixel_total)[:, None]
                - item * (norm_gain_grad / pixel_total)[:, None]
            )
        )[None]
        for grad_map, item in zip(flat_grads, centred)
    ]
    return (
        cls_loss,
        box_loss,
        decoded,
        input_grads[0],
        input_grads[1],
        input_grads[2],
        input_grads[3],
        norm_gain_grad,
        norm_bias_grad,
        fc6_weight_grad,
        fc6_bias_grad,
        fc7_weight_grad,
        fc7_bias_grad,
        cls_weight_grad,
        class_bias_grad,
        box_weight_grad,
        box_bias_grad,
    )


def solution(mesh):
    return jax.shard_map(
        local,
        mesh=mesh,
        in_specs=(
            P("roi", "col", None),
            P("roi", "col", None),
            P("roi", "col", None),
            P("roi", "col", None),
            P("col"),
            P("col"),
            P("roi", "col"),
            P("col"),
            P("roi", "col"),
            P(("roi", "col")),
            P(("roi", "col"), None),
            P(),
            P(("roi", "col"), None),
            P(),
            P(None, "roi"),
            P("roi"),
            P("roi"),
            P(None, "roi"),
            P("roi"),
            P(None, "roi"),
            P("roi"),
        ),
        out_specs=(
            P(),
            P(),
            P(None, ("roi", "col")),
            P("roi", "col", None),
            P("roi", "col", None),
            P("roi", "col", None),
            P("roi", "col", None),
            P("col"),
            P("col"),
            P("roi", "col"),
            P("col"),
            P("roi", "col"),
            P(("roi", "col")),
            P(("roi", "col"), None),
            P(),
            P(("roi", "col"), None),
            P(),
        ),
        check_vma=False,
    )
```

profile of v0, /device:TPU:12, one launch (start us, length us, event | category | flops | bytes accessed | tf_op | source)
XLA Modules:
  0.0 2122.2 jit_solution(15909105103889117558)
XLA Ops:
  23.6 19.8 all-reduce.4
  82.6 17.4 copy.165
  122.2 774.5 %while.33 = (s32[]{:T(128)}, bf16[6,64,64,7,7]{2,4,3,1,0:T(8,128)(2,1)}, f32[6,64]{1,0:T(8,128)S(1)}, f32[6,64]{1,0:T(8,128)S(1)}, s32[6,64]{1,0:T(8,128)S(1)}, ...) while((s32[]{:T(128)}, ...), condition=%wide.region_13.14_spmd, body=%wide.region_12.13_spmd.sunk | while | flops 5203210240 | bytes 103432640 | solution.py:125
  162.0 16.3 fusion.234
  180.4 16.2 fusion.238
  209.6 35.0 %fusion.236 = f32[64,7,64,7]{2,3,1,0:T(8,128)} fusion(bf16[64,7,256,64]{2,0,3,1:T(8,128)(2,1)} %convert_bitcast_fusion.19, f32[64,7,256]{2,1,0:T(8,128)S(1)} %copy-done.8, f32[64,7,256]{2,1,0:T(8,128)S(1)} %copy-done.7), kind=kOutput, calls=%fused_computation.clone.1 | convolution fusion | flops 103104512 | bytes 16400384 | tf_op jit(solution)/shard_map/while/body/eval_jaxpr/rjx,rixc->rcij/dot_general | solution.py:120
  289.5 16.4 fusion.234
  308.0 16.2 fusion.238
  337.2 35.0 %fusion.236 = f32[64,7,64,7]{2,3,1,0:T(8,128)} fusion(bf16[64,7,256,64]{2,0,3,1:T(8,128)(2,1)} %convert_bitcast_fusion.19, f32[64,7,256]{2,1,0:T(8,128)S(1)} %copy-done.8, f32[64,7,256]{2,1,0:T(8,128)S(1)} %copy-done.7), kind=kOutput, calls=%fused_computation.clone.1 | convolution fusion | flops 103104512 | bytes 16400384 | tf_op jit(solution)/shard_map/while/body/eval_jaxpr/rjx,rixc->rcij/dot_general | solution.py:120
  417.2 16.4 fusion.234
  435.7 16.2 fusion.238
  464.9 35.0 %fusion.236 = f32[64,7,64,7]{2,3,1,0:T(8,128)} fusion(bf16[64,7,256,64]{2,0,3,1:T(8,128)(2,1)} %convert_bitcast_fusion.19, f32[64,7,256]{2,1,0:T(8,128)S(1)} %copy-done.8, f32[64,7,256]{2,1,0:T(8,128)S(1)} %copy-done.7), kind=kOutput, calls=%fused_computation.clone.1 | convolution fusion | flops 103104512 | bytes 16400384 | tf_op jit(solution)/shard_map/while/body/eval_jaxpr/rjx,rixc->rcij/dot_general | solution.py:120
  544.8 16.4 fusion.234
  563.2 16.2 fusion.238
  592.4 35.0 %fusion.236 = f32[64,7,64,7]{2,3,1,0:T(8,128)} fusion(bf16[64,7,256,64]{2,0,3,1:T(8,128)(2,1)} %convert_bitcast_fusion.19, f32[64,7,256]{2,1,0:T(8,128)S(1)} %copy-done.8, f32[64,7,256]{2,1,0:T(8,128)S(1)} %copy-done.7), kind=kOutput, calls=%fused_computation.clone.1 | convolution fusion | flops 103104512 | bytes 16400384 | tf_op jit(solution)/shard_map/while/body/eval_jaxpr/rjx,rixc->rcij/dot_general | solution.py:120
  672.4 16.4 fusion.234
  690.9 16.2 fusion.238
  720.1 35.0 %fusion.236 = f32[64,7,64,7]{2,3,1,0:T(8,128)} fusion(bf16[64,7,256,64]{2,0,3,1:T(8,128)(2,1)} %convert_bitcast_fusion.19, f32[64,7,256]{2,1,0:T(8,128)S(1)} %copy-done.8, f32[64,7,256]{2,1,0:T(8,128)S(1)} %copy-done.7), kind=kOutput, calls=%fused_computation.clone.1 | convolution fusion | flops 103104512 | bytes 16400384 | tf_op jit(solution)/shard_map/while/body/eval_jaxpr/rjx,rixc->rcij/dot_general | solution.py:120
  800.0 16.4 fusion.234
  818.5 16.2 fusion.238
  847.7 35.0 %fusion.236 = f32[64,7,64,7]{2,3,1,0:T(8,128)} fusion(bf16[64,7,256,64]{2,0,3,1:T(8,128)(2,1)} %convert_bitcast_fusion.19, f32[64,7,256]{2,1,0:T(8,128)S(1)} %copy-done.8, f32[64,7,256]{2,1,0:T(8,128)S(1)} %copy-done.7), kind=kOutput, calls=%fused_computation.clone.1 | convolution fusion | flops 103104512 | bytes 16400384 | tf_op jit(solution)/shard_map/while/body/eval_jaxpr/rjx,rixc->rcij/dot_general | solution.py:120
  915.8 31.5 %all_gather.23 = bf16[1024,256]{1,0:T(8,128)(2,1)S(1)} all-gather(bf16[128,256]{1,0:T(8,128)(2,1)S(1)} %copy-done.26), channel_id=1, replica_groups=mesh['roi'=8,'col'=4] {'roi'}, dimensions={0}, use_global_device_ids=true | all-gather | bytes 589824 | tf_op jit(solution)/shard_map/all_gather | solution.py:132
  947.3 32.2 %all-gather.4.cloned.1.call-done = bf16[384,256,49]{0,1,2:T(8,128)(2,1)} async-done(((bf16[384,64,49]{0,1,2:T(8,128)(2,1)}), bf16[384,256,49]{0,1,2:T(8,128)(2,1)}) %all-gather.4.cloned.1.call-update) | async-done | bytes 9633808 | tf_op jit(solution)/shard_map/all_gather | solution.py:127
  991.7 14.0 reshape.1959
  1005.7 76.1 %all-gather.6.cloned.1.call-done = bf16[12544,256]{1,0:T(8,128)(2,1)} async-done(((bf16[1568,256]{1,0:T(8,128)(2,1)}), bf16[12544,256]{1,0:T(8,128)(2,1)}) %all-gather.6.cloned.1.call-update) | async-done | bytes 6422544 | tf_op jit(solution)/shard_map/all_gather | solution.py:131
  1092.5 40.5 %all-reduce = bf16[1024]{0:T(1024)(128)(2,1)S(1)} all-reduce(bf16[1024]{0:T(1024)(128)(2,1)S(1)} %dynamic-update-slice), channel_id=1, replica_groups=mesh['roi'=8,'col'=4] {'roi','col'}, use_global_device_ids=true, to_apply=%add | all-reduce | flops 1024 | bytes 4096
  1133.0 29.9 %all-gather = bf16[32,32,4]{1,2,0:T(4,128)(2,1)S(1)} all-gather(bf16[1,32,4]{1,2,0:T(4,128)(2,1)S(1)} %bitcast.450), channel_id=1, replica_groups=mesh['roi'=8,'col'=4] {'roi','col'}, dimensions={0}, use_global_device_ids=true | all-gather | bytes 8448 | tf_op jit(solution)/shard_map/all_gather | solution.py:142
  1163.8 41.9 %all_gather.25 = bf16[1024,81]{1,0:T(8,128)(2,1)S(1)} all-gather(bf16[32,81]{1,0:T(8,128)(2,1)S(1)} %copy-done.43), channel_id=1, replica_groups=mesh['roi'=8,'col'=4] {'roi','col'}, dimensions={0}, use_global_device_ids=true | all-gather | bytes 171072 | tf_op jit(solution)/shard_map/all_gather | solution.py:141
  1244.4 13.9 convert_element_type.428
  1261.4 46.1 %all-reduce.2 = (f32[]{:T(128)}, f32[]{:T(128)}, f32[1024]{0:T(1024)S(1)}, f32[81]{0:T(128)}, f32[4]{0:T(128)}) all-reduce(f32[]{:T(128)} %get-tuple-element.593, f32[]{:T(128)} %get-tuple-element.592, f32[1024]{0:T(1024)S(1)} %get-tuple-element.766, f32[81]{0:T(128)S(1)} %get-tuple-element.677, ...), channel_id=1, replica_groups=mesh['roi'=8,'col'=4] {'roi','col'}, use_global_device_ids=true, to_apply=%region_19.20 | all-reduce | flops 1111 | bytes 8888 | tf_op jit(solution)/shard_map/psum | solution.py:203
  1326.0 108.8 %reduce-scatter.11.cloned.1.call-done = bf16[384,64,49]{0,2,1:T(8,128)(2,1)} async-done(((bf16[384,256,49]{0,2,1:T(8,128)(2,1)}), bf16[384,64,49]{0,2,1:T(8,128)(2,1)}) %reduce-scatter.11.cloned.1.call-update) | async-done | bytes 2408464 | tf_op jit(solution)/shard_map/reduce_scatter | solution.py:234
  1452.2 549.1 %while.34 = (s32[]{:T(128)}, f32[64,256,256]{1,2,0:T(8,128)}, f32[64,128,128]{1,2,0:T(8,128)}, f32[64,64,64]{1,0,2:T(8,128)}, f32[64,32,32]{0,1,2:T(8,128)S(1)},...) while((s32[]{:T(128)}, f32[64,256,256]{1,2,0:T(8,128)}, ...), condition=%wide.region_27.28_spmd.clone, body=%wide.region_26.27_spmd.clone.sunk | while | flops 5213548544 | bytes 129337456 | solution.py:256
  1475.7 17.6 bitcast_add_fusion.11
  1500.6 38.0 %bitcast_add_fusion.10 = f32[64,256,256]{1,2,0:T(8,128)} fusion(f32[64,256,256]{1,2,0:T(8,128)} %get-tuple-element.1092, pred[]{:T(512)S(6)} %compare.3, bf16[64,7,256,64]{2,3,1,0:T(8,128)(2,1)} %convert_bitcast_fusion.21, f32[64,14,256]{2,0,1:T(8,128)S(1)} %subtract_maximum_fusion.41, f32[64]{0:T(128)S(1)} %get-tuple-element.1032), kind=kOutput, calls=%fused_computation.91.clone.1 | convolution fusion | flops 3766829056 | bytes 49152256 | tf_op jit(solution)/shard_map/while/body/eval_jaxpr/riy,rixc->cyx/dot_general | solution.py:249
  1562.0 19.8 bitcast_add_fusion.11
  1589.1 40.7 %bitcast_add_fusion.10 = f32[64,256,256]{1,2,0:T(8,128)} fusion(f32[64,256,256]{1,2,0:T(8,128)} %get-tuple-element.1092, pred[]{:T(512)S(6)} %compare.3, bf16[64,7,256,64]{2,3,1,0:T(8,128)(2,1)} %convert_bitcast_fusion.21, f32[64,14,256]{2,0,1:T(8,128)S(1)} %subtract_maximum_fusion.41, f32[64]{0:T(128)S(1)} %get-tuple-element.1032), kind=kOutput, calls=%fused_computation.91.clone.1 | convolution fusion | flops 3766829056 | bytes 49152256 | tf_op jit(solution)/shard_map/while/body/eval_jaxpr/riy,rixc->cyx/dot_general | solution.py:249
  1653.3 19.8 bitcast_add_fusion.11
  1680.5 40.7 %bitcast_add_fusion.10 = f32[64,256,256]{1,2,0:T(8,128)} fusion(f32[64,256,256]{1,2,0:T(8,128)} %get-tuple-element.1092, pred[]{:T(512)S(6)} %compare.3, bf16[64,7,256,64]{2,3,1,0:T(8,128)(2,1)} %convert_bitcast_fusion.21, f32[64,14,256]{2,0,1:T(8,128)S(1)} %subtract_maximum_fusion.41, f32[64]{0:T(128)S(1)} %get-tuple-element.1032), kind=kOutput, calls=%fused_computation.91.clone.1 | convolution fusion | flops 3766829056 | bytes 49152256 | tf_op jit(solution)/shard_map/while/body/eval_jaxpr/riy,rixc->cyx/dot_general | solution.py:249
  1744.7 19.8 bitcast_add_fusion.11
  1771.8 40.5 %bitcast_add_fusion.10 = f32[64,256,256]{1,2,0:T(8,128)} fusion(f32[64,256,256]{1,2,0:T(8,128)} %get-tuple-element.1092, pred[]{:T(512)S(6)} %compare.3, bf16[64,7,256,64]{2,3,1,0:T(8,128)(2,1)} %convert_bitcast_fusion.21, f32[64,14,256]{2,0,1:T(8,128)S(1)} %subtract_maximum_fusion.41, f32[64]{0:T(128)S(1)} %get-tuple-element.1032), kind=kOutput, calls=%fused_computation.91.clone.1 | convolution fusion | flops 3766829056 | bytes 49152256 | tf_op jit(solution)/shard_map/while/body/eval_jaxpr/riy,rixc->cyx/dot_general | solution.py:249
  1835.8 19.8 bitcast_add_fusion.11
  1862.9 40.5 %bitcast_add_fusion.10 = f32[64,256,256]{1,2,0:T(8,128)} fusion(f32[64,256,256]{1,2,0:T(8,128)} %get-tuple-element.1092, pred[]{:T(512)S(6)} %compare.3, bf16[64,7,256,64]{2,3,1,0:T(8,128)(2,1)} %convert_bitcast_fusion.21, f32[64,14,256]{2,0,1:T(8,128)S(1)} %subtract_maximum_fusion.41, f32[64]{0:T(128)S(1)} %get-tuple-element.1032), kind=kOutput, calls=%fused_computation.91.clone.1 | convolution fusion | flops 3766829056 | bytes 49152256 | tf_op jit(solution)/shard_map/while/body/eval_jaxpr/riy,rixc->cyx/dot_general | solution.py:249
  1926.8 19.8 bitcast_add_fusion.11
  1953.9 40.5 %bitcast_add_fusion.10 = f32[64,256,256]{1,2,0:T(8,128)} fusion(f32[64,256,256]{1,2,0:T(8,128)} %get-tuple-element.1092, pred[]{:T(512)S(6)} %compare.3, bf16[64,7,256,64]{2,3,1,0:T(8,128)(2,1)} %convert_bitcast_fusion.21, f32[64,14,256]{2,0,1:T(8,128)S(1)} %subtract_maximum_fusion.41, f32[64]{0:T(128)S(1)} %get-tuple-element.1032), kind=kOutput, calls=%fused_computation.91.clone.1 | convolution fusion | flops 3766829056 | bytes 49152256 | tf_op jit(solution)/shard_map/while/body/eval_jaxpr/riy,rixc->cyx/dot_general | solution.py:249
  2010.4 17.4 copy.178
  2047.9 19.2 all-reduce.3
  2076.0 14.7 reshape.1961
  2098.5 14.4 subtract_multiply_fusion
  (850 shorter events, 777.9 us)
Async XLA Ops:
  7.2 972.3 %all-gather.4.cloned.1.call-start = ((), (), s32[]{:S(2)}) async-start(), calls=%async_computation.6 | async-start | bytes 12042240 | tf_op jit(solution)/shard_map/all_gather | solution.py:127
  16.2 27.1 %copy-start.39 = (f32[64]{0:T(128)S(1)}, f32[64]{0:T(128)}, u32[]{:S(2)}) copy-start(f32[64]{0:T(128)} %param.29) | copy-start | bytes 772
  16.3 27.7 %copy-start.42 = (f32[64]{0:T(128)S(1)}, f32[64]{0:T(128)}, u32[]{:S(2)}) copy-start(f32[64]{0:T(128)} %param.30) | copy-start | bytes 772
  23.4 21.5 %copy-start.16 = (bf16[1,64,1024]{1,2,0:T(8,128)(2,1)}, bf16[1,64,1024]{1,2,0:T(8,128)(2,1)S(1)}, u32[]{:S(2)}) copy-start(bf16[1,64,1024]{1,2,0:T(8,128)(2,1)S(1)} %copy.164) | copy-start | bytes 393220
  43.9 56.1 %copy-start.22 = (f32[64]{0:T(128)}, f32[64]{0:T(128)S(1)}, u32[]{:S(2)}) copy-start(f32[64]{0:T(128)S(1)} %get-tuple-element.759) | copy-start | bytes 772
  43.9 56.1 %copy-start.24 = (f32[64]{0:T(128)}, f32[64]{0:T(128)S(1)}, u32[]{:S(2)}) copy-start(f32[64]{0:T(128)S(1)} %get-tuple-element.762) | copy-start | bytes 772
  146.8 13.1 copy-start.3
  196.6 13.0 copy-start.7
  196.6 13.0 copy-start.8
  274.3 13.1 copy-start.3
  324.2 13.0 copy-start.7
  324.2 13.0 copy-start.8
  401.9 13.1 copy-start.3
  451.8 13.0 copy-start.7
  451.8 13.0 copy-start.8
  529.5 13.1 copy-start.3
  579.4 13.0 copy-start.7
  579.4 13.0 copy-start.8
  657.2 13.1 copy-start.3
  707.1 13.0 copy-start.7
  707.1 13.0 copy-start.8
  784.8 13.1 copy-start.3
  834.7 13.0 copy-start.7
  834.7 13.0 copy-start.8
  896.7 9.4 copy-start.29
  906.2 9.6 copy-start.26
  915.0 166.8 %all-gather.6.cloned.1.call-start = ((), (), s32[]{:S(2)}) async-start(), calls=%async_computation.7 | async-start | bytes 7225344 | tf_op jit(solution)/shard_map/all_gather | solution.py:131
  915.7 292.3 %reduce-scatter.9.cloned.1.call-start = ((), (), s32[]{:S(2)}) async-start(), calls=%async_computation.8 | async-start | bytes 983040 | tf_op jit(solution)/shard_map/reduce_scatter | solution.py:137
  991.7 90.2 %copy-start.47 = (f32[256]{0:T(256)S(1)}, f32[256]{0:T(256)}, u32[]{:S(2)}) copy-start(f32[256]{0:T(256)} %param.32) | copy-start | bytes 3076
  1005.7 86.6 %copy-start.52 = (bf16[32]{0:T(256)(128)(2,1)S(1)}, bf16[32]{0:T(256)(128)(2,1)}, u32[]{:S(2)}) copy-start(bf16[32]{0:T(256)(128)(2,1)} %param.34) | copy-start | bytes 196
  1005.7 127.4 %copy-start.48 = (bf16[32,4]{0,1:T(4,128)(2,1)S(1)}, bf16[32,4]{0,1:T(4,128)(2,1)}, u32[]{:S(2)}) copy-start(bf16[32,4]{0,1:T(4,128)(2,1)} %param.37) | copy-start | bytes 772
  1005.7 158.1 %copy-start.43 = (bf16[32,81]{1,0:T(8,128)(2,1)S(1)}, bf16[32,81]{1,0:T(8,128)(2,1)}, u32[]{:S(2)}) copy-start(bf16[32,81]{1,0:T(8,128)(2,1)} %param.35) | copy-start | bytes 15556
  1005.7 203.4 %copy-start.53 = (f32[4]{0:T(128)S(1)}, f32[4]{0:T(128)}, u32[]{:S(2)}) copy-start(f32[4]{0:T(128)} %param.38) | copy-start | bytes 52
  1090.8 119.9 %copy-start.51 = (f32[81]{0:T(128)S(1)}, f32[81]{0:T(128)}, u32[]{:S(2)}) copy-start(f32[81]{0:T(128)} %param.36) | copy-start | bytes 976
  1092.2 232.5 %reduce-scatter.19.cloned.1.call-start = ((), (), s32[]{:S(2)}) async-start(), calls=%async_computation.13 | async-start | bytes 540672
  1210.7 224.1 %reduce-scatter.11.cloned.1.call-start = ((), (), s32[]{:S(2)}) async-start(), calls=%async_computation.9 | async-start | bytes 13762560 | tf_op jit(solution)/shard_map/reduce_scatter | solution.py:234
  1210.7 13.4 copy-start.1
  1258.3 854.6 %reduce-scatter.17.cloned.1.call-start = ((), (), s32[]{:S(2)}) async-start(), calls=%async_computation.12 | async-start | bytes 540672 | tf_op jit(solution)/shard_map/reduce_scatter | solution.py:220
  1259.7 853.2 %reduce-scatter.15.cloned.1.call-start = ((), (), s32[]{:S(2)}) async-start(), calls=%async_computation.11 | async-start | bytes 1179648 | tf_op jit(solution)/shard_map/reduce_scatter | solution.py:231
  1261.3 851.6 %reduce-scatter.13.cloned.1.call-start = ((), (), s32[]{:S(2)}) async-start(), calls=%async_computation.10 | async-start | bytes 14450688 | tf_op jit(solution)/shard_map/reduce_scatter | solution.py:230
  2010.4 17.6 copy-start.23
  2010.4 17.6 copy-start.25
  2035.4 12.1 copy-start.18
  2035.4 12.5 copy-start.50
  2035.4 31.7 %copy-start.17 = (bf16[1,64,1024]{1,2,0:T(8,128)(2,1)S(1)}, bf16[1,64,1024]{1,2,0:T(8,128)(2,1)}, u32[]{:S(2)}) copy-start(bf16[1,64,1024]{1,2,0:T(8,128)(2,1)} %copy-done.16) | copy-start | bytes 393220
  2035.5 31.7 %copy-start.40 = (f32[64]{0:T(128)S(1)}, f32[64]{0:T(128)}, u32[]{:S(2)}) copy-start(f32[64]{0:T(128)} %get-tuple-element.758) | copy-start | bytes 772
  2076.0 14.8 copy-start.15
  2076.0 17.3 copy-start.5
  (106 other events, 353.0 us)
Sparse Core Ops, SparseCore 0:
  915.1 64.3 all-gather.3
  981.7 100.0 all-gather.5
  1092.3 22.0 reduce-scatter.8
  1210.8 113.7 reduce-scatter.18
  1327.1 107.7 reduce-scatter.10
  1437.5 110.6 reduce-scatter.16
  1552.6 83.1 reduce-scatter.14
  1640.0 208.4 reduce-scatter.12
where the time goes:
time: 2140 us; the launch traced here: 2120 us
  matrix products  1110 us (52%)
  local copies, waits for them, and re-layouts  377 us (18%)
  blocking collectives  238 us (11%)
  waiting for transfers between devices  219 us (10%)
  other arithmetic  137 us (6%)
  loops' own time  22.5 us (1%)
    dot_general x24, matrix products, pool_step(): jnp.einsum('rjx,rixc->rcij', cols_w, inner_rows, preferred_element_type=j...  438 us
    dot_general x24, matrix products, unpool_step(): jnp.einsum('riy,rixc->cyx', rows_w, inner_grads, preferred_element_type=j...  427 us
    dot_general x24, matrix products, pool_step(): jnp.einsum('riy,cyx->rixc', rows_w, normed[level_idx], preferred_element_...  128 us
    reduce_scatter x1, waiting for transfers between devices, local(): lax.psum_scatter(partial_pool.astype(jnp.bfloat16), 'col', scatter_dimens...  109 us
    slice x72, local copies, waits for them, and re-layouts, axis_weights(): return 0.5 * (tent_value[:, 0::2, :] + tent_value[:, 1::2, :])  92.8 us
    dot_general x24, matrix products, unpool_step(): jnp.einsum('rcij,rjx->rixc', block_grads, cols_w, preferred_element_type=...  78.3 us
    all_gather x1, waiting for transfers between devices, local(): lax.all_gather(fc6_weight, 'roi', axis=0, tiled=True)  76.1 us
    convert_element_type x6, local copies, waits for them, and re-layouts, pool_step(): inner_rows = jnp.einsum('riy,cyx->rixc', rows_w, normed[level_idx], prefe...  53.6 us
  transfers between devices with their start and end apart: 8, of which 4 were waited for; matrix products, arithmetic and copies ran while one was open for 34% of the time, Pallas kernels for 0%

commit v1 on v0

v1 whole, which is shorter than its diff:
```python
import functools
import math

import jax
import jax.numpy as jnp
from jax import lax
from jax.experimental import pallas as pl
from jax.experimental.pallas import tpu as pltpu
from jax.sharding import PartitionSpec as P

CANVAS = 1024
EPSILON = 1e-05
LANES = 128
SPAN = 10
PAIR = 2
SIDES = tuple(CANVAS // (4 * 2**level) for level in range(4))
TILES = tuple(side * side // LANES for side in SIDES)
FIRST = tuple(sum(TILES[:level]) for level in range(4))
ALL_TILES = sum(TILES)
PADDED = ALL_TILES + max(SPAN - min(TILES), 0)
SLOTS = 32
USED = tuple(slot for slot in range(SLOTS) if slot % 8 < 7)
WIDE = len(USED) * LANES
F32_FIELDS = 7
I32_FIELDS = 6


def silu_slope(values):
    sigma = jax.nn.sigmoid(values)
    return sigma * (1.0 + values * (1.0 - sigma))


def contract_first(left_m, right_m):
    return lax.dot_general(
        left_m, right_m, (((0,), (0,)), ((), ())), preferred_element_type=jnp.float32
    )


def contract_last(left_m, right_m):
    return lax.dot_general(
        left_m, right_m, (((1,), (1,)), ((), ())), preferred_element_type=jnp.float32
    )


def region_tables(left, top, right, bottom, level):
    def by_level(values):
        chosen = jnp.full(level.shape, values[0])
        for at in range(1, 4):
            chosen = jnp.where(level == at, values[at], chosen)
        return chosen

    step = by_level([4.0 * 2**at for at in range(4)])
    side = by_level(list(SIDES))
    rows_log = by_level([(max(LANES // n, 1)).bit_length() - 1 for n in SIDES])
    across = by_level([max(n // LANES, 1) for n in SIDES])
    x_anchor, x_extent = left / step - 0.5, (right - left) / step
    y_anchor, y_extent = top / step - 0.5, (bottom - top) / step

    def window(anchor, extent):
        low = jnp.floor(anchor + extent * (0.5 / 14.0)).astype(jnp.int32)
        high = jnp.floor(anchor + extent * (13.5 / 14.0)).astype(jnp.int32) + 1
        return jnp.clip(low, 0, side - 1), jnp.clip(high, 0, side - 1)

    y_low, y_high = window(y_anchor, y_extent)
    x_low, x_high = window(x_anchor, x_extent)
    group_low, group_high = y_low >> rows_log, y_high >> rows_log
    chunks = (group_high - group_low + SPAN) // SPAN
    group = jnp.maximum(jnp.minimum(group_low, (side >> rows_log) - chunks * SPAN), 0)
    tile_x = x_low // LANES
    tiles_x = x_high // LANES - tile_x + 1
    first_tile = by_level(list(FIRST)) + group * across + tile_x
    mask = jnp.minimum(side, LANES) - 1
    shift = 7 - rows_log
    rows_per = (1 << rows_log).astype(jnp.float32)
    floats = jnp.stack(
        [
            x_anchor,
            x_extent,
            y_anchor,
            y_extent,
            (tile_x * LANES).astype(jnp.float32),
            group.astype(jnp.float32) * rows_per,
            rows_per,
        ]
    ).astype(jnp.float32)
    ints = jnp.stack([first_tile, across, mask, shift, chunks, tiles_x]).astype(jnp.int32)
    return floats.reshape(-1), ints.reshape(-1)


def window_weights(floats, ints, rois, region, chunk, tile_x):
    x_anchor, x_extent, y_anchor, y_extent, x_origin, y_origin, rows_per = (
        floats[at * rois + region] for at in range(F32_FIELDS)
    )
    first_tile, across, mask, shift = (ints[at * rois + region] for at in range(4))
    if chunk is not None:
        first_tile = first_tile + chunk * (SPAN * across) + tile_x
        x_origin = x_origin + (tile_x * LANES).astype(jnp.float32)
        y_origin = y_origin + (chunk * SPAN).astype(jnp.float32) * rows_per
    lane = lax.broadcasted_iota(jnp.int32, (8, LANES), 1)
    bin_at = lax.broadcasted_iota(jnp.int32, (8, LANES), 0)
    x_cell = (lane & mask).astype(jnp.float32) + x_origin
    y_cell = lax.shift_right_logical(lane, jnp.broadcast_to(shift, lane.shape)).astype(
        jnp.float32
    ) + y_origin
    part = jnp.where(bin_at < 7, (2.0 * bin_at.astype(jnp.float32) + 0.5) / 14.0, -1e6)
    near = y_anchor + y_extent * part - y_cell
    far = y_anchor + y_extent * (part + 1.0 / 14.0) - y_cell

    def tent(distance):
        return jnp.maximum(1.0 - jnp.abs(distance), 0.0)

    across_w = []
    for j in range(7):
        one = x_anchor + x_extent * ((2 * j + 0.5) / 14.0)
        two = x_anchor + x_extent * ((2 * j + 1.5) / 14.0)
        across_w.append(0.25 * (tent(one - x_cell) + tent(two - x_cell)))
    across_w.append(jnp.zeros((8, LANES), jnp.float32))
    packed = [
        jnp.concatenate([across_w[2 * at], across_w[2 * at + 1]], axis=0).astype(jnp.bfloat16)
        for at in range(4)
    ]
    blocks = []
    for at in range(SPAN):
        offset = rows_per * float(at)
        down = tent(near - offset) + tent(far - offset)
        both = jnp.concatenate([down, down], axis=0).astype(jnp.bfloat16)
        blocks.append(jnp.concatenate([both * item for item in packed], axis=0))
    return jnp.concatenate(blocks, axis=1), first_tile, across


def tile_lanes(first_tile, across, at):
    return pl.ds(pl.multiple_of((first_tile + at * across) * LANES, LANES), LANES)


def pool_kernel(
    rois, floats, ints, mean, scale, shift, p2, p3, p4, p5,
    pooled_out, centred_out, weight_out, maps, values, totals, sems,
):
    channels = mean.shape[1] // 2
    copies = []
    for level, plane in enumerate((p2, p3, p4, p5)):
        cells = TILES[level] * LANES
        copies.append(
            pltpu.make_async_copy(
                plane.at[0],
                maps.at[pl.ds(0, channels), pl.ds(FIRST[level] * LANES, cells)],
                sems.at[level],
            )
        )
        copies[-1].start()
    ones = jnp.ones((16, LANES), jnp.bfloat16)

    def fill(at, carry):
        maps[pl.ds(channels, 16), pl.ds(pl.multiple_of(at * LANES, LANES), LANES)] = ones
        return carry

    lax.fori_loop(0, ALL_TILES, fill, 0)
    extra = PADDED - ALL_TILES
    if extra:
        maps[:, pl.ds(ALL_TILES * LANES, extra * LANES)] = jnp.zeros(
            (channels + 16, extra * LANES), jnp.bfloat16
        )
    for copy in copies:
        copy.wait()
    low_lane = lax.broadcasted_iota(jnp.int32, (SLOTS, 2 * channels), 1) < channels

    def item(region, chunk, tile_x):
        kernel_w, first_tile, across = window_weights(floats, ints, rois, region, chunk, tile_x)
        cells = jnp.concatenate(
            [maps[:, tile_lanes(first_tile, across, at)] for at in range(SPAN)], axis=1
        )
        result = contract_last(kernel_w, cells)
        pair = jnp.concatenate(
            [result[:SLOTS, :channels], result[SLOTS:, :channels]], axis=1
        )
        total = jnp.where(
            low_lane,
            jnp.broadcast_to(result[:SLOTS, channels : channels + 1], low_lane.shape),
            jnp.broadcast_to(result[SLOTS:, channels : channels + 1], low_lane.shape),
        )
        return pair, total

    def step(at, carry):
        for lane_at in range(PAIR):
            region = at * PAIR + lane_at
            pair, total = item(region, None, None)
            values[pl.ds(region, SLOTS, stride=rois), :] = pair
            totals[pl.ds(region, SLOTS, stride=rois), :] = total
        for lane_at in range(PAIR):
            region = at * PAIR + lane_at
            tiles_x = ints[5 * rois + region]

            def more(index, inner):
                chunk = index // tiles_x
                pair, total = item(region, chunk, index - chunk * tiles_x)
                place = pl.ds(region, SLOTS, stride=rois)
                values[place, :] = values[place, :] + pair
                totals[place, :] = totals[place, :] + total
                return inner

            lax.fori_loop(1, ints[4 * rois + region] * tiles_x, more, 0)
        return carry

    lax.fori_loop(0, rois // PAIR, step, 0)
    for at, slot in enumerate(USED):
        rows = pl.ds(slot * rois, rois)
        lanes = pl.ds(at * LANES, LANES)
        total = totals[rows, :]
        centred = values[rows, :] - mean[...] * total
        centred_out[:, lanes] = centred.astype(jnp.bfloat16)
        weight_out[:, lanes] = total.astype(jnp.bfloat16)
        pooled_out[:, lanes] = (centred * scale[...] + shift[...] * total).astype(jnp.bfloat16)


def unpool_kernel(
    rois, floats, ints, base, slope, grads, p2, p3, p4, p5,
    o2, o3, o4, o5, maps, sums, slots, sems, out_sems,
):
    channels = base.shape[0]
    copies = []
    for level, plane in enumerate((p2, p3, p4, p5)):
        cells = TILES[level] * LANES
        copies.append(
            pltpu.make_async_copy(
                plane.at[0], maps.at[:, pl.ds(FIRST[level] * LANES, cells)], sems.at[level]
            )
        )
        copies[-1].start()
    for slot in range(SLOTS):
        rows = pl.ds(slot * rois, rois)
        if slot in USED:
            lanes = pl.ds(USED.index(slot) * LANES, LANES)
            slots[rows, :] = grads[:, lanes].astype(jnp.float32)
        else:
            slots[rows, :] = jnp.zeros((rois, LANES), jnp.float32)
    for copy in copies:
        copy.wait()
    base_v, slope_v = base[...], slope[...]

    def begin(at, carry):
        lanes = pl.ds(pl.multiple_of(at * LANES, LANES), LANES)
        sums[:, lanes] = base_v + slope_v * maps[:, lanes].astype(jnp.float32)
        return carry

    lax.fori_loop(0, ALL_TILES, begin, 0)
    extra = PADDED - ALL_TILES
    if extra:
        sums[:, pl.ds(ALL_TILES * LANES, extra * LANES)] = jnp.zeros(
            (channels, extra * LANES), jnp.float32
        )

    def item(region, chunk, tile_x):
        kernel_w, first_tile, across = window_weights(floats, ints, rois, region, chunk, tile_x)
        mine = slots[pl.ds(region, SLOTS, stride=rois), :]
        stacked = jnp.concatenate([mine[:, :channels], mine[:, channels:]], axis=0)
        turned = stacked.T.astype(jnp.bfloat16)
        result = jnp.dot(turned, kernel_w, preferred_element_type=jnp.float32)
        return result, first_tile, across

    def add(result, first_tile, across):
        for at in range(SPAN):
            lanes = tile_lanes(first_tile, across, at)
            sums[:, lanes] = sums[:, lanes] + result[:, at * LANES : (at + 1) * LANES]

    def step(at, carry):
        results = [item(at * PAIR + lane_at, None, None) for lane_at in range(PAIR)]
        for result in results:
            add(*result)
        for lane_at in range(PAIR):
            region = at * PAIR + lane_at
            tiles_x = ints[5 * rois + region]

            def more(index, inner):
                chunk = index // tiles_x
                add(*item(region, chunk, index - chunk * tiles_x))
                return inner

            lax.fori_loop(1, ints[4 * rois + region] * tiles_x, more, 0)
        return carry

    lax.fori_loop(0, rois // PAIR, step, 0)
    copies = []
    for level, plane in enumerate((o2, o3, o4, o5)):
        cells = TILES[level] * LANES
        copies.append(
            pltpu.make_async_copy(
                sums.at[:, pl.ds(FIRST[level] * LANES, cells)], plane.at[0], out_sems.at[level]
            )
        )
        copies[-1].start()
    for copy in copies:
        copy.wait()


ANY = pl.BlockSpec(memory_space=pl.ANY)
SMEM = pl.BlockSpec(memory_space=pltpu.SMEM)
VMEM = pl.BlockSpec(memory_space=pltpu.VMEM)
LIMIT = 60 * 1024 * 1024


def pool_maps(floats, ints, mean, scale, shift, planes, rois):
    channels = planes[0].shape[1]
    flat = jax.ShapeDtypeStruct((rois, WIDE), jnp.bfloat16)
    return pl.pallas_call(
        functools.partial(pool_kernel, rois),
        out_shape=(flat, flat, flat),
        in_specs=[SMEM, SMEM, VMEM, VMEM, VMEM, ANY, ANY, ANY, ANY],
        out_specs=(VMEM, VMEM, VMEM),
        scratch_shapes=[
            pltpu.VMEM((channels + 16, PADDED * LANES), jnp.bfloat16),
            pltpu.VMEM((SLOTS * rois, LANES), jnp.float32),
            pltpu.VMEM((SLOTS * rois, LANES), jnp.float32),
            pltpu.SemaphoreType.DMA((4,)),
        ],
        compiler_params=pltpu.CompilerParams(vmem_limit_bytes=LIMIT),
        name="pool",
    )(floats, ints, mean, scale, shift, *planes)


def unpool_maps(floats, ints, base, slope, grads, planes, rois):
    channels = planes[0].shape[1]
    return pl.pallas_call(
        functools.partial(unpool_kernel, rois),
        out_shape=tuple(jax.ShapeDtypeStruct(plane.shape, jnp.float32) for plane in planes),
        in_specs=[SMEM, SMEM, VMEM, VMEM, VMEM, ANY, ANY, ANY, ANY],
        out_specs=(ANY, ANY, ANY, ANY),
        scratch_shapes=[
            pltpu.VMEM((channels, ALL_TILES * LANES), jnp.bfloat16),
            pltpu.VMEM((channels, PADDED * LANES), jnp.float32),
            pltpu.VMEM((SLOTS * rois, LANES), jnp.float32),
            pltpu.SemaphoreType.DMA((4,)),
            pltpu.SemaphoreType.DMA((4,)),
        ],
        compiler_params=pltpu.CompilerParams(vmem_limit_bytes=LIMIT),
        name="unpool",
    )(floats, ints, base, slope, grads, *planes)


def local(
    p2, p3, p4, p5, norm_gain, norm_bias, fc6_weight, fc6_bias, fc7_weight, fc7_bias,
    cls_weight, cls_bias, box_weight, box_bias, roi_boxes, roi_level, roi_image,
    canvas_offsets, labels, target_boxes, valid,
):
    channels = p2.shape[1]
    rois = roi_level.shape[0]
    cols = lax.axis_size("col")
    rows = lax.axis_size("roi")
    hidden = fc6_bias.shape[0] * cols
    piece = fc6_bias.shape[0]
    high = rows // cols
    few = channels // high
    planes = (p2, p3, p4, p5)

    block = fc6_weight.reshape(few, 7, 7, piece)
    block = jnp.pad(block, ((0, 0), (0, 0), (0, 1), (0, 0))).reshape(few, 7, 2, 4, piece)
    block = block.transpose(3, 1, 2, 0, 4).reshape(len(USED) * 2, few, piece)
    pairs = [
        ((kappa * high + rho // cols) * cols + rho % cols, rho * cols + kappa)
        for rho in range(rows)
        for kappa in range(cols)
    ]
    block = lax.ppermute(block, ("roi", "col"), pairs)
    wide = lax.all_gather(block, "roi", axis=0)
    wide = wide.reshape(high, cols, len(USED) * 2, few, piece)
    wide = wide.transpose(2, 0, 3, 1, 4).reshape(WIDE, hidden)

    per = fc7_bias.shape[0]
    classes, boxes = cls_weight.shape[1], box_weight.shape[1]
    head = jnp.concatenate([cls_weight, box_weight, fc7_bias[:, None]], axis=1)
    head = jnp.pad(head, ((0, 0), (0, piece - head.shape[1])))
    bias_high = fc6_bias.astype(jnp.bfloat16)
    rest = fc6_bias - bias_high.astype(jnp.float32)
    bias_mid = rest.astype(jnp.bfloat16)
    bias_low = (rest - bias_mid.astype(jnp.float32)).astype(jnp.bfloat16)
    small = jnp.concatenate(
        [fc7_weight, head, jnp.stack([bias_high, bias_mid, bias_low])], axis=0
    )
    deep_rows = fc7_weight.shape[0]
    small = jnp.pad(small, ((0, -small.shape[0] % 16), (0, 0)))
    small = lax.all_gather(small, ("roi", "col"), axis=0)
    deep = small[:, :deep_rows].reshape(rows, cols, deep_rows, piece)
    deep = deep.transpose(0, 2, 1, 3).reshape(hidden, hidden)
    head = small[:, deep_rows : deep_rows + per].reshape(hidden, piece)[:, :LANES]
    bias_seven = head[:, classes + boxes].astype(jnp.float32)
    bias_six = small[:cols, deep_rows + per : deep_rows + per + 3].astype(jnp.float32)
    bias_six = jnp.sum(bias_six, axis=1).reshape(hidden)

    values = [plane[0].astype(jnp.float32) for plane in planes]
    pixel_total = rows * sum(plane.shape[1] for plane in values)
    first_sum = sum(jnp.sum(plane, axis=1) for plane in values)
    second_sum = sum(jnp.sum(plane * plane, axis=1) for plane in values)
    local_valid = jnp.sum(valid.astype(jnp.float32))
    first_sum, second_sum, valid_total = lax.psum((first_sum, second_sum, local_valid), "roi")
    mean = first_sum / pixel_total
    variance = second_sum / pixel_total - mean * mean
    inv_std = lax.rsqrt(variance + EPSILON)
    scale = norm_gain * inv_std

    picks = roi_image[None, :] == jnp.arange(4, dtype=jnp.int32)[:, None]
    shift_x = jnp.sum(jnp.where(picks, canvas_offsets[0][:, None], 0), axis=0)
    shift_y = jnp.sum(jnp.where(picks, canvas_offsets[1][:, None], 0), axis=0)
    floats, ints = region_tables(
        (roi_boxes[0] + shift_x).astype(jnp.float32),
        (roi_boxes[1] + shift_y).astype(jnp.float32),
        (roi_boxes[2] + shift_x).astype(jnp.float32),
        (roi_boxes[3] + shift_y).astype(jnp.float32),
        roi_level,
    )

    def twice(vector):
        return jnp.concatenate([vector, vector])[None]

    pooled, centred, weight = pool_maps(
        floats, ints, twice(mean), twice(scale), twice(norm_bias), planes, rois
    )

    partial_six = jnp.dot(pooled, wide, preferred_element_type=jnp.float32).astype(jnp.bfloat16)
    pre_six = lax.psum_scatter(partial_six, "col", scatter_dimension=0, tiled=True)
    pre_six = pre_six.astype(jnp.float32) + bias_six
    hidden_six = jax.nn.silu(pre_six).astype(jnp.bfloat16)
    pre_seven = contract_last(hidden_six, deep) + bias_seven
    hidden_seven = jax.nn.silu(pre_seven).astype(jnp.bfloat16)
    scores = jnp.dot(hidden_seven, head, preferred_element_type=jnp.float32)
    logits = scores[:, :classes] + cls_bias
    deltas = scores[:, classes : classes + boxes] + box_bias

    quarter = rois // cols
    first_row = lax.axis_index("col") * quarter
    mine_labels = lax.dynamic_slice_in_dim(labels, first_row, quarter)
    mine_valid = lax.dynamic_slice_in_dim(valid, first_row, quarter).astype(jnp.float32)
    mine_boxes = lax.dynamic_slice_in_dim(roi_boxes, first_row, quarter, axis=1).astype(jnp.float32)
    mine_goals = lax.dynamic_slice_in_dim(target_boxes, first_row, quarter, axis=1).astype(
        jnp.float32
    )
    prop_width = mine_boxes[2] - mine_boxes[0]
    prop_height = mine_boxes[3] - mine_boxes[1]
    prop_cx = mine_boxes[0] + 0.5 * prop_width
    prop_cy = mine_boxes[1] + 0.5 * prop_height
    goal_width = mine_goals[2] - mine_goals[0]
    goal_height = mine_goals[3] - mine_goals[1]
    goal_cx = mine_goals[0] + 0.5 * goal_width
    goal_cy = mine_goals[1] + 0.5 * goal_height
    targets = jnp.stack(
        [
            10.0 * (goal_cx - prop_cx) / prop_width,
            10.0 * (goal_cy - prop_cy) / prop_height,
            5.0 * jnp.log(goal_width / prop_width),
            5.0 * jnp.log(goal_height / prop_height),
        ],
        axis=1,
    )
    foreground = mine_valid * (mine_labels > 0).astype(jnp.float32)
    top_logit = jnp.max(logits, axis=1, keepdims=True)
    log_total = top_logit[:, 0] + jnp.log(jnp.sum(jnp.exp(logits - top_logit), axis=1))
    onehot = (mine_labels[:, None] == jnp.arange(classes, dtype=jnp.int32)[None, :]).astype(
        jnp.float32
    )
    picked = jnp.sum(onehot * logits, axis=1)
    misfit = deltas - targets
    huber_terms = jnp.where(jnp.abs(misfit) < 1.0, 0.5 * misfit * misfit, jnp.abs(misfit) - 0.5)
    class_part = jnp.sum(mine_valid * (log_total - picked))
    box_part = jnp.sum(foreground * jnp.sum(huber_terms, axis=1))
    centre_x = prop_cx + deltas[:, 0] / 10.0 * prop_width
    centre_y = prop_cy + deltas[:, 1] / 10.0 * prop_height
    new_width = prop_width * jnp.exp(deltas[:, 2] / 5.0)
    new_height = prop_height * jnp.exp(deltas[:, 3] / 5.0)
    decoded = jnp.stack(
        [
            centre_x - 0.5 * new_width,
            centre_y - 0.5 * new_height,
            centre_x + 0.5 * new_width,
            centre_y + 0.5 * new_height,
        ]
    ) / (CANVAS // 2)
    loss_scale = rois * rows / valid_total
    softmax = jnp.exp(logits - log_total[:, None])
    logit_grads = loss_scale * mine_valid[:, None] * (softmax - onehot)
    delta_grads = loss_scale * foreground[:, None] * jnp.clip(misfit, -1.0, 1.0)
    score_grads = jnp.concatenate([logit_grads, delta_grads], axis=1)
    score_grads = jnp.pad(score_grads, ((0, 0), (0, LANES - score_grads.shape[1])))
    score_grads = score_grads.astype(jnp.bfloat16)

    head_term = contract_first(hidden_seven, score_grads)
    hidden_grads = contract_last(score_grads, head)
    pre_seven_grads = (hidden_grads * silu_slope(pre_seven)).astype(jnp.bfloat16)
    deep_term = contract_first(pre_seven_grads, hidden_six)
    six_hidden_grads = jnp.dot(pre_seven_grads, deep, preferred_element_type=jnp.float32)
    pre_six_grads = (six_hidden_grads * silu_slope(pre_six)).astype(jnp.bfloat16)
    six_grads_all = lax.all_gather(pre_six_grads, "col", axis=0, tiled=True)

    wide_term = contract_first(pooled, six_grads_all).astype(jnp.bfloat16)
    wide_term = wide_term.reshape(len(USED) * 2, high, few, cols, piece)
    wide_term = wide_term.transpose(1, 3, 0, 2, 4).reshape(rows * len(USED) * 2, few, piece)
    wide_grad = lax.psum_scatter(wide_term, "roi", scatter_dimension=0, tiled=True)
    wide_grad = lax.ppermute(wide_grad, ("roi", "col"), [(there, here) for here, there in pairs])
    wide_grad = wide_grad.reshape(4, 7, 2, few, piece).transpose(3, 1, 2, 0, 4)
    wide_grad = wide_grad.reshape(few, 7, 8, piece)[:, :, :7].reshape(few * 49, piece)
    fc6_weight_grad = wide_grad.astype(jnp.float32)

    sums = jnp.concatenate(
        [
            jnp.sum(score_grads.astype(jnp.float32), axis=0),
            jnp.stack([class_part, box_part]),
        ]
    )
    everyone = rows * cols
    deep_term = deep_term.reshape(rows, deep_rows, cols, piece).transpose(0, 2, 1, 3)
    deep_term = deep_term.reshape(everyone, deep_rows, piece)
    seven_bias_term = jnp.sum(pre_seven_grads.astype(jnp.float32), axis=0)
    head_term = jnp.concatenate(
        [head_term[:, : classes + boxes], seven_bias_term[:, None]], axis=1
    )
    head_term = jnp.pad(head_term, ((0, 0), (0, piece - head_term.shape[1])))
    head_term = head_term.reshape(everyone, per, piece)
    six_bias_term = jnp.sum(pre_six_grads.astype(jnp.float32), axis=0).reshape(cols, 1, piece)
    six_bias_term = jnp.broadcast_to(six_bias_term[None], (rows, cols, 1, piece))
    six_bias_term = six_bias_term.reshape(everyone, 1, piece)
    sums = jnp.pad(sums, (0, piece - sums.shape[0]))
    sums = jnp.broadcast_to(sums[None, None], (everyone, 1, piece))
    small_term = jnp.concatenate([deep_term, head_term, six_bias_term, sums], axis=1)
    small_term = jnp.pad(small_term, ((0, 0), (0, -small_term.shape[1] % 8), (0, 0)))
    small_grad = lax.psum_scatter(small_term, ("roi", "col"), scatter_dimension=0, tiled=True)[0]
    fc7_weight_grad = small_grad[:deep_rows]
    head_grad = small_grad[deep_rows : deep_rows + per]
    cls_weight_grad = head_grad[:, :classes]
    box_weight_grad = head_grad[:, classes : classes + boxes]
    fc7_bias_grad = head_grad[:, classes + boxes]
    fc6_bias_grad = small_grad[deep_rows + per]
    sums = small_grad[deep_rows + per + 1]
    class_bias_grad = sums[:classes]
    box_bias_grad = sums[classes : classes + boxes]
    cls_loss = sums[LANES] / valid_total
    box_loss = sums[LANES + 1] / valid_total

    pool_grads = contract_last(six_grads_all, wide)
    gain_part = jnp.sum(pool_grads * centred.astype(jnp.float32), axis=0)
    shift_part = jnp.sum(pool_grads * weight.astype(jnp.float32), axis=0)
    gain_part = jnp.sum(gain_part.reshape(-1, channels), axis=0) * inv_std
    shift_part = jnp.sum(shift_part.reshape(-1, channels), axis=0)
    norm_gain_grad, norm_bias_grad = lax.psum((gain_part, shift_part), "roi")

    scaled = (pool_grads * jnp.tile(scale, WIDE // channels)).astype(jnp.bfloat16)
    slope = -scale * inv_std * norm_gain_grad / pixel_total
    base = -scale * norm_bias_grad / pixel_total - slope * mean

    def spread(vector):
        return jnp.broadcast_to(vector[:, None], (channels, LANES))

    input_grads = unpool_maps(floats, ints, spread(base), spread(slope), scaled, planes, rois)
    return (
        cls_loss,
        box_loss,
        decoded,
        input_grads[0],
        input_grads[1],
        input_grads[2],
        input_grads[3],
        norm_gain_grad,
        norm_bias_grad,
        fc6_weight_grad,
        fc6_bias_grad,
        fc7_weight_grad,
        fc7_bias_grad,
        cls_weight_grad,
        class_bias_grad,
        box_weight_grad,
        box_bias_grad,
    )


def solution(mesh):
    return jax.shard_map(
        local,
        mesh=mesh,
        in_specs=(
            P("roi", "col", None),
            P("roi", "col", None),
            P("roi", "col", None),
            P("roi", "col", None),
            P("col"),
            P("col"),
            P("roi", "col"),
            P("col"),
            P("roi", "col"),
            P(("roi", "col")),
            P(("roi", "col"), None),
            P(),
            P(("roi", "col"), None),
            P(),
            P(None, "roi"),
            P("roi"),
            P("roi"),
            P(None, "roi"),
            P("roi"),
            P(None, "roi"),
            P("roi"),
        ),
        out_specs=(
            P(),
            P(),
            P(None, ("roi", "col")),
            P("roi", "col", None),
            P("roi", "col", None),
            P("roi", "col", None),
            P("roi", "col", None),
            P("col"),
            P("col"),
            P("roi", "col"),
            P("col"),
            P("roi", "col"),
            P(("roi", "col")),
            P(("roi", "col"), None),
            P(),
            P(("roi", "col"), None),
            P(),
        ),
        check_vma=False,
    )
```

time: 2140 us -> 602 us (0.28)
  matrix products: 1110 us -> 27.7 us
  local copies, waits for them, and re-layouts: 377 us -> 89.2 us
  Pallas kernels: 0 us -> 213 us
  blocking collectives: 238 us -> 67.1 us
  other arithmetic: 137 us -> 22.9 us
  waiting for transfers between devices: 219 us -> 149 us
  loops' own time: 22.5 us -> 0 us
    dot_general x100 -> x3, matrix products: 1080 us -> 4.87 us  [the longest x1 3.88 us: local(): jnp.dot(pooled, wide, preferred_element_type=jnp.float32)]
    pallas_call x0 -> x2, Pallas kernels: none -> 213 us  [the longest x1 114 us: unpool_maps(): pl.pallas_call(functools.partial(unpool_kernel, rois), out_shape=tuple((j...]
    convert_element_type x24 -> x2, local copies, waits for them, and re-layouts: 112 us -> 2.33 us  [local(): fc6_weight_grad = wide_grad.astype(jnp.float32)]
    all_gather x2, waiting for transfers between devices: 108 us -> 0.02 us  [the longest x1 0.02 us: local(): wide = lax.all_gather(block, 'roi', axis=0)]
    all_gather x4 -> x1, blocking collectives: 112 us -> 8.58 us  [local(): six_grads_all = lax.all_gather(pre_six_grads, 'col', axis=0, tiled=True)]
    slice x73 -> x12, local copies, waits for them, and re-layouts: 92.8 us -> 11.7 us  [the longest x1 1.81 us: local(): deep = small[:, :deep_rows].reshape(rows, cols, deep_rows, piece)]
    while x223 -> x0, local copies, waits for them, and re-layouts: 55.8 us -> none  [the longest x3 26.4 us: local(): lax.scan(unpool_step, start_grads, (regions, pool_grads))]
    psum x2 -> x1, blocking collectives: 65.3 us -> 19.6 us  [local(): norm_gain_grad, norm_bias_grad = lax.psum((gain_part, shift_part), 'roi')]
  transfers between devices with their start and end apart: 8 -> 7, of which waited for: 4 -> 3; matrix products, arithmetic and copies ran while one was open for 34% -> 16% of each run, Pallas kernels for 0% -> 36%
where the time goes in v1:
time: 602 us; the launch traced here: 594 us
  Pallas kernels  213 us (35%)
  waiting for transfers between devices  149 us (25%)
  local copies, waits for them, and re-layouts  89.2 us (15%)
  blocking collectives  67.1 us (11%)
  matrix products  27.7 us (5%)
  other arithmetic  22.9 us (4%)
  between operations  20.2 us (3%)
    pallas_call x1, Pallas kernels, unpool_maps(): pl.pallas_call(functools.partial(unpool_kernel, rois), out_shape=tuple((j...  114 us
    pallas_call x1, Pallas kernels, pool_maps(): pl.pallas_call(functools.partial(pool_kernel, rois), out_shape=(flat, fla...  98.6 us
    reduce_scatter x1, waiting for transfers between devices, local(): lax.psum_scatter(small_term, ('roi', 'col'), scatter_dimension=0, tiled=T...  89.1 us
    ppermute x1, waiting for transfers between devices, local(): block = lax.ppermute(block, ('roi', 'col'), pairs)  42.6 us
    psum x1, blocking collectives, local(): lax.psum((first_sum, second_sum, local_valid), 'roi')  39 us
    reshape x1, local copies, waits for them, and re-layouts, local(): wide = wide.reshape(high, cols, len(USED) * 2, few, piece)  21.1 us
    reshape x2, local copies, waits for them, and re-layouts, local(): wide_term = wide_term.reshape(len(USED) * 2, high, few, cols, piece)  20.3 us
    psum x1, blocking collectives, local(): norm_gain_grad, norm_bias_grad = lax.psum((gain_part, shift_part), 'roi')  19.6 us
  transfers between devices with their start and end apart: 7, of which 3 were waited for; matrix products, arithmetic and copies ran while one was open for 16% of the time, Pallas kernels for 36%

profile of v1, /device:TPU:12, one launch (start us, length us, event | category | flops | bytes accessed | tf_op | source)
XLA Modules:
  0.0 593.9 jit_solution(15250647681412529471)
XLA Ops:
  7.3 1.5 reshape.399
  8.8 1.1 pad.29
  9.9 1.8 reshape.400
  11.9 1.9 collective-permute-start
  13.8 42.6 %collective-permute-done = bf16[56,32,256]{2,1,0:T(8,128)(2,1)S(1)} collective-permute-done((bf16[56,32,256]{2,1,0:T(8,128)(2,1)S(1)}, bf16[56,32,256]{2,1,0:T(8,128)(2,1)S(1)}, u32[]{:S(2)}, u32[]{:S(2)}) %collective-permute-start) | collective-permute-done | bytes 917536 | tf_op jit(solution)/shard_map/ppermute | solution.py:362
  56.4 0.9 copy-done.4
  57.4 0.8 subtract_convert_fusion
  58.9 0.8 copy.116
  59.8 0.9 concatenate.32
  62.2 0.8 select_reduce_fusion.1
  65.1 1.3 convert_reduce_fusion.9
  66.4 1.0 fusion.19
  68.5 5.6 fusion
  74.1 39.0 %all-reduce.8 = (f32[64]{0:T(128)S(1)}, f32[64]{0:T(128)S(1)}, f32[]{:T(128)}) all-reduce(f32[64]{0:T(128)S(1)} %get-tuple-element.202, f32[64]{0:T(128)S(1)} %get-tuple-element.201, f32[]{:T(128)} %convert_reduce_fusion.9), channel_id=1, replica_groups=mesh['roi'=8,'col'=4] {'roi'}, use_global_device_ids=true, to_apply=%region_8.9 | all-reduce | flops 129 | bytes 1032 | tf_op jit(solution)/shard_map/psum | solution.py:393
  114.9 98.6 %pool.1 = (bf16[384,3584]{1,0:T(8,128)(2,1)}, bf16[384,3584]{1,0:T(8,128)(2,1)}, bf16[384,3584]{1,0:T(8,128)(2,1)}) custom-call(f32[2688]{0:T(1024)} %reshape.397.floats, s32[2304]{0:T(1024)} %reshape.398.ints, f32[1,128]{1,0:T(1,128)} %maximum_bitcast_fusion.mean, f32[1,128]{1,0:T(1,128)} %maximum_bitcast_fusion.1.scale, ...), custom_call_target="tpu_custom_call" | custom-call | tf_op jit(solution)/shard_map/pool/pallas_call | solution.py:304
  213.5 21.1 %copy.115 = bf16[2,4,56,32,256]{4,1,3,0,2:T(4,128)(2,1)} copy(bf16[2,4,56,32,256]{4,3,2,1,0:T(8,128)(2,1)} %bitcast.177) | data formatting | bytes 14680064 | tf_op jit(solution)/shard_map/reshape | solution.py:364
  234.6 5.6 copy.128
  240.3 3.0 copy-done.1
  243.4 3.9 convolution_convert_fusion.1
  247.3 0.8 dynamic-slice_convert_fusion
  248.9 0.8 convert_multiply_fusion.5
  250.4 1.1 slice.181
  251.5 1.8 slice.180
  254.1 3.0 copy.118
  257.4 17.6 %reduce-scatter.4.cloned.1.call-done = bf16[96,1024]{1,0:T(8,128)(2,1)} async-done(((bf16[384,1024]{1,0:T(8,128)(2,1)}), bf16[96,1024]{1,0:T(8,128)(2,1)}) %reduce-scatter.4.cloned.1.call-update) | async-done | bytes 196624 | tf_op jit(solution)/shard_map/reduce_scatter | solution.py:418
  275.0 2.3 multiply_convert_fusion.1
  279.2 0.8 convert_reduce_fusion.4
  280.0 8.6 %all_gather.19 = bf16[384,1024]{1,0:T(8,128)(2,1)S(1)} all-gather(bf16[96,1024]{1,0:T(8,128)(2,1)S(1)} %get-tuple-element.198), channel_id=1, replica_groups=mesh['roi'=8,'col'=4] {'col'}, dimensions={0}, use_global_device_ids=true | all-gather | bytes 983040 | tf_op jit(solution)/shard_map/all_gather | solution.py:489
  288.5 6.1 %convolution_convert_fusion = bf16[3584,1024]{1,0:T(8,128)(2,1)} fusion(bf16[384,3584]{1,0:T(8,128)(2,1)S(1)} %copy-done.14, bf16[384,1024]{1,0:T(8,128)(2,1)S(1)} %all_gather.19), kind=kOutput, calls=%fused_computation.3 | convolution fusion | flops 2822242304 | bytes 10878976 | tf_op jit(solution)/shard_map/dot_general | solution.py:34
  294.6 12.8 %reshape.412 = bf16[56,2,32,4,256]{4,3,2,1,0:T(4,128)(2,1)} reshape(bf16[3584,1024]{1,0:T(8,128)(2,1)} %convolution_convert_fusion) | data formatting | bytes 14680064 | tf_op jit(solution)/shard_map/reshape | solution.py:492
  307.4 7.5 %copy.123 = bf16[56,2,32,4,256]{4,2,0,3,1:T(8,128)(2,1)} copy(bf16[56,2,32,4,256]{4,3,2,1,0:T(4,128)(2,1)} %reshape.412) | data formatting | bytes 14680064 | tf_op jit(solution)/shard_map/reshape | solution.py:492
  315.5 2.8 fusion.61
  318.3 5.6 reshape.407
  323.9 3.0 copy.120
  327.0 1.4 select_maximum_fusion.3
  328.4 2.7 select_maximum_fusion
  331.2 11.2 %multiply_reduce_fusion.1 = (f32[3584]{0:T(1024)S(1)}, f32[3584]{0:T(1024)S(1)}, bf16[384,3584]{1,0:T(8,128)(2,1)}) fusion(bf16[384,3584]{1,0:T(8,128)(2,1)} %get-tuple-element.25, bf16[384,3584]{1,0:T(8,128)(2,1)} %get-tuple-element.26, f32[3584]{0:T(1024)S(1)} %mul.330, bf16[384,1024]{1,0:T(8,128)(2,1)S(1)} %all_gather.19, bf16[3584,1024]{1,0:T(8,128)(2,1)} %bitcast.176), kind=kOutput, calls=%fused_computation.10 | convolution fusion | flops 2829575168 | bytes 16427008 | tf_op jit(solution)/shard_map/dot_general | solution.py:40
  342.8 19.6 %all-reduce.7 = (f32[64]{0:T(128)S(1)}, f32[64]{0:T(128)S(1)}) all-reduce(f32[64]{0:T(128)S(1)} %mul.327, f32[64]{0:T(128)S(1)} %reduce_sum.237), channel_id=1, replica_groups=mesh['roi'=8,'col'=4] {'roi'}, use_global_device_ids=true, to_apply=%region_31.32 | all-reduce | flops 128 | bytes 1024 | tf_op jit(solution)/shard_map/psum | solution.py:540
  363.8 114.5 %unpool.1 = (f32[1,64,65536]{2,1,0:T(8,128)}, f32[1,64,16384]{2,1,0:T(8,128)}, f32[1,64,4096]{2,1,0:T(8,128)}, f32[1,64,1024]{2,1,0:T(8,128)}) custom-call(f32[2688]{0:T(1024)} %reshape.397.floats, s32[2304]{0:T(1024)} %reshape.398.ints, f32[64,128]{1,0:T(8,128)} %broadcast_in_dim.141.base, f32[64,128]{1,0:T(8,128)} %broadcast_in_dim.142.slope, ...), custom_call_target="tpu_custom_call" | custom-call | tf_op jit(solution)/shard_map/unpool/pallas_call | solution.py:322
  478.9 2.2 collective-permute-start.1
  481.1 89.1 %reduce-scatter.6.cloned.1.call-done = f32[1,168,256]{2,1,0:T(8,128)} async-done(((f32[32,168,256]{2,1,0:T(8,128)}), f32[1,168,256]{2,1,0:T(8,128)}) %reduce-scatter.6.cloned.1.call-update) | async-done | bytes 172048 | tf_op jit(solution)/shard_map/reduce_scatter | solution.py:522
  571.7 1.3 fusion.71
  576.4 1.3 slice.193
  578.3 1.2 slice_bitcast_fusion.3
  579.5 1.3 slice_bitcast_fusion.2
  580.8 1.6 slice_bitcast_fusion
  582.6 0.9 copy.125
  583.6 1.4 reshape.417
  (127 shorter events, 17.5 us)
Async XLA Ops:
  7.2 52.5 %copy-start.7 = (bf16[32,81]{1,0:T(8,128)(2,1)S(1)}, bf16[32,81]{1,0:T(8,128)(2,1)}, u32[]{:S(2)}) copy-start(bf16[32,81]{1,0:T(8,128)(2,1)} %param.31) | copy-start | bytes 15556
  7.2 54.2 %copy-start.6 = (s32[4,384]{1,0:T(4,128)S(1)}, s32[4,384]{1,0:T(4,128)}, u32[]{:S(2)}) copy-start(s32[4,384]{1,0:T(4,128)} %param.35) | copy-start | bytes 18436
  7.2 60.2 %copy-start.2 = (bf16[1,64,4096]{2,1,0:T(8,128)(2,1)S(1)}, bf16[1,64,4096]{2,1,0:T(8,128)(2,1)}, u32[]{:S(2)}) copy-start(bf16[1,64,4096]{2,1,0:T(8,128)(2,1)} %p4.3) | copy-start | bytes 1572868
  7.2 60.5 %copy-start = (bf16[1,64,16384]{2,1,0:T(8,128)(2,1)S(1)}, bf16[1,64,16384]{2,1,0:T(8,128)(2,1)}, u32[]{:S(2)}) copy-start(bf16[1,64,16384]{2,1,0:T(8,128)(2,1)} %p3.3) | copy-start | bytes 6291460
  7.2 206.3 %all-gather.5.cloned.1.call-start = ((), (), s32[]{:S(2)}) async-start(), calls=%async_computation.6 | async-start | bytes 8257536 | tf_op jit(solution)/shard_map/all_gather | solution.py:363
  11.9 44.5 %collective-permute-start = (bf16[56,32,256]{2,1,0:T(8,128)(2,1)S(1)}, bf16[56,32,256]{2,1,0:T(8,128)(2,1)S(1)}, u32[]{:S(2)}, u32[]{:S(2)}) collective-permute-start(bf16[56,32,256]{2,1,0:T(8,128)(2,1)S(1)} %bitcast.189), channel_id=1, source_target_pairs={{0,0},{8,1},{16,2},{24,3},{1,4},{9,5},{17,6},{25,7},{2,8},{10,9},{... | collective-permute-start | bytes 2752520 | tf_op jit(solution)/shard_map/ppermute | solution.py:362
  56.4 0.9 copy-start.4
  57.3 193.1 %all-gather.7.cloned.1.call-start = ((), (), s32[]{:S(2)}) async-start(), calls=%async_computation.7 | async-start | bytes 2973696 | tf_op jit(solution)/shard_map/all_gather | solution.py:380
  61.3 213.7 %reduce-scatter.4.cloned.1.call-start = ((), (), s32[]{:S(2)}) async-start(), calls=%async_computation.3 | async-start | bytes 983040 | tf_op jit(solution)/shard_map/reduce_scatter | solution.py:418
  67.5 45.6 %copy-start.15 = (f32[64]{0:T(128)S(1)}, f32[64]{0:T(128)}, u32[]{:S(2)}) copy-start(f32[64]{0:T(128)} %param.26) | copy-start | bytes 772
  67.5 46.2 %copy-start.12 = (f32[64]{0:T(128)S(1)}, f32[64]{0:T(128)}, u32[]{:S(2)}) copy-start(f32[64]{0:T(128)} %param.25) | copy-start | bytes 772
  234.6 8.7 %copy-start.13 = (bf16[384,3584]{1,0:T(8,128)(2,1)S(1)}, bf16[384,3584]{1,0:T(8,128)(2,1)}, u32[]{:S(2)}) copy-start(bf16[384,3584]{1,0:T(8,128)(2,1)} %get-tuple-element.24) | copy-start | bytes 8257540
  240.3 3.1 copy-start.1
  247.3 231.6 %reduce-scatter.8.cloned.1.call-start = ((), (), s32[]{:S(2)}) async-start(), calls=%async_computation.5 | async-start | bytes 8257536 | tf_op jit(solution)/shard_map/reduce_scatter | solution.py:494
  254.1 23.4 %copy-start.8 = (f32[81]{0:T(128)S(1)}, f32[81]{0:T(128)}, u32[]{:S(2)}) copy-start(f32[81]{0:T(128)} %param.32) | copy-start | bytes 976
  254.1 23.5 %copy-start.9 = (f32[4]{0:T(128)S(1)}, f32[4]{0:T(128)}, u32[]{:S(2)}) copy-start(f32[4]{0:T(128)} %param.34) | copy-start | bytes 52
  257.1 22.0 %copy-start.3 = (bf16[8,128,4,256]{1,0,3,2:T(8,128)(2,1)S(1)}, bf16[8,128,4,256]{1,0,3,2:T(8,128)(2,1)}, u32[]{:S(2)}) copy-start(bf16[8,128,4,256]{1,0,3,2:T(8,128)(2,1)} %copy.118) | copy-start | bytes 6291460
  275.0 4.1 copy-start.5
  277.3 11.2 %copy-start.14 = (bf16[384,3584]{1,0:T(8,128)(2,1)S(1)}, bf16[384,3584]{1,0:T(8,128)(2,1)}, u32[]{:S(2)}) copy-start(bf16[384,3584]{1,0:T(8,128)(2,1)} %get-tuple-element.24) | copy-start | bytes 8257540
  314.9 255.3 %reduce-scatter.6.cloned.1.call-start = ((), (), s32[]{:S(2)}) async-start(), calls=%async_computation.4 | async-start | bytes 5677056 | tf_op jit(solution)/shard_map/reduce_scatter | solution.py:522
  362.4 115.9 %copy-start.10 = (f32[64]{0:T(128)}, f32[64]{0:T(128)S(1)}, u32[]{:S(2)}) copy-start(f32[64]{0:T(128)S(1)} %get-tuple-element.140) | copy-start | bytes 772
  362.4 115.9 %copy-start.11 = (f32[64]{0:T(128)}, f32[64]{0:T(128)S(1)}, u32[]{:S(2)}) copy-start(f32[64]{0:T(128)S(1)} %get-tuple-element.141) | copy-start | bytes 772
  478.9 103.5 %collective-permute-start.1 = (bf16[56,32,256]{2,1,0:T(8,128)(2,1)}, bf16[56,32,256]{2,1,0:T(8,128)(2,1)S(1)}, u32[]{:S(2)}, u32[]{:S(2)}) collective-permute-start(bf16[56,32,256]{2,1,0:T(8,128)(2,1)} %reduce-scatter.8.cloned.1.call-done), channel_id=1, source_target_pairs={{0,0},{1,8},{2,16},{3,24},{4,1},{5,9},{6,17},{7,25},{8,2},{9,10},{... | collective-permute-start | bytes 2752520 | tf_op jit(solution)/shard_map/ppermute | solution.py:495
Sparse Core Ops, SparseCore 0:
  57.5 130.9 all-gather.4
  191.9 57.9 all-gather.6
  253.0 21.9 reduce-scatter.3
  315.0 133.0 reduce-scatter.7
  454.5 115.7 reduce-scatter.5

commit v2 on v1

--- a/solution.py
+++ b/solution.py
@@ -12,7 +12,9 @@
 EPSILON = 1e-05
 LANES = 128
 SPAN = 10
-PAIR = 2
+GROUP = 16
+MORE = 8
+SPARE = 8
 SIDES = tuple(CANVAS // (4 * 2**level) for level in range(4))
 TILES = tuple(side * side // LANES for side in SIDES)
 FIRST = tuple(sum(TILES[:level]) for level in range(4))
@@ -72,6 +74,18 @@
     mask = jnp.minimum(side, LANES) - 1
     shift = 7 - rows_log
     rows_per = (1 << rows_log).astype(jnp.float32)
+    nothing = jnp.zeros((SPARE,), jnp.int32)
+    parts = chunks * tiles_x
+    key = 2 * (level > 0).astype(jnp.int32) + (parts > 1).astype(jnp.int32)
+    rois = level.shape[0]
+    at = jnp.arange(rois, dtype=jnp.int32)
+    before = (key[None, :] < key[:, None]) | (
+        (key[None, :] == key[:, None]) & (at[None, :] < at[:, None])
+    )
+    rank = jnp.sum(before.astype(jnp.int32), axis=1)
+    order = jnp.sum(jnp.where(rank[None, :] == at[:, None], at[None, :], 0), axis=1)
+    order = jnp.concatenate([order, jnp.full((GROUP,), rois, jnp.int32)])
+    ends = jnp.stack([jnp.sum((key <= last).astype(jnp.int32)) for last in range(4)])
     floats = jnp.stack(
         [
             x_anchor,
@@ -83,11 +97,15 @@
             rows_per,
         ]
     ).astype(jnp.float32)
-    ints = jnp.stack([first_tile, across, mask, shift, chunks, tiles_x]).astype(jnp.int32)
-    return floats.reshape(-1), ints.reshape(-1)
+    ints = jnp.stack([first_tile, across, mask, shift, parts, tiles_x]).astype(jnp.int32)
+    away = jnp.full((F32_FIELDS, SPARE), -1e6, jnp.float32)
+    floats = jnp.concatenate([floats, away], axis=1)
+    ints = jnp.concatenate([ints, jnp.broadcast_to(nothing, (I32_FIELDS, SPARE))], axis=1)
+    return floats.reshape(-1), ints.reshape(-1), jnp.concatenate([order, ends])
 
 
 def window_weights(floats, ints, rois, region, chunk, tile_x):
+    rois = rois + SPARE
     x_anchor, x_extent, y_anchor, y_extent, x_origin, y_origin, rows_per = (
         floats[at * rois + region] for at in range(F32_FIELDS)
     )
@@ -132,11 +150,56 @@
     return pl.ds(pl.multiple_of((first_tile + at * across) * LANES, LANES), LANES)
 
 
+def for_groups(order, start, stop, size, body):
+    def step(at, carry):
+        first = start + at * size
+        inside = [first + index < stop for index in range(size)]
+        spare = order.shape[0] - 5
+        places = [
+            jnp.where(good, first + index, spare) for index, good in enumerate(inside)
+        ]
+        body([order[place] for place in places])
+        return carry
+
+    lax.fori_loop(0, (stop - start + size - 1) // size, step, 0)
+
+
+def for_parts(ints, order, rois, start, stop, size, body):
+    stride = rois + SPARE
+
+    def second(regions):
+        for region in regions:
+            tiles_x = ints[5 * stride + region]
+            wide = (tiles_x > 1).astype(jnp.int32)
+            body(region, 1 - wide, wide)
+
+    for_groups(order, start, stop, size, second)
+
+    def later(at, carry):
+        region = order[at]
+        tiles_x = ints[5 * stride + region]
+
+        def part(index, inner):
+            chunk = index // tiles_x
+            body(region, chunk, index - chunk * tiles_x)
+            return inner
+
+        return lax.fori_loop(2, ints[4 * stride + region], part, carry)
+
+    lax.fori_loop(start, stop, later, 0)
+
+
+def ends_of(order):
+    size = order.shape[0]
+    return [order[size - 4 + at] for at in range(4)]
+
+
 def pool_kernel(
-    rois, floats, ints, mean, scale, shift, p2, p3, p4, p5,
-    pooled_out, centred_out, weight_out, maps, values, totals, sems,
+    rois, floats, ints, order, mean, scale, shift, p2, p3, p4, p5,
+    pooled_out, centred_out, weight_out, maps, values, sems,
 ):
     channels = mean.shape[1] // 2
+    stride = rois + SPARE
     copies = []
     for level, plane in enumerate((p2, p3, p4, p5)):
         cells = TILES[level] * LANES
@@ -148,13 +211,14 @@
             )
         )
         copies[-1].start()
-    ones = jnp.ones((16, LANES), jnp.bfloat16)
+    ones = jnp.ones((16, 8 * LANES), jnp.bfloat16)
 
     def fill(at, carry):
-        maps[pl.ds(channels, 16), pl.ds(pl.multiple_of(at * LANES, LANES), LANES)] = ones
+        lanes = pl.ds(pl.multiple_of(at * 8 * LANES, 8 * LANES), 8 * LANES)
+        maps[pl.ds(channels, 16), lanes] = ones
         return carry
 
-    lax.fori_loop(0, ALL_TILES, fill, 0)
+    lax.fori_loop(0, ALL_TILES // 8, fill, 0)
     extra = PADDED - ALL_TILES
     if extra:
         maps[:, pl.ds(ALL_TILES * LANES, extra * LANES)] = jnp.zeros(
@@ -162,87 +226,82 @@
         )
     for copy in copies:
         copy.wait()
-    low_lane = lax.broadcasted_iota(jnp.int32, (SLOTS, 2 * channels), 1) < channels
 
     def item(region, chunk, tile_x):
         kernel_w, first_tile, across = window_weights(floats, ints, rois, region, chunk, tile_x)
         cells = jnp.concatenate(
             [maps[:, tile_lanes(first_tile, across, at)] for at in range(SPAN)], axis=1
         )
-        result = contract_last(kernel_w, cells)
-        pair = jnp.concatenate(
-            [result[:SLOTS, :channels], result[SLOTS:, :channels]], axis=1
-        )
-        total = jnp.where(
-            low_lane,
-            jnp.broadcast_to(result[:SLOTS, channels : channels + 1], low_lane.shape),
-            jnp.broadcast_to(result[SLOTS:, channels : channels + 1], low_lane.shape),
-        )
-        return pair, total
-
-    def step(at, carry):
-        for lane_at in range(PAIR):
-            region = at * PAIR + lane_at
-            pair, total = item(region, None, None)
-            values[pl.ds(region, SLOTS, stride=rois), :] = pair
-            totals[pl.ds(region, SLOTS, stride=rois), :] = total
-        for lane_at in range(PAIR):
-            region = at * PAIR + lane_at
-            tiles_x = ints[5 * rois + region]
-
-            def more(index, inner):
-                chunk = index // tiles_x
-                pair, total = item(region, chunk, index - chunk * tiles_x)
-                place = pl.ds(region, SLOTS, stride=rois)
-                values[place, :] = values[place, :] + pair
-                totals[place, :] = totals[place, :] + total
-                return inner
-
-            lax.fori_loop(1, ints[4 * rois + region] * tiles_x, more, 0)
-        return carry
-
-    lax.fori_loop(0, rois // PAIR, step, 0)
+        return contract_last(kernel_w, cells)
+
+    def place(region):
+        return pl.ds(region, 2 * SLOTS, stride=stride)
+
+    def first(regions):
+        for region in regions:
+            values[place(region), : channels + 16] = item(region, None, None)
+
+    def further(region, chunk, tile_x):
+        values[place(region), : channels + 16] = values[place(region), : channels + 16] + item(region, chunk, tile_x)
+
+    low_end, low_multi, rest_end, all_end = ends_of(order)
+    for_groups(order, 0, all_end, GROUP, first)
+    for_parts(ints, order, rois, low_end, low_multi, MORE, further)
+    for_parts(ints, order, rois, rest_end, all_end, MORE, further)
+    low_lane = lax.broadcasted_iota(jnp.int32, (rois, LANES), 1) < channels
     for at, slot in enumerate(USED):
-        rows = pl.ds(slot * rois, rois)
         lanes = pl.ds(at * LANES, LANES)
-        total = totals[rows, :]
-        centred = values[rows, :] - mean[...] * total
+        one = values[pl.ds(slot * stride, rois), :]
+        two = values[pl.ds((slot + SLOTS) * stride, rois), :]
+        value = jnp.where(low_lane, one, pltpu.roll(two, channels, 1))
+        total = jnp.where(low_lane, one[:, channels : channels + 1], two[:, channels : channels + 1])
+        centred = value - mean[...] * total
         centred_out[:, lanes] = centred.astype(jnp.bfloat16)
         weight_out[:, lanes] = total.astype(jnp.bfloat16)
         pooled_out[:, lanes] = (centred * scale[...] + shift[...] * total).astype(jnp.bfloat16)
 
 
 def unpool_kernel(
-    rois, floats, ints, base, slope, grads, p2, p3, p4, p5,
+    rois, floats, ints, order, base, slope, grads, p2, p3, p4, p5,
     o2, o3, o4, o5, maps, sums, slots, sems, out_sems,
 ):
     channels = base.shape[0]
-    copies = []
-    for level, plane in enumerate((p2, p3, p4, p5)):
-        cells = TILES[level] * LANES
-        copies.append(
-            pltpu.make_async_copy(
-                plane.at[0], maps.at[:, pl.ds(FIRST[level] * LANES, cells)], sems.at[level]
-            )
+    stride = rois + SPARE
+    planes, outs = (p2, p3, p4, p5), (o2, o3, o4, o5)
+    pieces = [(level, at) for level in range(4) for at in range(4 if level == 0 else 1)]
+
+    def fetch(index):
+        level, at = pieces[index]
+        cells = TILES[level] * LANES // (4 if level == 0 else 1)
+        return pltpu.make_async_copy(
+            planes[level].at[0, :, pl.ds(at * cells, cells)],
+            maps.at[:, pl.ds(FIRST[level] * LANES + at * cells, cells)],
+            sems.at[index],
         )
-        copies[-1].start()
+
+    for index in range(len(pieces)):
+        fetch(index).start()
     for slot in range(SLOTS):
-        rows = pl.ds(slot * rois, rois)
+        rows = pl.ds(slot * stride, rois)
+        slots[pl.ds(slot * stride + rois, SPARE), :] = jnp.zeros((SPARE, LANES), jnp.float32)
         if slot in USED:
             lanes = pl.ds(USED.index(slot) * LANES, LANES)
             slots[rows, :] = grads[:, lanes].astype(jnp.float32)
         else:
             slots[rows, :] = jnp.zeros((rois, LANES), jnp.float32)
-    for copy in copies:
-        copy.wait()
     base_v, slope_v = base[...], slope[...]
 
     def begin(at, carry):
-        lanes = pl.ds(pl.multiple_of(at * LANES, LANES), LANES)
-        sums[:, lanes] = base_v + slope_v * maps[:, lanes].astype(jnp.float32)
+        for part in range(4):
+            lanes = pl.ds(pl.multiple_of((at * 4 + part) * LANES, LANES), LANES)
+            sums[:, lanes] = base_v + slope_v * maps[:, lanes].astype(jnp.float32)
         return carry
 
-    lax.fori_loop(0, ALL_TILES, begin, 0)
+    for index, (level, at) in enumerate(pieces):
+        tiles = TILES[level] // (4 if level == 0 else 1)
+        start = FIRST[level] + at * tiles
+        fetch(index).wait()
+        lax.fori_loop(start // 4, (start + tiles) // 4, begin, 0)
     extra = PADDED - ALL_TILES
     if extra:
         sums[:, pl.ds(ALL_TILES * LANES, extra * LANES)] = jnp.zeros(
@@ -251,45 +310,34 @@
 
     def item(region, chunk, tile_x):
         kernel_w, first_tile, across = window_weights(floats, ints, rois, region, chunk, tile_x)
-        mine = slots[pl.ds(region, SLOTS, stride=rois), :]
+        mine = slots[pl.ds(region, SLOTS, stride=stride), :]
         stacked = jnp.concatenate([mine[:, :channels], mine[:, channels:]], axis=0)
         turned = stacked.T.astype(jnp.bfloat16)
         result = jnp.dot(turned, kernel_w, preferred_element_type=jnp.float32)
-        return result, first_tile, across
-
-    def add(result, first_tile, across):
         for at in range(SPAN):
             lanes = tile_lanes(first_tile, across, at)
             sums[:, lanes] = sums[:, lanes] + result[:, at * LANES : (at + 1) * LANES]
 
-    def step(at, carry):
-        results = [item(at * PAIR + lane_at, None, None) for lane_at in range(PAIR)]
-        for result in results:
-            add(*result)
-        for lane_at in range(PAIR):
-            region = at * PAIR + lane_at
-            tiles_x = ints[5 * rois + region]
-
-            def more(index, inner):
-                chunk = index // tiles_x
-                add(*item(region, chunk, index - chunk * tiles_x))
-                return inner
-
-            lax.fori_loop(1, ints[4 * rois + region] * tiles_x, more, 0)
-        return carry
-
-    lax.fori_loop(0, rois // PAIR, step, 0)
-    copies = []
-    for level, plane in enumerate((o2, o3, o4, o5)):
+    def first(regions):
+        for region in regions:
+            item(region, None, None)
+
+    def send(level):
         cells = TILES[level] * LANES
-        copies.append(
-            pltpu.make_async_copy(
-                sums.at[:, pl.ds(FIRST[level] * LANES, cells)], plane.at[0], out_sems.at[level]
-            )
+        return pltpu.make_async_copy(
+            sums.at[:, pl.ds(FIRST[level] * LANES, cells)], outs[level].at[0], out_sems.at[level]
         )
-        copies[-1].start()
-    for copy in copies:
-        copy.wait()
+
+    low_end, low_multi, rest_end, all_end = ends_of(order)
+    for_groups(order, 0, low_multi, GROUP, first)
+    for_parts(ints, order, rois, low_end, low_multi, MORE, item)
+    send(0).start()
+    for_groups(order, low_multi, all_end, GROUP, first)
+    for_parts(ints, order, rois, rest_end, all_end, MORE, item)
+    for level in range(1, 4):
+        send(level).start()
+    for level in range(4):
+        send(level).wait()
 
 
 ANY = pl.BlockSpec(memory_space=pl.ANY)
@@ -298,42 +346,41 @@
 LIMIT = 60 * 1024 * 1024
 
 
-def pool_maps(floats, ints, mean, scale, shift, planes, rois):
+def pool_maps(floats, ints, order, mean, scale, shift, planes, rois):
     channels = planes[0].shape[1]
     flat = jax.ShapeDtypeStruct((rois, WIDE), jnp.bfloat16)
     return pl.pallas_call(
         functools.partial(pool_kernel, rois),
         out_shape=(flat, flat, flat),
-        in_specs=[SMEM, SMEM, VMEM, VMEM, VMEM, ANY, ANY, ANY, ANY],
+        in_specs=[SMEM, SMEM, SMEM, VMEM, VMEM, VMEM, ANY, ANY, ANY, ANY],
         out_specs=(VMEM, VMEM, VMEM),
         scratch_shapes=[
             pltpu.VMEM((channels + 16, PADDED * LANES), jnp.bfloat16),
-            pltpu.VMEM((SLOTS * rois, LANES), jnp.float32),
-            pltpu.VMEM((SLOTS * rois, LANES), jnp.float32),
+            pltpu.VMEM((2 * SLOTS * (rois + SPARE), LANES), jnp.float32),
             pltpu.SemaphoreType.DMA((4,)),
         ],
         compiler_params=pltpu.CompilerParams(vmem_limit_bytes=LIMIT),
         name="pool",
-    )(floats, ints, mean, scale, shift, *planes)
-
-
-def unpool_maps(floats, ints, base, slope, grads, planes, rois):
+    )(floats, ints, order, mean, scale, shift, *planes)
+
+
+def unpool_maps(floats, ints, order, base, slope, grads, planes, rois):
     channels = planes[0].shape[1]
     return pl.pallas_call(
         functools.partial(unpool_kernel, rois),
         out_shape=tuple(jax.ShapeDtypeStruct(plane.shape, jnp.float32) for plane in planes),
-        in_specs=[SMEM, SMEM, VMEM, VMEM, VMEM, ANY, ANY, ANY, ANY],
+        in_specs=[SMEM, SMEM, SMEM, VMEM, VMEM, VMEM, ANY, ANY, ANY, ANY],
         out_specs=(ANY, ANY, ANY, ANY),
         scratch_shapes=[
             pltpu.VMEM((channels, ALL_TILES * LANES), jnp.bfloat16),
             pltpu.VMEM((channels, PADDED * LANES), jnp.float32),
-            pltpu.VMEM((SLOTS * rois, LANES), jnp.float32),
-            pltpu.SemaphoreType.DMA((4,)),
+            pltpu.VMEM((SLOTS * (rois + SPARE), LANES), jnp.float32),
+            pltpu.SemaphoreType.DMA((7,)),
             pltpu.SemaphoreType.DMA((4,)),
         ],
         compiler_params=pltpu.CompilerParams(vmem_limit_bytes=LIMIT),
         name="unpool",
-    )(floats, ints, base, slope, grads, *planes)
+    )(floats, ints, order, base, slope, grads, *planes)
 
 
 def local(
@@ -399,7 +446,7 @@
     picks = roi_image[None, :] == jnp.arange(4, dtype=jnp.int32)[:, None]
     shift_x = jnp.sum(jnp.where(picks, canvas_offsets[0][:, None], 0), axis=0)
     shift_y = jnp.sum(jnp.where(picks, canvas_offsets[1][:, None], 0), axis=0)
-    floats, ints = region_tables(
+    floats, ints, order = region_tables(
         (roi_boxes[0] + shift_x).astype(jnp.float32),
         (roi_boxes[1] + shift_y).astype(jnp.float32),
         (roi_boxes[2] + shift_x).astype(jnp.float32),
@@ -411,7 +458,7 @@
         return jnp.concatenate([vector, vector])[None]
 
     pooled, centred, weight = pool_maps(
-        floats, ints, twice(mean), twice(scale), twice(norm_bias), planes, rois
+        floats, ints, order, twice(mean), twice(scale), twice(norm_bias), planes, rois
     )
 
     partial_six = jnp.dot(pooled, wide, preferred_element_type=jnp.float32).astype(jnp.bfloat16)
@@ -546,7 +593,7 @@
     def spread(vector):
         return jnp.broadcast_to(vector[:, None], (channels, LANES))
 
-    input_grads = unpool_maps(floats, ints, spread(base), spread(slope), scaled, planes, rois)
+    input_grads = unpool_maps(floats, ints, order, spread(base), spread(slope), scaled, planes, rois)
     return (
         cls_loss,
         box_loss,
@@ -568,9 +615,810 @@
     )
 
 
+MESH = pl.DeviceIdType.MESH
+KEPT = tuple(at for at in range(2 * len(USED)) if at % 2 == 0 or at // 2 < 21)
+LEADING = 42
+SPARES = tuple(at for at in range(2 * len(USED)) if at not in KEPT)
+SMALL = 6
+
+
+def ring_of(rows):
+    return list(range(0, rows, 2)) + list(range(rows - 1, 0, -2))
+
+
+def greet(axis, count):
+    barrier = pltpu.get_barrier_semaphore()
+    me = lax.axis_index(axis)
+    for step in range(1, count):
+        pl.semaphore_signal(
+            barrier,
+            inc=1,
+            device_id={axis: lax.rem(me + step, count)},
+            device_id_type=MESH,
+        )
+
+
+def met(count):
+    pl.semaphore_wait(pltpu.get_barrier_semaphore(), count)
+
+
+def remote(src, dst, sends, recvs, at, axis, peer):
+    return pltpu.make_async_remote_copy(
+        src_ref=src,
+        dst_ref=dst,
+        send_sem=sends.at[at],
+        recv_sem=recvs.at[at],
+        device_id={axis: peer},
+        device_id_type=MESH,
+    )
+
+
+def share(slots, axis, count, sends, recvs, first=0):
+    me = lax.axis_index(axis)
+    copies = [
+        remote(slots.at[me], slots.at[me], sends, recvs, first + step - 1, axis,
+               lax.rem(me + step, count))
+        for step in range(1, count)
+    ]
+    for copy in copies:
+        copy.start()
+    return copies
+
+
+def neighbours(me):
+    core, chip = lax.rem(me, 2), lax.div(me, 2)
+    return me + 1 - 2 * core, me + 2 - 4 * chip
+
+
+class Relay:
+    def __init__(self, view, sends, recvs, first):
+        me = lax.axis_index("col")
+        core, chip = neighbours(me)
+        self.near = remote(view(me), view(me), sends, recvs, first, "col", core)
+        self.far = remote(view(me), view(me), sends, recvs, first + 1, "col", chip)
+        self.passed = remote(view(chip), view(chip), sends, recvs, first + 2, "col", core)
+
+    def start(self):
+        self.far.start()
+        self.near.start()
+
+    def forward(self):
+        self.far.wait_recv()
+        self.passed.start()
+
+    def wait(self):
+        self.near.wait()
+        self.far.wait_send()
+        self.passed.wait()
+
+
+def stats_kernel(
+    rows, pixels, facts, p2, p3, p4, p5, out, maps, slots, sems, sends, recvs
+):
+    channels = maps.shape[0]
+    planes = (p2, p3, p4, p5)
+    pieces = [(level, at) for level in range(4) for at in range(4 if level == 0 else 1)]
+    greet("roi", rows)
+
+    def fetch(index):
+        level, at = pieces[index]
+        cells = TILES[level] * LANES // (4 if level == 0 else 1)
+        return pltpu.make_async_copy(
+            planes[level].at[0, :, pl.ds(at * cells, cells)],
+            maps.at[:, pl.ds(FIRST[level] * LANES + at * cells, cells)],
+            sems.at[index],
+        )
+
+    for index in range(len(pieces)):
+        fetch(index).start()
+
+    def add(at, carry):
+        one, two = carry
+        for part in range(4):
+            lanes = pl.ds(pl.multiple_of((at * 4 + part) * LANES, LANES), LANES)
+            value = maps[:, lanes].astype(jnp.float32)
+            one, two = one + value, two + value * value
+        return one, two
+
+    carry = (jnp.zeros((channels, LANES), jnp.float32),) * 2
+    for index, (level, at) in enumerate(pieces):
+        tiles = TILES[level] // (4 if level == 0 else 1)
+        start = FIRST[level] + at * tiles
+        fetch(index).wait()
+        carry = lax.fori_loop(start // 4, (start + tiles) // 4, add, carry)
+    sums = [jnp.sum(item.T, axis=0, keepdims=True) for item in carry]
+    me = lax.axis_index("roi")
+    slots[me] = jnp.concatenate(
+        [jnp.concatenate(sums, axis=1), facts[1:2], jnp.zeros((6, LANES), jnp.float32)], axis=0
+    )
+    met(rows - 1)
+    for copy in share(slots, "roi", rows, sends, recvs):
+        copy.wait()
+    total = slots[0]
+    for at in range(1, rows):
+        total = total + slots[at]
+    turned = pltpu.roll(total, channels, 1)
+    low = lax.broadcasted_iota(jnp.int32, total.shape, 1) < channels
+    mean = jnp.where(low, total, turned) / pixels
+    inv_std = lax.rsqrt(jnp.where(low, turned, total) / pixels - mean * mean + EPSILON)
+    scale = facts[...] * inv_std
+    out[...] = jnp.concatenate(
+        [mean[:1], scale[:1], inv_std[:1], total[1:2], jnp.zeros((4, LANES), jnp.float32)], axis=0
+    )
+
+
+def gather_small_kernel(rows, cols, mine, out, sends, recvs, col_sends, col_recvs, sem):
+    row, col = lax.axis_index("roi"), lax.axis_index("col")
+    greet("roi", rows)
+    greet("col", cols)
+    own = pltpu.make_async_copy(mine, out.at[col, row], sem)
+    own.start()
+    own.wait()
+    met(rows + cols - 2)
+    copies = [
+        remote(mine, out.at[col, row], sends, recvs, step - 1, "roi", lax.rem(row + step, rows))
+        for step in range(1, rows)
+    ]
+    for copy in copies:
+        copy.start()
+    for copy in copies:
+        copy.wait()
+    relay = Relay(lambda at: out.at[at], col_sends, col_recvs, 0)
+    relay.start()
+    relay.forward()
+    relay.wait()
+
+
+def place_wide(pieces, wide, sems, rows, high):
+    few, piece = pieces.shape[2], pieces.shape[3]
+    copies = []
+    for position, owner in enumerate(ring_of(rows)):
+        span = pl.ds((owner % high) * few, few)
+        lanes = pl.ds((owner // high) * piece, piece)
+        copies.append(
+            pltpu.make_async_copy(
+                pieces.at[position, pl.ds(0, LEADING)],
+                wide.at[pl.ds(0, LEADING), span, lanes],
+                sems.at[position, 0],
+            )
+        )
+        for at in range(LEADING, len(KEPT)):
+            copies.append(
+                pltpu.make_async_copy(
+                    pieces.at[position, at],
+                    wide.at[KEPT[at], span, lanes],
+                    sems.at[position, at - LEADING + 1],
+                )
+            )
+    for copy in copies:
+        copy.start()
+    for at in SPARES:
+        wide[at] = jnp.zeros(wide.shape[1:], wide.dtype)
+    return copies
+
+
+def head_kernel(
+    rows, cols, classes, boxes, pooled, facts, score_bias, small, pieces,
+    g6_all, g7_out, hid6_out, hid7_out, gs_out, scores_out, losses_out,
+    wide, mine, taken, sems, sends, recvs, relay_sends, relay_recvs,
+):
+    me = lax.axis_index("col")
+    rois, hidden = g6_all.shape
+    quarter, piece = rois // cols, hidden // cols
+    greet("col", cols)
+    copies = place_wide(pieces, wide, sems, rows, rows // cols)
+    met(cols - 1)
+    for copy in copies:
+        copy.wait()
+
+    def sending(part, step):
+        lanes = pl.ds(pl.multiple_of(part * piece, piece), piece)
+        peer = lax.rem(me + step, cols)
+        return pltpu.make_async_remote_copy(
+            src_ref=mine.at[peer, :, lanes],
+            dst_ref=taken.at[step - 1, :, lanes],
+            send_sem=sends.at[step - 1, part],
+            recv_sem=recvs.at[step - 1, part],
+            device_id={"col": peer},
+            device_id_type=MESH,
+        )
+
+    def first_layer(part, carry):
+        lanes = pl.ds(pl.multiple_of(part * piece, piece), piece)
+        weights = wide[:, :, lanes].reshape(WIDE, piece)
+        result = jnp.dot(pooled[...], weights, preferred_element_type=jnp.float32)
+        result = result.astype(jnp.bfloat16)
+        for at in range(cols):
+            mine[at, :, lanes] = result[at * quarter : (at + 1) * quarter]
+        for step in range(1, cols):
+            sending(part, step).start()
+        return carry
+
+    lax.fori_loop(0, cols, first_layer, 0)
+    for part in range(cols):
+        for step in range(1, cols):
+            sending(part, step).wait()
+    pre_six = mine[me].astype(jnp.float32)
+    for step in range(1, cols):
+        pre_six = pre_six + taken[step - 1].astype(jnp.float32)
+    bias = jnp.concatenate(
+        [jnp.sum(small[at, 0, 5, :3].astype(jnp.float32), axis=0, keepdims=True) for at in range(cols)],
+        axis=1,
+    )
+    pre_six = pre_six + bias
+    sigma_six = jax.nn.sigmoid(pre_six)
+    hidden_six = (pre_six * sigma_six).astype(jnp.bfloat16)
+    hid6_out[...] = hidden_six
+    deep = [small[at, :, :4].reshape(hidden, piece) for at in range(cols)]
+    head = jnp.concatenate(
+        [small[at, row, 4, :, :LANES] for row in range(rows) for at in range(cols)], axis=0
+    )
+    lane = lax.broadcasted_iota(jnp.int32, (quarter, LANES), 1)
+    pick = (lane == classes + boxes).astype(jnp.bfloat16)
+    pre_seven = contract_last(pick, head)
+    for at in range(cols):
+        pre_seven = pre_seven + contract_last(
+            hidden_six[:, at * piece : (at + 1) * piece], deep[at]
+        )
+    sigma_seven = jax.nn.sigmoid(pre_seven)
+    hidden_seven = (pre_seven * sigma_seven).astype(jnp.bfloat16)
+    hid7_out[...] = hidden_seven
+    scores = jnp.dot(hidden_seven, head, preferred_element_type=jnp.float32) + score_bias[...]
+    scores_out[...] = scores
+    targets, onehot, weights = facts[0], facts[1], facts[2]
+    is_class = lane < classes
+    top = jnp.max(jnp.where(is_class, scores, -jnp.inf), axis=1, keepdims=True)
+    powers = jnp.where(is_class, jnp.exp(jnp.where(is_class, scores - top, 0.0)), 0.0)
+    log_total = top + jnp.log(jnp.sum(powers, axis=1, keepdims=True))
+    picked = jnp.sum(onehot * scores, axis=1, keepdims=True)
+    softmax = jnp.where(is_class, jnp.exp(jnp.where(is_class, scores - log_total, 0.0)), 0.0)
+    misfit = jnp.where(is_class, 0.0, scores - targets)
+    size = jnp.abs(misfit)
+    huber = jnp.where(size < 1.0, 0.5 * misfit * misfit, size - 0.5)
+    class_part = jnp.sum(weights[:, :1] * (log_total - picked), axis=0, keepdims=True)
+    box_part = jnp.sum(jnp.where(is_class, 0.0, weights * huber), axis=0, keepdims=True)
+    losses_out[...] = jnp.concatenate(
+        [
+            jnp.broadcast_to(class_part, (1, LANES)),
+            box_part,
+            jnp.zeros((6, LANES), jnp.float32),
+        ],
+        axis=0,
+    )
+    grads = jnp.where(is_class, softmax - onehot, jnp.clip(misfit, -1.0, 1.0))
+    score_grads = (weights * grads).astype(jnp.bfloat16)
+    gs_out[...] = score_grads
+    slope_seven = sigma_seven * (1.0 + pre_seven * (1.0 - sigma_seven))
+    g7 = (contract_last(score_grads, head) * slope_seven).astype(jnp.bfloat16)
+    g7_out[...] = g7
+    place = pl.ds(pl.multiple_of(me * quarter, quarter), quarter)
+    for at in range(cols):
+        lanes = slice(at * piece, (at + 1) * piece)
+        back = jnp.dot(g7, deep[at], preferred_element_type=jnp.float32)
+        sigma, value = sigma_six[:, lanes], pre_six[:, lanes]
+        back = back * (sigma * (1.0 + value * (1.0 - sigma)))
+        g6_all[place, lanes] = back.astype(jnp.bfloat16)
+    relay = Relay(
+        lambda at: g6_all.at[pl.ds(pl.multiple_of(at * quarter, quarter), quarter)],
+        relay_sends, relay_recvs, 0,
+    )
+    relay.start()
+    relay.forward()
+    relay.wait()
+
+
+def wide_grad_kernel(
+    rows, cols, pooled, g6_all, g7, hid6, hid7, gs, losses,
+    terms, g7_all, gs_all, losses_all,
+    hid6_own, hid7_all, buffers, extras, head_term, out_sems, sends, recvs,
+):
+    me = lax.axis_index("col")
+    rois, hidden = g6_all.shape
+    quarter, piece = rois // cols, hidden // cols
+    high = rows // cols
+    few = buffers.shape[2] // 4
+    ring = ring_of(rows)
+    greet("col", cols)
+
+    def block(at):
+        return pl.ds(pl.multiple_of(at * quarter, quarter), quarter)
+
+    g7_all[block(me), :] = g7[...]
+    hid7_all[block(me), :] = hid7[...]
+    gs_all[block(me), :] = gs[...]
+    losses_all[me] = losses[...]
+    own = pl.ds(pl.multiple_of(me * piece, piece), piece)
+    hid6_own[block(me), :] = hid6[:, own]
+    met(cols - 1)
+    relays = [
+        Relay(lambda at: g7_all.at[block(at)], sends, recvs, 0),
+        Relay(lambda at: hid7_all.at[block(at)], sends, recvs, 3),
+    ]
+    for relay in relays:
+        relay.start()
+    copies = []
+    for step in range(1, cols):
+        peer = lax.rem(me + step, cols)
+        theirs = pl.ds(pl.multiple_of(peer * piece, piece), piece)
+        copies.append(
+            remote(hid6.at[:, theirs], hid6_own.at[block(me)], sends, recvs, 5 + step, "col", peer)
+        )
+        copies.append(
+            remote(gs, gs_all.at[block(me)], sends, recvs, 8 + step, "col", peer)
+        )
+        copies.append(
+            remote(losses, losses_all.at[me], sends, recvs, 11 + step, "col", peer)
+        )
+    for copy in copies:
+        copy.start()
+
+    def leaving(slot, at):
+        size = 4 * few
+        span = pl.ds(pl.multiple_of(at * size, size), size)
+        return pltpu.make_async_copy(buffers.at[slot], terms.at[:, span], out_sems.at[slot])
+
+    def step(pair, carry):
+        for slot in range(2):
+            at = pair * 2 + slot
+
+            @pl.when(pair > 0)
+            def _():
+                leaving(slot, at - 2).wait()
+
+            lanes = pl.ds(pl.multiple_of(at * 2 * LANES, 2 * LANES), 2 * LANES)
+            result = contract_first(pooled[:, lanes], g6_all[...]).astype(jnp.bfloat16)
+            for position, owner in enumerate(ring):
+                columns = slice((owner // high) * piece, (owner // high + 1) * piece)
+                for part in range(4):
+                    first = (part * high + owner % high) * few
+                    buffers[slot, position, part * few : (part + 1) * few, :] = result[
+                        first : first + few, columns
+                    ]
+            leaving(slot, at).start()
+        return carry
+
+    pairs = len(USED) // 4
+    lax.fori_loop(0, pairs, step, 0)
+    for relay in relays:
+        relay.forward()
+    for relay in relays:
+        relay.wait()
+    for copy in copies:
+        copy.wait()
+    deep_term = contract_first(g7_all[...], hid6_own[...]).astype(jnp.bfloat16)
+    head_term[...] = contract_first(hid7_all[...], gs_all[...])
+    owned, per = hidden // rows, hidden // (rows * cols)
+    for position, owner in enumerate(ring):
+        extras[position, :owned, :] = deep_term[owner * owned : (owner + 1) * owned]
+        mine = pl.ds(pl.multiple_of(owner * owned + me * per, per), per)
+        extras[position, owned : owned + per, :] = jnp.concatenate(
+            [head_term[mine, :], jnp.zeros((per, piece - LANES), jnp.float32)], axis=1
+        ).astype(jnp.bfloat16)
+    for slot in range(2):
+        leaving(slot, 2 * pairs - 2 + slot).wait()
+    copies = [
+        pltpu.make_async_copy(
+            extras.at[:, pl.ds(at * few, few)],
+            terms.at[:, pl.ds(SPARES[at] * few, few)],
+            out_sems.at[2 + at],
+        )
+        for at in range((owned + per) // few)
+    ]
+    for copy in copies:
+        copy.start()
+    for copy in copies:
+        copy.wait()
+
+
+def pool_grad_kernel(
+    rows, cols, pixels, g6_all, g7_all, gs_all, losses_all, centred, weight, stats, pieces,
+    grads, totals, base, slope, wide, slots, sems, sends, recvs,
+):
+    row, col = lax.axis_index("roi"), lax.axis_index("col")
+    rois, hidden = g6_all.shape
+    channels = base.shape[0]
+    piece = hidden // cols
+    greet("roi", rows)
+    copies = place_wide(pieces, wide, sems, rows, rows // cols)
+    own = pl.ds(pl.multiple_of(col * piece, piece), piece)
+
+    def columns(values):
+        return jnp.sum(values.astype(jnp.float32), axis=0, keepdims=True)
+
+    def as_rows(vector):
+        return [
+            vector[:, at * LANES : (at + 1) * LANES] for at in range(vector.shape[1] // LANES)
+        ]
+
+    bias_rows = as_rows(columns(g6_all[:, own])) + as_rows(columns(g7_all[...]))
+    bias_rows += [columns(gs_all[...])]
+    losses = losses_all[0]
+    for at in range(1, cols):
+        losses = losses + losses_all[at]
+    for copy in copies:
+        copy.wait()
+    scale = stats[1:2]
+
+    def step(at, carry):
+        gain, shift = carry
+        lanes = pl.ds(pl.multiple_of(at * 2 * LANES, 2 * LANES), 2 * LANES)
+        weights = wide[pl.ds(at * 4, 4)].reshape(2 * LANES, hidden)
+        result = contract_last(g6_all[...], weights)
+        with_centred = result * centred[:, lanes].astype(jnp.float32)
+        with_weight = result * weight[:, lanes].astype(jnp.float32)
+        both = jnp.concatenate([scale, scale], axis=1)
+        grads[:, lanes] = (result * both).astype(jnp.bfloat16)
+        for half in range(2):
+            part = slice(half * LANES, (half + 1) * LANES)
+            gain = gain + jnp.sum(with_centred[:, part].reshape(rois // 8, 8, LANES), axis=0)
+            shift = shift + jnp.sum(with_weight[:, part].reshape(rois // 8, 8, LANES), axis=0)
+        return gain, shift
+
+    nothing = jnp.zeros((8, LANES), jnp.float32)
+    gain, shift = lax.fori_loop(0, len(USED) // 2, step, (nothing, nothing))
+    low = lax.broadcasted_iota(jnp.int32, (8, LANES), 1) < channels
+    both = jnp.where(
+        low, gain + pltpu.roll(gain, channels, 1), shift + pltpu.roll(shift, channels, 1)
+    )
+    both = jnp.sum(both, axis=0, keepdims=True)
+    lines = [both] + bias_rows + [losses[:2]]
+    count = 1 + len(bias_rows) + 2
+    lines.append(jnp.zeros((16 - count, LANES), jnp.float32))
+    slots[row] = jnp.concatenate(lines, axis=0)
+    met(rows - 1)
+    for copy in share(slots, "roi", rows, sends, recvs):
+        copy.wait()
+    total = slots[0]
+    for at in range(1, rows):
+        total = total + slots[at]
+    gain_grad = total[:1] * stats[2:3]
+    totals[...] = jnp.concatenate([total[:15], gain_grad], axis=0)
+    slope_row = -stats[1:2] * stats[2:3] * gain_grad / pixels
+    shift_grad = pltpu.roll(jnp.broadcast_to(total[:1], (8, LANES)), channels, 1)[:1]
+    base_row = -stats[1:2] * shift_grad / pixels - slope_row * stats[:1]
+    slope[...] = jnp.broadcast_to(slope_row[:, :channels], (LANES, channels)).T
+    base[...] = jnp.broadcast_to(base_row[:, :channels], (LANES, channels)).T
+
+
+def restore_kernel(few, term, out, half):
+    for part in range(out.shape[1] // LANES):
+        lanes = slice(part * LANES, (part + 1) * LANES)
+        for slot in range(len(KEPT)):
+            at = KEPT[slot]
+            place = pl.ds(at // 2 % 7 * 7 + at // 14 + 4 * (at % 2), few, stride=49)
+            half[part, place, :] = term[at * few : (at + 1) * few, lanes].astype(jnp.float32)
+        out[:, lanes] = half[part]
+
+
+def comm_params(number):
+    return pltpu.CompilerParams(
+        vmem_limit_bytes=LIMIT, collective_id=number, has_side_effects=True
+    )
+
+
+def shaped(shape, dtype):
+    return jax.ShapeDtypeStruct(shape, dtype)
+
+
+def statistics(facts, planes, rows, pixels):
+    channels = planes[0].shape[1]
+    return pl.pallas_call(
+        functools.partial(stats_kernel, rows, pixels),
+        out_shape=shaped((8, LANES), jnp.float32),
+        in_specs=[VMEM, ANY, ANY, ANY, ANY],
+        out_specs=VMEM,
+        scratch_shapes=[
+            pltpu.VMEM((channels, ALL_TILES * LANES), jnp.bfloat16),
+            pltpu.VMEM((rows, 8, LANES), jnp.float32),
+            pltpu.SemaphoreType.DMA((7,)),
+            pltpu.SemaphoreType.DMA((rows - 1,)),
+            pltpu.SemaphoreType.DMA((rows - 1,)),
+        ],
+        compiler_params=comm_params(0),
+        name="statistics",
+    )(facts, *planes)
+
+
+def gather_small(mine, rows, cols):
+    return pl.pallas_call(
+        functools.partial(gather_small_kernel, rows, cols),
+        out_shape=shaped((cols, rows) + mine.shape, mine.dtype),
+        in_specs=[VMEM],
+        out_specs=VMEM,
+        scratch_shapes=[
+            pltpu.SemaphoreType.DMA((rows - 1,)),
+            pltpu.SemaphoreType.DMA((rows - 1,)),
+            pltpu.SemaphoreType.DMA((3,)),
+            pltpu.SemaphoreType.DMA((3,)),
+            pltpu.SemaphoreType.DMA,
+        ],
+        compiler_params=comm_params(1),
+        name="gather_small",
+    )(mine)
+
+
+def run_head(pooled, facts, score_bias, small, pieces, rows, cols, classes, boxes):
+    rois, channels = pooled.shape[0], LANES // 2
+    quarter, hidden = rois // cols, pieces.shape[3] * cols
+    bf16, f32 = jnp.bfloat16, jnp.float32
+    return pl.pallas_call(
+        functools.partial(head_kernel, rows, cols, classes, boxes),
+        out_shape=(
+            shaped((rois, hidden), bf16),
+            shaped((quarter, hidden), bf16),
+            shaped((quarter, hidden), bf16),
+            shaped((quarter, hidden), bf16),
+            shaped((quarter, LANES), bf16),
+            shaped((quarter, LANES), f32),
+            shaped((8, LANES), f32),
+        ),
+        in_specs=[VMEM, VMEM, VMEM, VMEM, ANY],
+        out_specs=(VMEM,) * 7,
+        scratch_shapes=[
+            pltpu.VMEM((2 * len(USED), channels, hidden), bf16),
+            pltpu.VMEM((cols, quarter, hidden), bf16),
+            pltpu.VMEM((cols - 1, quarter, hidden), bf16),
+            pltpu.SemaphoreType.DMA((rows, 8)),
+            pltpu.SemaphoreType.DMA((cols - 1, cols)),
+            pltpu.SemaphoreType.DMA((cols - 1, cols)),
+            pltpu.SemaphoreType.DMA((3,)),
+            pltpu.SemaphoreType.DMA((3,)),
+        ],
+        compiler_params=comm_params(2),
+        name="head",
+    )(pooled, facts, score_bias, small, pieces)
+
+
+def wide_grads(pooled, g6_all, g7, hid6, hid7, gs, losses, rows, cols):
+    rois, hidden = g6_all.shape
+    piece, few = hidden // cols, LANES // 2 // (rows // cols)
+    owned, per = hidden // rows, hidden // (rows * cols)
+    bf16, f32 = jnp.bfloat16, jnp.float32
+    return pl.pallas_call(
+        functools.partial(wide_grad_kernel, rows, cols),
+        out_shape=(
+            shaped((rows, 2 * len(USED) * few, piece), bf16),
+            shaped((rois, hidden), bf16),
+            shaped((rois, LANES), bf16),
+            shaped((cols, 8, LANES), f32),
+        ),
+        in_specs=[VMEM] * 7,
+        out_specs=(ANY, VMEM, VMEM, VMEM),
+        scratch_shapes=[
+            pltpu.VMEM((rois, piece), bf16),
+            pltpu.VMEM((rois, hidden), bf16),
+            pltpu.VMEM((2, rows, 4 * few, piece), bf16),
+            pltpu.VMEM((rows, owned + per, piece), bf16),
+            pltpu.VMEM((hidden, LANES), f32),
+            pltpu.SemaphoreType.DMA((2 + len(SPARES),)),
+            pltpu.SemaphoreType.DMA((15,)),
+            pltpu.SemaphoreType.DMA((15,)),
+        ],
+        compiler_params=comm_params(3),
+        name="wide_grads",
+    )(pooled, g6_all, g7, hid6, hid7, gs, losses)
+
+
+def pool_grads(g6_all, g7_all, gs_all, losses_all, centred, weight, stats, pieces, rows, cols, pixels):
+    rois, hidden = g6_all.shape
+    channels = LANES // 2
+    bf16, f32 = jnp.bfloat16, jnp.float32
+    return pl.pallas_call(
+        functools.partial(pool_grad_kernel, rows, cols, pixels),
+        out_shape=(
+            shaped((rois, WIDE), bf16),
+            shaped((16, LANES), f32),
+            shaped((channels, LANES), f32),
+            shaped((channels, LANES), f32),
+        ),
+        in_specs=[VMEM] * 7 + [ANY],
+        out_specs=(VMEM,) * 4,
+        scratch_shapes=[
+            pltpu.VMEM((2 * len(USED), channels, hidden), bf16),
+            pltpu.VMEM((rows, 16, LANES), f32),
+            pltpu.SemaphoreType.DMA((rows, 8)),
+            pltpu.SemaphoreType.DMA((rows - 1,)),
+            pltpu.SemaphoreType.DMA((rows - 1,)),
+        ],
+        compiler_params=comm_params(4),
+        name="pool_grads",
+    )(g6_all, g7_all, gs_all, losses_all, centred, weight, stats, pieces)
+
+
+def restore(term, few):
+    return pl.pallas_call(
+        functools.partial(restore_kernel, few),
+        out_shape=shaped((49 * few, term.shape[1]), jnp.float32),
+        in_specs=[VMEM],
+        out_specs=VMEM,
+        scratch_shapes=[pltpu.VMEM((term.shape[1] // LANES, 49 * few, LANES), jnp.float32)],
+        compiler_params=pltpu.CompilerParams(vmem_limit_bytes=LIMIT),
+        name="restore",
+    )(term)
+
+
+def targets_of(mine_boxes, mine_goals):
+    prop_width = mine_boxes[2] - mine_boxes[0]
+    prop_height = mine_boxes[3] - mine_boxes[1]
+    prop_cx = mine_boxes[0] + 0.5 * prop_width
+    prop_cy = mine_boxes[1] + 0.5 * prop_height
+    goal_width = mine_goals[2] - mine_goals[0]
+    goal_height = mine_goals[3] - mine_goals[1]
+    goal_cx = mine_goals[0] + 0.5 * goal_width
+    goal_cy = mine_goals[1] + 0.5 * goal_height
+    return jnp.stack(
+        [
+            10.0 * (goal_cx - prop_cx) / prop_width,
+            10.0 * (goal_cy - prop_cy) / prop_height,
+            5.0 * jnp.log(goal_width / prop_width),
+            5.0 * jnp.log(goal_height / prop_height),
+        ],
+        axis=1,
+    )
+
+
+def decode(mine_boxes, deltas):
+    prop_width = mine_boxes[2] - mine_boxes[0]
+    prop_height = mine_boxes[3] - mine_boxes[1]
+    prop_cx = mine_boxes[0] + 0.5 * prop_width
+    prop_cy = mine_boxes[1] + 0.5 * prop_height
+    centre_x = prop_cx + deltas[:, 0] / 10.0 * prop_width
+    centre_y = prop_cy + deltas[:, 1] / 10.0 * prop_height
+    new_width = prop_width * jnp.exp(deltas[:, 2] / 5.0)
+    new_height = prop_height * jnp.exp(deltas[:, 3] / 5.0)
+    return jnp.stack(
+        [
+            centre_x - 0.5 * new_width,
+            centre_y - 0.5 * new_height,
+            centre_x + 0.5 * new_width,
+            centre_y + 0.5 * new_height,
+        ]
+    ) / (CANVAS // 2)
+
+
+def local_near(
+    p2, p3, p4, p5, norm_gain, norm_bias, fc6_weight, fc6_bias, fc7_weight, fc7_bias,
+    cls_weight, cls_bias, box_weight, box_bias, roi_boxes, roi_level, roi_image,
+    canvas_offsets, labels, target_boxes, valid,
+):
+    channels = p2.shape[1]
+    rois = roi_level.shape[0]
+    cols = lax.axis_size("col")
+    rows = lax.axis_size("roi")
+    piece = fc6_bias.shape[0]
+    high = rows // cols
+    few = channels // high
+    planes = (p2, p3, p4, p5)
+    pixels = rows * sum(plane.shape[2] for plane in planes)
+    ring = ring_of(rows)
+    per = fc7_bias.shape[0]
+    classes, boxes = cls_weight.shape[1], box_weight.shape[1]
+    bf16, f32 = jnp.bfloat16, jnp.float32
+
+    block = fc6_weight.reshape(few, 7, 7, piece)
+    block = jnp.pad(block, ((0, 0), (0, 0), (0, 1), (0, 0))).reshape(few, 7, 2, 4, piece)
+    block = block.transpose(3, 1, 2, 0, 4).reshape(2 * len(USED), few, piece)
+    block = jnp.concatenate([block[:LEADING], block[LEADING::2]])
+    pairs = [
+        ((kappa * high + rho % high) * cols + rho // high, rho * cols + kappa)
+        for rho in range(rows)
+        for kappa in range(cols)
+    ]
+    block = lax.ppermute(block, ("roi", "col"), pairs)
+    pieces = lax.all_gather(block, "roi", axis=0, axis_index_groups=[ring])
+
+    head = jnp.concatenate([cls_weight, box_weight, fc7_bias[:, None]], axis=1)
+    head = jnp.pad(head, ((0, 0), (0, piece - head.shape[1])))
+    bias_high = fc6_bias.astype(bf16)
+    rest = fc6_bias - bias_high.astype(f32)
+    bias_mid = rest.astype(bf16)
+    bias_low = (rest - bias_mid.astype(f32)).astype(bf16)
+    bias = jnp.pad(jnp.stack([bias_high, bias_mid, bias_low]), ((0, few - 3), (0, 0)))
+    small = jnp.concatenate([fc7_weight, head, bias], axis=0).reshape(SMALL, few, piece)
+
+    def twice(vector):
+        return jnp.concatenate([vector, vector])[None]
+
+    count = jnp.sum(valid.astype(f32))
+    norm_facts = jnp.concatenate(
+        [twice(norm_gain), jnp.full((1, LANES), count), jnp.zeros((6, LANES), f32)]
+    )
+    stats = statistics(norm_facts, planes, rows, float(pixels))
+    valid_total = stats[3, 0]
+
+    picks = roi_image[None, :] == jnp.arange(4, dtype=jnp.int32)[:, None]
+    shift_x = jnp.sum(jnp.where(picks, canvas_offsets[0][:, None], 0), axis=0)
+    shift_y = jnp.sum(jnp.where(picks, canvas_offsets[1][:, None], 0), axis=0)
+    floats, ints, order = region_tables(
+        (roi_boxes[0] + shift_x).astype(f32),
+        (roi_boxes[1] + shift_y).astype(f32),
+        (roi_boxes[2] + shift_x).astype(f32),
+        (roi_boxes[3] + shift_y).astype(f32),
+        roi_level,
+    )
+    pooled, centred, weight = pool_maps(
+        floats, ints, order, stats[:1], stats[1:2], twice(norm_bias), planes, rois
+    )
+    small = gather_small(small, rows, cols)
+
+    quarter = rois // cols
+    first_row = lax.axis_index("col") * quarter
+    mine_labels = lax.dynamic_slice_in_dim(labels, first_row, quarter)
+    mine_valid = lax.dynamic_slice_in_dim(valid, first_row, quarter).astype(f32)
+    mine_boxes = lax.dynamic_slice_in_dim(roi_boxes, first_row, quarter, axis=1).astype(f32)
+    mine_goals = lax.dynamic_slice_in_dim(target_boxes, first_row, quarter, axis=1).astype(f32)
+    foreground = mine_valid * (mine_labels > 0).astype(f32)
+    loss_scale = rois * rows / valid_total
+    lane = jnp.arange(LANES, dtype=jnp.int32)[None, :]
+    after = LANES - classes - boxes
+    facts = jnp.stack(
+        [
+            jnp.pad(targets_of(mine_boxes, mine_goals), ((0, 0), (classes, after))),
+            (mine_labels[:, None] == lane).astype(f32),
+            loss_scale
+            * jnp.where(
+                lane < classes,
+                mine_valid[:, None],
+                jnp.where(lane < classes + boxes, foreground[:, None], 0.0),
+            ),
+        ]
+    )
+    score_bias = jnp.pad(jnp.concatenate([cls_bias, box_bias]), (0, after))[None]
+    g6_all, g7, hid6, hid7, gs, scores, losses = run_head(
+        pooled, facts, score_bias, small, pieces, rows, cols, classes, boxes
+    )
+    decoded = decode(mine_boxes, scores[:, classes : classes + boxes])
+
+    terms, g7_all, gs_all, losses_all = wide_grads(
+        pooled, g6_all, g7, hid6, hid7, gs, losses, rows, cols
+    )
+    wide_rows = terms.shape[1]
+    term = lax.psum_scatter(
+        terms.reshape(rows * wide_rows, piece), "roi", scatter_dimension=0, tiled=True,
+        axis_index_groups=[ring],
+    )
+    back = lax.ppermute(term, ("roi", "col"), [(there, here) for here, there in pairs])
+    fc6_weight_grad = restore(back, few)
+    extra = [
+        term[SPARES[at] * few : (SPARES[at] + 1) * few].astype(f32)
+        for at in range((fc7_weight.shape[0] + per) // few)
+    ]
+    fc7_weight_grad = jnp.concatenate(extra[:-1], axis=0)
+    cls_weight_grad = extra[-1][:, :classes]
+    box_weight_grad = extra[-1][:, classes : classes + boxes]
+
+    grads, totals, base, slope = pool_grads(
+        g6_all, g7_all, gs_all, losses_all, centred, weight, stats, pieces, rows, cols,
+        float(pixels),
+    )
+    input_grads = unpool_maps(floats, ints, order, base, slope, grads, planes, rois)
+    fc6_bias_grad = totals[1 : 1 + piece // LANES].reshape(-1)
+    seven = totals[1 + piece // LANES :][: cols * piece // LANES].reshape(-1)
+    place = (lax.axis_index("roi") * cols + lax.axis_index("col")) * per
+    fc7_bias_grad = lax.dynamic_slice_in_dim(seven, place, per)
+    line = 1 + (cols + 1) * piece // LANES
+    return (
+        totals[line + 1, 0] / (rois * rows),
+        jnp.sum(totals[line + 2]) / (rois * rows),
+        decoded,
+        *input_grads,
+        totals[15, :channels],
+        totals[0, channels:],
+        fc6_weight_grad,
+        fc6_bias_grad,
+        fc7_weight_grad,
+        fc7_bias_grad,
+        cls_weight_grad,
+        totals[line, :classes],
+        box_weight_grad,
+        totals[line, classes : classes + boxes],
+    )
+
+
 def solution(mesh):
+    near = mesh.shape["roi"] == 2 * mesh.shape["col"] and mesh.shape["col"] == 4
     return jax.shard_map(
-        local,
+        local_near if near else local,
         mesh=mesh,
         in_specs=(
             P("roi", "col", None),

time: 602 us -> 389 us (0.65)
  local copies, waits for them, and re-layouts: 89.2 us -> 21.2 us
  blocking collectives: 67.1 us -> 0 us
  waiting for transfers between devices: 149 us -> 94.3 us
  matrix products: 27.7 us -> 0 us
  Pallas kernels: 213 us -> 236 us
  other arithmetic: 22.9 us -> 10.5 us
    pallas_call x0 -> x6, Pallas kernels: none -> 132 us  [the longest x1 48.4 us: gather_small(): pl.pallas_call(functools.partial(gather_small_kernel, rows, cols), out_sh...]
    psum x2 -> x0, blocking collectives: 58.5 us -> none  [the longest x1 39 us: local(): lax.psum((first_sum, second_sum, local_valid), 'roi')]
    pallas_call x1, Pallas kernels: 114 us -> 58.1 us  [unpool_maps(): pl.pallas_call(functools.partial(unpool_kernel, rois), out_shape=tuple((j...]
    pallas_call x1, Pallas kernels: 98.6 us -> 45.7 us  [pool_maps(): pl.pallas_call(functools.partial(pool_kernel, rois), out_shape=(flat, fla...]
    reduce_scatter x3 -> x1, waiting for transfers between devices: 107 us -> 57.3 us  [local_near(): lax.psum_scatter(terms.reshape(rows * wide_rows, piece), 'roi', scatter_d...]
    reshape x11 -> x6, local copies, waits for them, and re-layouts: 51.9 us -> 4.86 us  [the longest x1 1.36 us: local_near(): block = fc6_weight.reshape(few, 7, 7, piece)]
    dot_general x9 -> x0, matrix products: 27.7 us -> none  [the longest x3 13.7 us: contract_last(): lax.dot_general(left_m, right_m, (((1,), (1,)), ((), ())), preferred_elem...]
    unnamed x37 -> x36, local copies, waits for them, and re-layouts: 11.3 us -> 2.64 us
  transfers between devices with their start and end apart: 7 -> 4, of which waited for: 3 -> 2; matrix products, arithmetic and copies ran while one was open for 16% -> 7% of each run, Pallas kernels for 36% -> 48%
where the time goes in v2:
time: 389 us; the launch traced here: 386 us
  Pallas kernels  236 us (61%)
  waiting for transfers between devices  94.3 us (24%)
  local copies, waits for them, and re-layouts  21.2 us (5%)
  between operations  18.8 us (5%)
  other arithmetic  10.5 us (3%)
  starting transfers between devices  5.43 us (1%)
    pallas_call x1, Pallas kernels, unpool_maps(): pl.pallas_call(functools.partial(unpool_kernel, rois), out_shape=tuple((j...  58.1 us
    reduce_scatter x1, waiting for transfers between devices, local_near(): lax.psum_scatter(terms.reshape(rows * wide_rows, piece), 'roi', scatter_d...  57.3 us
    pallas_call x1, Pallas kernels, gather_small(): pl.pallas_call(functools.partial(gather_small_kernel, rows, cols), out_sh...  48.4 us
    pallas_call x1, Pallas kernels, pool_maps(): pl.pallas_call(functools.partial(pool_kernel, rois), out_shape=(flat, fla...  45.7 us
    ppermute x1, waiting for transfers between devices, local_near(): block = lax.ppermute(block, ('roi', 'col'), pairs)  37 us
    pallas_call x1, Pallas kernels, run_head(): pl.pallas_call(functools.partial(head_kernel, rows, cols, classes, boxes)...  28 us
    pallas_call x1, Pallas kernels, pool_grads(): pl.pallas_call(functools.partial(pool_grad_kernel, rows, cols, pixels), o...  23 us
    pallas_call x1, Pallas kernels, wide_grads(): pl.pallas_call(functools.partial(wide_grad_kernel, rows, cols), out_shape...  18.6 us
  transfers between devices with their start and end apart: 4, of which 2 were waited for; matrix products, arithmetic and copies ran while one was open for 7% of the time, Pallas kernels for 48%

profile of v2, /device:TPU:12, one launch (start us, length us, event | category | flops | bytes accessed | tf_op | source)
XLA Modules:
  0.0 386.4 jit_solution(5378561841199639772)
XLA Ops:
  7.2 1.4 reshape.447
  8.8 0.2 reshape.448
  9.1 0.2 copy.81
  9.3 0.2 copy.80
  9.6 2.9 collective-permute-start
  12.4 37.0 %collective-permute-done = bf16[49,32,256]{2,1,0:T(8,128)(2,1)S(1)} collective-permute-done((bf16[49,32,256]{2,1,0:T(8,128)(2,1)S(1)}, bf16[49,32,256]{2,1,0:T(8,128)(2,1)S(1)}, u32[]{:S(2)}, u32[]{:S(2)}) %collective-permute-start) | collective-permute-done | bytes 802848 | tf_op jit(solution)/shard_map/ppermute | solution.py:1307
  49.4 0.9 copy-done.1
  50.5 0.7 convert_reduce_fusion.2
  51.4 0.7 reshape.445.ints
  52.1 0.7 reshape.444.floats
  52.8 0.6 convert_reduce_fusion.1
  53.4 0.7 pad.58.clone
  54.2 0.8 dynamic-slice_convert_fusion
  55.2 0.7 maximum_maximum_fusion.facts
  55.9 11.8 %statistics.1.stats = f32[8,128]{1,0:T(8,128)} custom-call(f32[8,128]{1,0:T(8,128)} %maximum_maximum_fusion.facts, bf16[1,64,65536]{2,1,0:T(8,128)(2,1)} %p2.5, bf16[1,64,16384]{2,1,0:T(8,128)(2,1)} %p3.5, bf16[1,64,4096]{2,1,0:T(8,128)(2,1)} %p4.5, bf16[1,64,1024]{2,1,0:T(8,128)(2,1)} %p5.5), custom_call_target="tpu_custom_call" | custom-call | tf_op jit(solution)/shard_map/statistics/pallas_call | solution.py:1105
  67.7 1.2 slice.150
  69.2 0.6 pad_maximum_fusion.2
  69.9 48.4 %gather_small.1.small = bf16[4,8,6,32,256]{4,3,2,1,0:T(8,128)(2,1)} custom-call(bf16[6,32,256]{2,1,0:T(8,128)(2,1)} %bitcast.136), custom_call_target="tpu_custom_call" | custom-call | tf_op jit(solution)/shard_map/gather_small/pallas_call | solution.py:1123
  119.0 0.2 convert_reduce_fusion
  119.4 3.3 concatenate.38.order
  122.6 0.6 maximum_bitcast_fusion.1.shift
  123.2 1.3 fusion.46
  124.5 45.7 %pool.1 = (bf16[384,3584]{1,0:T(8,128)(2,1)}, bf16[384,3584]{1,0:T(8,128)(2,1)}, bf16[384,3584]{1,0:T(8,128)(2,1)}) custom-call(f32[2744]{0:T(1024)} %reshape.444.floats, s32[2352]{0:T(1024)} %reshape.445.ints, s32[404]{0:T(512)} %concatenate.38.order, f32[1,128]{1,0:T(1,128)} %get-tuple-element.178.mean, f32[1,128]{1,0:T(1,128)} %get-tuple-element.177.scale, ...), custom_call_target="tpu_custom_call" | custom-call | tf_op jit(solution)/shard_map/pool/pallas_call | solution.py:352
  170.2 0.6 fusion.36.score_bias
  170.8 0.8 compare_select_fusion
  171.8 0.7 pad_maximum_fusion.1.facts
  172.5 28.0 %head.1 = (bf16[384,1024]{1,0:T(8,128)(2,1)}, bf16[96,1024]{1,0:T(8,128)(2,1)}, bf16[96,1024]{1,0:T(8,128)(2,1)}, bf16[96,1024]{1,0:T(8,128)(2,1)}, bf16[96,128]...) custom-call(bf16[384,3584]{1,0:T(8,128)(2,1)} %get-tuple-element.39.pooled, ...), custom_call_target="tpu_custom_call" | custom-call | tf_op jit(solution)/shard_map/head/pallas_call | solution.py:1144
  200.4 18.6 %wide_grads.1 = (bf16[8,1792,256]{2,1,0:T(8,128)(2,1)}, bf16[384,1024]{1,0:T(8,128)(2,1)}, bf16[384,128]{1,0:T(8,128)(2,1)}, f32[4,8,128]{2,1,0:T(8,128)}) custom-call(bf16[384,3584]{1,0:T(8,128)(2,1)} %get-tuple-element.39.pooled, bf16[384,1024]{1,0:T(8,128)(2,1)} %get-tuple-element.40.g6_all, bf16[96,1024]{1,0:T(8,128)(2,1)} %get-tuple-element.41.g7, ...), custom_call_target="tpu_custom_call" | custom-call | tf_op jit(solution)/shard_map/wide_grads/pallas_call | solution.py:1177
  219.1 23.0 %pool_grads.1 = (bf16[384,3584]{1,0:T(8,128)(2,1)}, f32[16,128]{1,0:T(8,128)}, f32[64,128]{1,0:T(8,128)}, f32[64,128]{1,0:T(8,128)}) custom-call(bf16[384,1024]{1,0:T(8,128)(2,1)} %get-tuple-element.40.g6_all, bf16[384,1024]{1,0:T(8,128)(2,1)} %get-tuple-element.46.g7_all, bf16[384,128]{1,0:T(8,128)(2,1)} %get-tuple-element.47.gs_all, ...), custom_call_target="tpu_custom_call" | custom-call | tf_op jit(solution)/shard_map/pool_grads/pallas_call | solution.py:1206
  242.2 0.2 exponential_reduce_fusion.1
  242.4 1.3 slice_bitcast_fusion.2
  243.7 1.2 slice_bitcast_fusion.3
  244.9 0.7 slice_bitcast_fusion
  245.6 57.3 %reduce-scatter.2.cloned.1.call-done = bf16[1792,256]{1,0:T(8,128)(2,1)} async-done(((bf16[14336,256]{1,0:T(8,128)(2,1)}), bf16[1792,256]{1,0:T(8,128)(2,1)}) %reduce-scatter.2.cloned.1.call-update) | async-done | bytes 917520 | tf_op jit(solution)/shard_map/reduce_scatter | solution.py:1376
  302.9 2.5 collective-permute-start.1
  305.4 1.3 slice_reduce_fusion.4
  306.7 1.2 slice.154
  307.9 0.6 dynamic_slice.19
  309.7 58.1 %unpool.1 = (f32[1,64,65536]{2,1,0:T(8,128)}, f32[1,64,16384]{2,1,0:T(8,128)}, f32[1,64,4096]{2,1,0:T(8,128)}, f32[1,64,1024]{2,1,0:T(8,128)}) custom-call(f32[2744]{0:T(1024)} %reshape.444.floats, s32[2352]{0:T(1024)} %reshape.445.ints, s32[404]{0:T(512)} %concatenate.38.order, f32[64,128]{1,0:T(8,128)} %get-tuple-element.53.base, ...), custom_call_target="tpu_custom_call" | custom-call | tf_op jit(solution)/shard_map/unpool/pallas_call | solution.py:369
  367.9 0.6 maximum_multiply_fusion
  368.5 1.3 slice_bitcast_fusion.4
  369.7 1.2 slice_bitcast_fusion.1
  371.0 0.8 slice_convert_fusion
  371.8 0.6 slice.179
  372.4 0.7 copy.82
  373.1 0.7 maximum_convert_fusion
  373.8 0.9 copy-done
  374.7 2.6 restore.1
  (86 shorter events, 1.8 us)
Async XLA Ops:
  7.2 165.3 %all-gather.3.cloned.1.call-start = ((), (), s32[]{:S(2)}) async-start(), calls=%async_computation.2 | async-start | bytes 7225344 | tf_op jit(solution)/shard_map/all_gather | solution.py:1308
  9.0 41.4 %copy-start.4 = (s32[4,384]{1,0:T(4,128)S(1)}, s32[4,384]{1,0:T(4,128)}, u32[]{:S(2)}) copy-start(s32[4,384]{1,0:T(4,128)} %param.35) | copy-start | bytes 18436
  9.0 41.4 %copy-start.10 = (s32[2,4]{1,0:T(2,128)S(1)}, s32[2,4]{1,0:T(2,128)}, u32[]{:S(2)}) copy-start(s32[2,4]{1,0:T(2,128)} %param.38) | copy-start | bytes 100
  9.0 41.4 %copy-start.7 = (s32[384]{0:T(512)S(1)}, s32[384]{0:T(512)}, u32[]{:S(2)}) copy-start(s32[384]{0:T(512)} %param.37) | copy-start | bytes 4612
  9.0 41.5 %copy-start.8 = (s32[384]{0:T(512)S(1)}, s32[384]{0:T(512)}, u32[]{:S(2)}) copy-start(s32[384]{0:T(512)} %param.36) | copy-start | bytes 4612
  9.0 43.8 %copy-start.6 = (s32[384]{0:T(512)S(1)}, s32[384]{0:T(512)}, u32[]{:S(2)}) copy-start(s32[384]{0:T(512)} %param.41) | copy-start | bytes 4612
  9.1 46.1 %copy-start.13 = (f32[64]{0:T(128)S(1)}, f32[64]{0:T(128)}, u32[]{:S(2)}) copy-start(f32[64]{0:T(128)} %param.25) | copy-start | bytes 772
  9.6 39.8 %collective-permute-start = (bf16[49,32,256]{2,1,0:T(8,128)(2,1)S(1)}, bf16[49,32,256]{2,1,0:T(8,128)(2,1)S(1)}, u32[]{:S(2)}, u32[]{:S(2)}) collective-permute-start(bf16[49,32,256]{2,1,0:T(8,128)(2,1)S(1)} %pad_maximum_fusion), channel_id=1, source_target_pairs={{0,0},{8,1},{16,2},{24,3},{4,4},{12,5},{20,6},{28,7},{1,8},{9,9},{... | collective-permute-start | bytes 2408456 | tf_op jit(solution)/shard_map/ppermute | solution.py:1307
  49.4 0.9 copy-start.1
  50.3 252.6 %reduce-scatter.2.cloned.1.call-start = ((), (), s32[]{:S(2)}) async-start(), calls=%async_computation.1 | async-start | bytes 8257536 | tf_op jit(solution)/shard_map/reduce_scatter | solution.py:1376
  55.9 13.0 %copy-start.11 = (f32[256]{0:T(256)S(1)}, f32[256]{0:T(256)}, u32[]{:S(2)}) copy-start(f32[256]{0:T(256)} %param.28) | copy-start | bytes 3076
  55.9 13.0 %copy-start.9 = (bf16[32,4]{0,1:T(4,128)(2,1)S(1)}, bf16[32,4]{0,1:T(4,128)(2,1)}, u32[]{:S(2)}) copy-start(bf16[32,4]{0,1:T(4,128)(2,1)} %param.33) | copy-start | bytes 772
  55.9 13.1 %copy-start.12 = (bf16[32]{0:T(256)(128)(2,1)S(1)}, bf16[32]{0:T(256)(128)(2,1)}, u32[]{:S(2)}) copy-start(bf16[32]{0:T(256)(128)(2,1)} %param.30) | copy-start | bytes 196
  55.9 13.2 %copy-start.5 = (bf16[32,81]{1,0:T(8,128)(2,1)S(1)}, bf16[32,81]{1,0:T(8,128)(2,1)}, u32[]{:S(2)}) copy-start(bf16[32,81]{1,0:T(8,128)(2,1)} %param.31) | copy-start | bytes 15556
  55.9 13.3 %copy-start.3 = (bf16[128,256]{1,0:T(8,128)(2,1)S(1)}, bf16[128,256]{1,0:T(8,128)(2,1)}, u32[]{:S(2)}) copy-start(bf16[128,256]{1,0:T(8,128)(2,1)} %param.29) | copy-start | bytes 196612
  67.7 54.9 %copy-start.14 = (f32[64]{0:T(128)S(1)}, f32[64]{0:T(128)}, u32[]{:S(2)}) copy-start(f32[64]{0:T(128)} %param.26) | copy-start | bytes 772
  124.5 45.7 %copy-start.15 = (f32[4]{0:T(128)S(1)}, f32[4]{0:T(128)}, u32[]{:S(2)}) copy-start(f32[4]{0:T(128)} %param.34) | copy-start | bytes 52
  124.5 45.7 %copy-start.16 = (f32[81]{0:T(128)S(1)}, f32[81]{0:T(128)}, u32[]{:S(2)}) copy-start(f32[81]{0:T(128)} %param.32) | copy-start | bytes 976
  219.1 23.1 %copy-start.2 = (f32[96,128]{1,0:T(8,128)S(1)}, f32[96,128]{1,0:T(8,128)}, u32[]{:S(2)}) copy-start(f32[96,128]{1,0:T(8,128)} %get-tuple-element.52) | copy-start | bytes 147460
  302.9 70.9 %collective-permute-start.1 = (bf16[1792,256]{1,0:T(8,128)(2,1)}, bf16[1792,256]{1,0:T(8,128)(2,1)S(1)}, u32[]{:S(2)}, u32[]{:S(2)}) collective-permute-start(bf16[1792,256]{1,0:T(8,128)(2,1)} %reduce-scatter.2.cloned.1.call-done), channel_id=1, source_target_pairs={{0,0},{1,8},{2,16},{3,24},{4,4},{5,12},{6,20},{7,28},{8,1},{9,9},{... | collective-permute-start | bytes 2752520 | tf_op jit(solution)/shard_map/ppermute | solution.py:1380
  373.8 0.9 copy-start
Sparse Core Ops, SparseCore 0:
  50.4 86.2 all-gather.2
  219.2 83.6 reduce-scatter.1

commit v3 on v2

--- a/solution.py
+++ b/solution.py
@@ -619,11 +619,23 @@
 KEPT = tuple(at for at in range(2 * len(USED)) if at % 2 == 0 or at // 2 < 21)
 LEADING = 42
 SPARES = tuple(at for at in range(2 * len(USED)) if at not in KEPT)
-SMALL = 6
+SMALL = 5
 
 
 def ring_of(rows):
     return list(range(0, rows, 2)) + list(range(rows - 1, 0, -2))
+
+
+def origin(kappa, rows, cols, position):
+    far = position >= rows // 2
+    plane = rows - 1 - position if far else position
+    code = lax.rem(plane + cols - kappa, cols)
+    return 2 * lax.rem(code, 2) + lax.div(code, 2), int(far)
+
+
+def position_of(kappa, rows, cols, block, half):
+    plane = lax.rem(2 * (block % 2) + block // 2 + kappa, cols)
+    return rows - 1 - plane if half else plane
 
 
 def greet(axis, count):
@@ -749,19 +761,34 @@
 
 def gather_small_kernel(rows, cols, mine, out, sends, recvs, col_sends, col_recvs, sem):
     row, col = lax.axis_index("roi"), lax.axis_index("col")
+    depth = rows // 2
+    plane, side = lax.div(row, 2), lax.rem(row, 2)
+    partner = row + 1 - 2 * side
     greet("roi", rows)
     greet("col", cols)
     own = pltpu.make_async_copy(mine, out.at[col, row], sem)
     own.start()
     own.wait()
     met(rows + cols - 2)
-    copies = [
-        remote(mine, out.at[col, row], sends, recvs, step - 1, "roi", lax.rem(row + step, rows))
-        for step in range(1, rows)
+    along = [
+        remote(mine, out.at[col, row], sends, recvs, step - 1, "roi",
+               lax.rem(plane + step, depth) * 2 + side)
+        for step in range(1, depth)
     ]
-    for copy in copies:
+    across = []
+    for step in range(depth):
+        source = lax.rem(plane + depth - step, depth) * 2 + side
+        block = out.at[col, source]
+        across.append(remote(block, block, sends, recvs, depth - 1 + step, "roi", partner))
+    for copy in along:
         copy.start()
-    for copy in copies:
+    across[0].start()
+    for step in range(1, depth):
+        along[step - 1].wait_recv()
+        across[step].start()
+    for copy in along:
+        copy.wait_send()
+    for copy in across:
         copy.wait()
     relay = Relay(lambda at: out.at[at], col_sends, col_recvs, 0)
     relay.start()
@@ -769,12 +796,14 @@
     relay.wait()
 
 
-def place_wide(pieces, wide, sems, rows, high):
+def place_wide(pieces, wide, sems, rows, cols):
     few, piece = pieces.shape[2], pieces.shape[3]
+    kappa = lax.axis_index("col")
     copies = []
-    for position, owner in enumerate(ring_of(rows)):
-        span = pl.ds((owner % high) * few, few)
-        lanes = pl.ds((owner // high) * piece, piece)
+    for position in range(rows):
+        block, half = origin(kappa, rows, cols, position)
+        span = pl.ds(half * few, few)
+        lanes = pl.ds(pl.multiple_of(block * piece, piece), piece)
         copies.append(
             pltpu.make_async_copy(
                 pieces.at[position, pl.ds(0, LEADING)],
@@ -806,7 +835,7 @@
     rois, hidden = g6_all.shape
     quarter, piece = rois // cols, hidden // cols
     greet("col", cols)
-    copies = place_wide(pieces, wide, sems, rows, rows // cols)
+    copies = place_wide(pieces, wide, sems, rows, cols)
     met(cols - 1)
     for copy in copies:
         copy.wait()
@@ -841,8 +870,13 @@
     pre_six = mine[me].astype(jnp.float32)
     for step in range(1, cols):
         pre_six = pre_six + taken[step - 1].astype(jnp.float32)
+    lines = [small[at, 0, 4, :16, LANES:].astype(jnp.float32) for at in range(cols)]
     bias = jnp.concatenate(
-        [jnp.sum(small[at, 0, 5, :3].astype(jnp.float32), axis=0, keepdims=True) for at in range(cols)],
+        [
+            (line[part : part + 1] + line[part + 2 : part + 3]) + line[part + 4 : part + 5]
+            for line in lines
+            for part in range(2)
+        ],
         axis=1,
     )
     pre_six = pre_six + bias
@@ -877,17 +911,18 @@
     huber = jnp.where(size < 1.0, 0.5 * misfit * misfit, size - 0.5)
     class_part = jnp.sum(weights[:, :1] * (log_total - picked), axis=0, keepdims=True)
     box_part = jnp.sum(jnp.where(is_class, 0.0, weights * huber), axis=0, keepdims=True)
+    grads = jnp.where(is_class, softmax - onehot, jnp.clip(misfit, -1.0, 1.0))
+    score_grads = (weights * grads).astype(jnp.bfloat16)
+    gs_out[...] = score_grads
     losses_out[...] = jnp.concatenate(
         [
             jnp.broadcast_to(class_part, (1, LANES)),
             box_part,
-            jnp.zeros((6, LANES), jnp.float32),
+            jnp.sum(score_grads.astype(jnp.float32), axis=0, keepdims=True),
+            jnp.zeros((5, LANES), jnp.float32),
         ],
         axis=0,
     )
-    grads = jnp.where(is_class, softmax - onehot, jnp.clip(misfit, -1.0, 1.0))
-    score_grads = (weights * grads).astype(jnp.bfloat16)
-    gs_out[...] = score_grads
     slope_seven = sigma_seven * (1.0 + pre_seven * (1.0 - sigma_seven))
     g7 = (contract_last(score_grads, head) * slope_seven).astype(jnp.bfloat16)
     g7_out[...] = g7
@@ -909,13 +944,13 @@
 
 def wide_grad_kernel(
     rows, cols, pooled, g6_all, g7, hid6, hid7, gs, losses,
-    terms, g7_all, gs_all, losses_all,
-    hid6_own, hid7_all, buffers, extras, head_term, out_sems, sends, recvs,
+    terms, g7_all, losses_all,
+    hid6_own, buffers, extras, head_mine, head_taken, out_sems, sends, recvs,
 ):
     me = lax.axis_index("col")
     rois, hidden = g6_all.shape
     quarter, piece = rois // cols, hidden // cols
-    high = rows // cols
+    owned, per = hidden // rows, hidden // (rows * cols)
     few = buffers.shape[2] // 4
     ring = ring_of(rows)
     greet("col", cols)
@@ -924,30 +959,29 @@
         return pl.ds(pl.multiple_of(at * quarter, quarter), quarter)
 
     g7_all[block(me), :] = g7[...]
-    hid7_all[block(me), :] = hid7[...]
-    gs_all[block(me), :] = gs[...]
     losses_all[me] = losses[...]
     own = pl.ds(pl.multiple_of(me * piece, piece), piece)
     hid6_own[block(me), :] = hid6[:, own]
+    head_term = contract_first(hid7[...], gs[...]).astype(jnp.bfloat16)
+    for row in range(rows):
+        for at in range(cols):
+            first = row * owned + at * per
+            head_mine[at, row] = head_term[first : first + per]
     met(cols - 1)
-    relays = [
-        Relay(lambda at: g7_all.at[block(at)], sends, recvs, 0),
-        Relay(lambda at: hid7_all.at[block(at)], sends, recvs, 3),
-    ]
-    for relay in relays:
-        relay.start()
+    relay = Relay(lambda at: g7_all.at[block(at)], sends, recvs, 0)
+    relay.start()
     copies = []
     for step in range(1, cols):
         peer = lax.rem(me + step, cols)
         theirs = pl.ds(pl.multiple_of(peer * piece, piece), piece)
         copies.append(
-            remote(hid6.at[:, theirs], hid6_own.at[block(me)], sends, recvs, 5 + step, "col", peer)
+            remote(hid6.at[:, theirs], hid6_own.at[block(me)], sends, recvs, 2 + step, "col", peer)
         )
         copies.append(
-            remote(gs, gs_all.at[block(me)], sends, recvs, 8 + step, "col", peer)
+            remote(head_mine.at[peer], head_taken.at[step - 1], sends, recvs, 5 + step, "col", peer)
         )
         copies.append(
-            remote(losses, losses_all.at[me], sends, recvs, 11 + step, "col", peer)
+            remote(losses, losses_all.at[me], sends, recvs, 8 + step, "col", peer)
         )
     for copy in copies:
         copy.start()
@@ -967,33 +1001,35 @@
 
             lanes = pl.ds(pl.multiple_of(at * 2 * LANES, 2 * LANES), 2 * LANES)
             result = contract_first(pooled[:, lanes], g6_all[...]).astype(jnp.bfloat16)
-            for position, owner in enumerate(ring):
-                columns = slice((owner // high) * piece, (owner // high + 1) * piece)
-                for part in range(4):
-                    first = (part * high + owner % high) * few
-                    buffers[slot, position, part * few : (part + 1) * few, :] = result[
-                        first : first + few, columns
-                    ]
+            for column in range(cols):
+                columns = slice(column * piece, (column + 1) * piece)
+                for half in range(2):
+                    position = position_of(me, rows, cols, column, half)
+                    for part in range(4):
+                        first = (part * 2 + half) * few
+                        buffers[slot, position, part * few : (part + 1) * few, :] = result[
+                            first : first + few, columns
+                        ]
             leaving(slot, at).start()
         return carry
 
     pairs = len(USED) // 4
-    lax.fori_loop(0, pairs, step, 0)
-    for relay in relays:
-        relay.forward()
-    for relay in relays:
-        relay.wait()
+    lax.fori_loop(0, pairs - 3, step, 0)
+    relay.forward()
+    lax.fori_loop(pairs - 3, pairs, step, 0)
+    relay.wait()
     for copy in copies:
         copy.wait()
     deep_term = contract_first(g7_all[...], hid6_own[...]).astype(jnp.bfloat16)
-    head_term[...] = contract_first(hid7_all[...], gs_all[...])
-    owned, per = hidden // rows, hidden // (rows * cols)
+    nothing = jnp.zeros((per, piece - LANES), jnp.bfloat16)
     for position, owner in enumerate(ring):
         extras[position, :owned, :] = deep_term[owner * owned : (owner + 1) * owned]
-        mine = pl.ds(pl.multiple_of(owner * owned + me * per, per), per)
+        total = head_mine[me, owner].astype(jnp.float32)
+        for at in range(cols - 1):
+            total = total + head_taken[at, owner].astype(jnp.float32)
         extras[position, owned : owned + per, :] = jnp.concatenate(
-            [head_term[mine, :], jnp.zeros((per, piece - LANES), jnp.float32)], axis=1
-        ).astype(jnp.bfloat16)
+            [total.astype(jnp.bfloat16), nothing], axis=1
+        )
     for slot in range(2):
         leaving(slot, 2 * pairs - 2 + slot).wait()
     copies = [
@@ -1011,7 +1047,7 @@
 
 
 def pool_grad_kernel(
-    rows, cols, pixels, g6_all, g7_all, gs_all, losses_all, centred, weight, stats, pieces,
+    rows, cols, pixels, g6_all, g7_all, losses_all, centred, weight, stats, pieces,
     grads, totals, base, slope, wide, slots, sems, sends, recvs,
 ):
     row, col = lax.axis_index("roi"), lax.axis_index("col")
@@ -1019,7 +1055,7 @@
     channels = base.shape[0]
     piece = hidden // cols
     greet("roi", rows)
-    copies = place_wide(pieces, wide, sems, rows, rows // cols)
+    copies = place_wide(pieces, wide, sems, rows, cols)
     own = pl.ds(pl.multiple_of(col * piece, piece), piece)
 
     def columns(values):
@@ -1031,7 +1067,6 @@
         ]
 
     bias_rows = as_rows(columns(g6_all[:, own])) + as_rows(columns(g7_all[...]))
-    bias_rows += [columns(gs_all[...])]
     losses = losses_all[0]
     for at in range(1, cols):
         losses = losses + losses_all[at]
@@ -1061,8 +1096,8 @@
         low, gain + pltpu.roll(gain, channels, 1), shift + pltpu.roll(shift, channels, 1)
     )
     both = jnp.sum(both, axis=0, keepdims=True)
-    lines = [both] + bias_rows + [losses[:2]]
-    count = 1 + len(bias_rows) + 2
+    lines = [both] + bias_rows + [losses[2:3], losses[:2]]
+    count = 1 + len(bias_rows) + 3
     lines.append(jnp.zeros((16 - count, LANES), jnp.float32))
     slots[row] = jnp.concatenate(lines, axis=0)
     met(rows - 1)
@@ -1179,27 +1214,26 @@
         out_shape=(
             shaped((rows, 2 * len(USED) * few, piece), bf16),
             shaped((rois, hidden), bf16),
-            shaped((rois, LANES), bf16),
             shaped((cols, 8, LANES), f32),
         ),
         in_specs=[VMEM] * 7,
-        out_specs=(ANY, VMEM, VMEM, VMEM),
+        out_specs=(ANY, VMEM, VMEM),
         scratch_shapes=[
             pltpu.VMEM((rois, piece), bf16),
-            pltpu.VMEM((rois, hidden), bf16),
             pltpu.VMEM((2, rows, 4 * few, piece), bf16),
             pltpu.VMEM((rows, owned + per, piece), bf16),
-            pltpu.VMEM((hidden, LANES), f32),
+            pltpu.VMEM((cols, rows, per, LANES), bf16),
+            pltpu.VMEM((cols - 1, rows, per, LANES), bf16),
             pltpu.SemaphoreType.DMA((2 + len(SPARES),)),
-            pltpu.SemaphoreType.DMA((15,)),
-            pltpu.SemaphoreType.DMA((15,)),
+            pltpu.SemaphoreType.DMA((12,)),
+            pltpu.SemaphoreType.DMA((12,)),
         ],
         compiler_params=comm_params(3),
         name="wide_grads",
     )(pooled, g6_all, g7, hid6, hid7, gs, losses)
 
 
-def pool_grads(g6_all, g7_all, gs_all, losses_all, centred, weight, stats, pieces, rows, cols, pixels):
+def pool_grads(g6_all, g7_all, losses_all, centred, weight, stats, pieces, rows, cols, pixels):
     rois, hidden = g6_all.shape
     channels = LANES // 2
     bf16, f32 = jnp.bfloat16, jnp.float32
@@ -1211,7 +1245,7 @@
             shaped((channels, LANES), f32),
             shaped((channels, LANES), f32),
         ),
-        in_specs=[VMEM] * 7 + [ANY],
+        in_specs=[VMEM] * 6 + [ANY],
         out_specs=(VMEM,) * 4,
         scratch_shapes=[
             pltpu.VMEM((2 * len(USED), channels, hidden), bf16),
@@ -1222,7 +1256,7 @@
         ],
         compiler_params=comm_params(4),
         name="pool_grads",
-    )(g6_all, g7_all, gs_all, losses_all, centred, weight, stats, pieces)
+    )(g6_all, g7_all, losses_all, centred, weight, stats, pieces)
 
 
 def restore(term, few):
@@ -1299,13 +1333,14 @@
     block = jnp.pad(block, ((0, 0), (0, 0), (0, 1), (0, 0))).reshape(few, 7, 2, 4, piece)
     block = block.transpose(3, 1, 2, 0, 4).reshape(2 * len(USED), few, piece)
     block = jnp.concatenate([block[:LEADING], block[LEADING::2]])
-    pairs = [
-        ((kappa * high + rho % high) * cols + rho // high, rho * cols + kappa)
-        for rho in range(rows)
-        for kappa in range(cols)
-    ]
+    pairs = []
+    for kappa in range(cols):
+        for block_at in range(cols):
+            for half in range(high):
+                plane = (2 * (block_at % 2) + block_at // 2 + kappa) % cols
+                source = (kappa * high + half) * cols + block_at
+                pairs.append((source, (plane * high + half) * cols + kappa))
     block = lax.ppermute(block, ("roi", "col"), pairs)
-    pieces = lax.all_gather(block, "roi", axis=0, axis_index_groups=[ring])
 
     head = jnp.concatenate([cls_weight, box_weight, fc7_bias[:, None]], axis=1)
     head = jnp.pad(head, ((0, 0), (0, piece - head.shape[1])))
@@ -1313,8 +1348,10 @@
     rest = fc6_bias - bias_high.astype(f32)
     bias_mid = rest.astype(bf16)
     bias_low = (rest - bias_mid.astype(f32)).astype(bf16)
-    bias = jnp.pad(jnp.stack([bias_high, bias_mid, bias_low]), ((0, few - 3), (0, 0)))
-    small = jnp.concatenate([fc7_weight, head, bias], axis=0).reshape(SMALL, few, piece)
+    bias = jnp.concatenate([item.reshape(2, LANES) for item in (bias_high, bias_mid, bias_low)])
+    bias = jnp.pad(bias, ((0, per - bias.shape[0]), (0, 0)))
+    head = jnp.concatenate([head[:, :LANES], bias], axis=1)
+    small = jnp.concatenate([fc7_weight, head], axis=0).reshape(SMALL, few, piece)
 
     def twice(vector):
         return jnp.concatenate([vector, vector])[None]
@@ -1336,10 +1373,12 @@
         (roi_boxes[3] + shift_y).astype(f32),
         roi_level,
     )
+    block = lax.optimization_barrier((block, stats, floats, order))[0]
+    pieces = lax.all_gather(block, "roi", axis=0, axis_index_groups=[ring])
     pooled, centred, weight = pool_maps(
         floats, ints, order, stats[:1], stats[1:2], twice(norm_bias), planes, rois
     )
-    small = gather_small(small, rows, cols)
+    small = gather_small(lax.optimization_barrier((small, pooled))[0], rows, cols)
 
     quarter = rois // cols
     first_row = lax.axis_index("col") * quarter
@@ -1369,7 +1408,7 @@
     )
     decoded = decode(mine_boxes, scores[:, classes : classes + boxes])
 
-    terms, g7_all, gs_all, losses_all = wide_grads(
+    terms, g7_all, losses_all = wide_grads(
         pooled, g6_all, g7, hid6, hid7, gs, losses, rows, cols
     )
     wide_rows = terms.shape[1]
@@ -1377,6 +1416,12 @@
         terms.reshape(rows * wide_rows, piece), "roi", scatter_dimension=0, tiled=True,
         axis_index_groups=[ring],
     )
+    grads, totals, base, slope = pool_grads(
+        g6_all, g7_all, losses_all, centred, weight, stats, pieces, rows, cols,
+        float(pixels),
+    )
+    input_grads = unpool_maps(floats, ints, order, base, slope, grads, planes, rois)
+    term = lax.optimization_barrier((term, input_grads[3]))[0]
     back = lax.ppermute(term, ("roi", "col"), [(there, here) for here, there in pairs])
     fc6_weight_grad = restore(back, few)
     extra = [
@@ -1387,11 +1432,6 @@
     cls_weight_grad = extra[-1][:, :classes]
     box_weight_grad = extra[-1][:, classes : classes + boxes]
 
-    grads, totals, base, slope = pool_grads(
-        g6_all, g7_all, gs_all, losses_all, centred, weight, stats, pieces, rows, cols,
-        float(pixels),
-    )
-    input_grads = unpool_maps(floats, ints, order, base, slope, grads, planes, rois)
     fc6_bias_grad = totals[1 : 1 + piece // LANES].reshape(-1)
     seven = totals[1 + piece // LANES :][: cols * piece // LANES].reshape(-1)
     place = (lax.axis_index("roi") * cols + lax.axis_index("col")) * per

time: 389 us -> 317 us (0.81)
  waiting for transfers between devices: 94.3 us -> 35.1 us
  Pallas kernels: 236 us -> 230 us
  local copies, waits for them, and re-layouts: 21.2 us -> 17.1 us
    reduce_scatter x1, waiting for transfers between devices: 57.3 us -> 1.03 us  [local_near(): lax.psum_scatter(terms.reshape(rows * wide_rows, piece), 'roi', scatter_d...]
    ppermute x1, waiting for transfers between devices: 37 us -> 0.01 us  [local_near(): block = lax.ppermute(block, ('roi', 'col'), pairs)]
    ppermute x1, waiting for transfers between devices: 0.01 us -> 34 us  [local_near(): lax.ppermute(term, ('roi', 'col'), [(there, here) for here, there in pairs])]
    pallas_call x1, Pallas kernels: 48.4 us -> 38.9 us  [gather_small(): pl.pallas_call(functools.partial(gather_small_kernel, rows, cols), out_sh...]
    pallas_call x1, Pallas kernels: 11.8 us -> 18 us  [statistics(): pl.pallas_call(functools.partial(stats_kernel, rows, pixels), out_shape=s...]
  transfers between devices with their start and end apart: 4 -> 4, of which waited for: 2 -> 2; matrix products, arithmetic and copies ran while one was open for 7% -> 7% of each run, Pallas kernels for 48% -> 58%
where the time goes in v3:
time: 317 us; the launch traced here: 316 us
  Pallas kernels  230 us (73%)
  waiting for transfers between devices  35.1 us (11%)
  between operations  18.8 us (6%)
  local copies, waits for them, and re-layouts  17.1 us (5%)
  other arithmetic  9.83 us (3%)
  starting transfers between devices  5.48 us (2%)
    pallas_call x1, Pallas kernels, unpool_maps(): pl.pallas_call(functools.partial(unpool_kernel, rois), out_shape=tuple((j...  58.3 us
    pallas_call x1, Pallas kernels, pool_maps(): pl.pallas_call(functools.partial(pool_kernel, rois), out_shape=(flat, fla...  45.9 us
    pallas_call x1, Pallas kernels, gather_small(): pl.pallas_call(functools.partial(gather_small_kernel, rows, cols), out_sh...  38.9 us
    ppermute x1, waiting for transfers between devices, local_near(): lax.ppermute(term, ('roi', 'col'), [(there, here) for here, there in pairs])  34 us
    pallas_call x1, Pallas kernels, run_head(): pl.pallas_call(functools.partial(head_kernel, rows, cols, classes, boxes)...  27.8 us
    pallas_call x1, Pallas kernels, pool_grads(): pl.pallas_call(functools.partial(pool_grad_kernel, rows, cols, pixels), o...  22 us
    pallas_call x1, Pallas kernels, statistics(): pl.pallas_call(functools.partial(stats_kernel, rows, pixels), out_shape=s...  18 us
    pallas_call x1, Pallas kernels, wide_grads(): pl.pallas_call(functools.partial(wide_grad_kernel, rows, cols), out_shape...  16.2 us
  transfers between devices with their start and end apart: 4, of which 2 were waited for; matrix products, arithmetic and copies ran while one was open for 7% of the time, Pallas kernels for 58%

profile of v3, /device:TPU:12, one launch (start us, length us, event | category | flops | bytes accessed | tf_op | source)
XLA Modules:
  0.0 316.1 jit_solution(14001182140689440544)
XLA Ops:
  7.2 1.4 reshape.459
  8.6 0.2 pad.26
  8.8 0.2 reshape.460
  9.1 0.2 copy.81
  9.3 0.2 copy.80
  9.6 2.9 collective-permute-start
  12.5 0.6 convert_reduce_fusion.1
  13.1 0.7 pad.58.clone
  14.0 0.7 convert_reduce_fusion.2
  14.8 0.7 reshape.453.floats
  15.6 0.7 maximum_maximum_fusion.1.facts
  16.3 18.0 %statistics.1.stats = f32[8,128]{1,0:T(8,128)} custom-call(f32[8,128]{1,0:T(8,128)} %maximum_maximum_fusion.1.facts, bf16[1,64,65536]{2,1,0:T(8,128)(2,1)} %p2.5, bf16[1,64,16384]{2,1,0:T(8,128)(2,1)} %p3.5, bf16[1,64,4096]{2,1,0:T(8,128)(2,1)} %p4.5, bf16[1,64,1024]{2,1,0:T(8,128)(2,1)} %p5.5), custom_call_target="tpu_custom_call" | custom-call | tf_op jit(solution)/shard_map/statistics/pallas_call | solution.py:1140
  34.3 0.2 convert_reduce_fusion
  34.7 3.3 %concatenate.44.order = s32[404]{0:T(512)} concatenate(s32[384]{0:T(512)S(1)} %select_reduce_fusion, s32[16]{0:T(128)S(1)} %broadcast.311, s32[1]{0:T(128)} %bitcast.2, s32[1]{0:T(128)} %bitcast.3, s32[1]{0:T(128)} %bitcast.4, s32[1]{0:T(128)} %bitcast.5), dimensions={0} | concatenate | bytes 3232 | tf_op jit(solution)/shard_map/concatenate | solution.py:104
  38.0 0.9 copy-done.1
  39.0 1.2 slice.153
  40.4 0.7 reshape.454.ints
  41.1 0.8 dynamic-slice_convert_fusion
  42.0 0.6 maximum_bitcast_fusion.1.shift
  42.6 1.3 fusion.48
  43.9 45.9 %pool.1 = (bf16[384,3584]{1,0:T(8,128)(2,1)}, bf16[384,3584]{1,0:T(8,128)(2,1)}, bf16[384,3584]{1,0:T(8,128)(2,1)}) custom-call(f32[2744]{0:T(1024)} %reshape.453.floats, s32[2352]{0:T(1024)} %reshape.454.ints, s32[404]{0:T(512)} %concatenate.44.order, f32[1,128]{1,0:T(1,128)} %get-tuple-element.182.mean, f32[1,128]{1,0:T(1,128)} %get-tuple-element.181.scale, ...), custom_call_target="tpu_custom_call" | custom-call | tf_op jit(solution)/shard_map/pool/pallas_call | solution.py:352
  90.0 0.6 maximum_maximum_fusion
  90.6 38.9 %gather_small.1.small = bf16[4,8,5,32,256]{4,3,2,1,0:T(8,128)(2,1)} custom-call(bf16[5,32,256]{2,1,0:T(8,128)(2,1)} %bitcast.142), custom_call_target="tpu_custom_call" | custom-call | tf_op jit(solution)/shard_map/gather_small/pallas_call | solution.py:1158
  130.2 0.6 fusion.37.score_bias
  130.8 0.8 compare_select_fusion
  131.9 0.7 pad_maximum_fusion.1.facts
  132.5 27.8 %head.1 = (bf16[384,1024]{1,0:T(8,128)(2,1)}, bf16[96,1024]{1,0:T(8,128)(2,1)}, bf16[96,1024]{1,0:T(8,128)(2,1)}, bf16[96,1024]{1,0:T(8,128)(2,1)}, bf16[96,128]...) custom-call(bf16[384,3584]{1,0:T(8,128)(2,1)} %get-tuple-element.41.pooled, ...), custom_call_target="tpu_custom_call" | custom-call | tf_op jit(solution)/shard_map/head/pallas_call | solution.py:1179
  160.4 16.2 %wide_grads.1 = (bf16[8,1792,256]{2,1,0:T(8,128)(2,1)}, bf16[384,1024]{1,0:T(8,128)(2,1)}, f32[4,8,128]{2,1,0:T(8,128)}) custom-call(bf16[384,3584]{1,0:T(8,128)(2,1)} %get-tuple-element.41.pooled, bf16[384,1024]{1,0:T(8,128)(2,1)} %get-tuple-element.44.g6_all, bf16[96,1024]{1,0:T(8,128)(2,1)} %get-tuple-element.45.g7, ...), custom_call_target="tpu_custom_call" | custom-call | tf_op jit(solution)/shard_map/wide_grads/pallas_call | solution.py:1212
  176.7 22.0 %pool_grads.1 = (bf16[384,3584]{1,0:T(8,128)(2,1)}, f32[16,128]{1,0:T(8,128)}, f32[64,128]{1,0:T(8,128)}, f32[64,128]{1,0:T(8,128)}) custom-call(bf16[384,1024]{1,0:T(8,128)(2,1)} %get-tuple-element.44.g6_all, bf16[384,1024]{1,0:T(8,128)(2,1)} %get-tuple-element.50.g7_all, f32[4,8,128]{2,1,0:T(8,128)} %get-tuple-element.51.losses_all, ...), custom_call_target="tpu_custom_call" | custom-call | tf_op jit(solution)/shard_map/pool_grads/pallas_call | solution.py:1240
  198.7 58.3 %unpool.1 = (f32[1,64,65536]{2,1,0:T(8,128)}, f32[1,64,16384]{2,1,0:T(8,128)}, f32[1,64,4096]{2,1,0:T(8,128)}, f32[1,64,1024]{2,1,0:T(8,128)}) custom-call(f32[2744]{0:T(1024)} %reshape.453.floats, s32[2352]{0:T(1024)} %reshape.454.ints, s32[404]{0:T(512)} %concatenate.44.order, f32[64,128]{1,0:T(8,128)} %get-tuple-element.56.base, ...), custom_call_target="tpu_custom_call" | custom-call | tf_op jit(solution)/shard_map/unpool/pallas_call | solution.py:369
  257.0 0.2 exponential_reduce_fusion.1
  257.2 0.5 slice_bitcast_fusion.3
  257.7 0.6 slice_bitcast_fusion.2
  258.3 1.0 reduce-scatter.2.cloned.1.call-done
  259.4 2.5 collective-permute-start.1
  261.9 0.6 slice_reduce_fusion.4
  262.5 0.5 slice.158
  264.3 0.6 dynamic_slice.19
  264.9 0.6 maximum_multiply_fusion
  265.5 0.6 slice_bitcast_fusion.1
  266.1 0.6 slice_bitcast_fusion.4
  266.7 0.8 slice_convert_fusion
  267.5 0.6 slice.178
  268.1 0.7 copy.82
  268.8 0.7 maximum_convert_fusion
  269.4 34.0 %collective-permute-done.1.term = bf16[1792,256]{1,0:T(8,128)(2,1)S(1)} collective-permute-done((bf16[1792,256]{1,0:T(8,128)(2,1)}, bf16[1792,256]{1,0:T(8,128)(2,1)S(1)}, u32[]{:S(2)}, u32[]{:S(2)}) %collective-permute-start.1) | collective-permute-done | bytes 917536 | tf_op jit(solution)/shard_map/ppermute | solution.py:1425
  303.5 0.9 copy-done
  304.4 2.6 restore.1
  (85 shorter events, 1.6 us)
Async XLA Ops:
  7.2 125.3 %all-gather.3.cloned.1.call-start = ((), (), s32[]{:S(2)}) async-start(), calls=%async_computation.2 | async-start | bytes 7225344 | tf_op jit(solution)/shard_map/all_gather | solution.py:1377
  9.0 3.4 %copy-start.7 = (s32[384]{0:T(512)S(1)}, s32[384]{0:T(512)}, u32[]{:S(2)}) copy-start(s32[384]{0:T(512)} %param.41) | copy-start | bytes 4612
  9.0 4.8 %copy-start.11 = (s32[2,4]{1,0:T(2,128)S(1)}, s32[2,4]{1,0:T(2,128)}, u32[]{:S(2)}) copy-start(s32[2,4]{1,0:T(2,128)} %param.38) | copy-start | bytes 100
  9.0 4.8 %copy-start.4 = (s32[4,384]{1,0:T(4,128)S(1)}, s32[4,384]{1,0:T(4,128)}, u32[]{:S(2)}) copy-start(s32[4,384]{1,0:T(4,128)} %param.35) | copy-start | bytes 18436
  9.0 4.9 %copy-start.8 = (s32[384]{0:T(512)S(1)}, s32[384]{0:T(512)}, u32[]{:S(2)}) copy-start(s32[384]{0:T(512)} %param.37) | copy-start | bytes 4612
  9.0 5.0 %copy-start.9 = (s32[384]{0:T(512)S(1)}, s32[384]{0:T(512)}, u32[]{:S(2)}) copy-start(s32[384]{0:T(512)} %param.36) | copy-start | bytes 4612
  9.1 6.5 %copy-start.14 = (f32[64]{0:T(128)S(1)}, f32[64]{0:T(128)}, u32[]{:S(2)}) copy-start(f32[64]{0:T(128)} %param.25) | copy-start | bytes 772
  9.6 28.4 %collective-permute-start = (bf16[49,32,256]{2,1,0:T(8,128)(2,1)S(1)}, bf16[49,32,256]{2,1,0:T(8,128)(2,1)S(1)}, u32[]{:S(2)}, u32[]{:S(2)}) collective-permute-start(bf16[49,32,256]{2,1,0:T(8,128)(2,1)S(1)} %pad_maximum_fusion), channel_id=1, source_target_pairs={{0,0},{4,4},{1,16},{5,20},{2,8},{6,12},{3,24},{7,28},{8,9},{12,13}... | collective-permute-start | bytes 2408456 | tf_op jit(solution)/shard_map/ppermute | solution.py:1343
  16.3 23.9 %copy-start.13 = (bf16[32]{0:T(256)(128)(2,1)S(1)}, bf16[32]{0:T(256)(128)(2,1)}, u32[]{:S(2)}) copy-start(bf16[32]{0:T(256)(128)(2,1)} %param.30) | copy-start | bytes 196
  16.3 24.0 %copy-start.10 = (bf16[32,4]{0,1:T(4,128)(2,1)S(1)}, bf16[32,4]{0,1:T(4,128)(2,1)}, u32[]{:S(2)}) copy-start(bf16[32,4]{0,1:T(4,128)(2,1)} %param.33) | copy-start | bytes 772
  16.3 25.8 %copy-start.15 = (f32[64]{0:T(128)S(1)}, f32[64]{0:T(128)}, u32[]{:S(2)}) copy-start(f32[64]{0:T(128)} %param.26) | copy-start | bytes 772
  38.0 0.9 copy-start.1
  38.9 220.5 %reduce-scatter.2.cloned.1.call-start = ((), (), s32[]{:S(2)}) async-start(), calls=%async_computation.1 | async-start | bytes 8257536 | tf_op jit(solution)/shard_map/reduce_scatter | solution.py:1415
  43.9 45.9 %copy-start.12 = (f32[256]{0:T(256)S(1)}, f32[256]{0:T(256)}, u32[]{:S(2)}) copy-start(f32[256]{0:T(256)} %param.28) | copy-start | bytes 3076
  43.9 46.0 %copy-start.5 = (bf16[32,81]{1,0:T(8,128)(2,1)S(1)}, bf16[32,81]{1,0:T(8,128)(2,1)}, u32[]{:S(2)}) copy-start(bf16[32,81]{1,0:T(8,128)(2,1)} %param.31) | copy-start | bytes 15556
  43.9 46.1 %copy-start.3 = (bf16[128,256]{1,0:T(8,128)(2,1)S(1)}, bf16[128,256]{1,0:T(8,128)(2,1)}, u32[]{:S(2)}) copy-start(bf16[128,256]{1,0:T(8,128)(2,1)} %param.29) | copy-start | bytes 196612
  89.8 40.4 %copy-start.16 = (f32[4]{0:T(128)S(1)}, f32[4]{0:T(128)}, u32[]{:S(2)}) copy-start(f32[4]{0:T(128)} %param.34) | copy-start | bytes 52
  89.8 40.4 %copy-start.17 = (f32[81]{0:T(128)S(1)}, f32[81]{0:T(128)}, u32[]{:S(2)}) copy-start(f32[81]{0:T(128)} %param.32) | copy-start | bytes 976
  198.6 58.3 %copy-start.2 = (f32[96,128]{1,0:T(8,128)S(1)}, f32[96,128]{1,0:T(8,128)}, u32[]{:S(2)}) copy-start(f32[96,128]{1,0:T(8,128)} %get-tuple-element.55) | copy-start | bytes 147460
  198.6 58.6 %copy-start.6 = (f32[16,128]{1,0:T(8,128)S(1)}, f32[16,128]{1,0:T(8,128)}, u32[]{:S(2)}) copy-start(f32[16,128]{1,0:T(8,128)} %get-tuple-element.54) | copy-start | bytes 24580
  259.4 44.1 %collective-permute-start.1 = (bf16[1792,256]{1,0:T(8,128)(2,1)}, bf16[1792,256]{1,0:T(8,128)(2,1)S(1)}, u32[]{:S(2)}, u32[]{:S(2)}) collective-permute-start(bf16[1792,256]{1,0:T(8,128)(2,1)} %reduce-scatter.2.cloned.1.call-done), channel_id=1, source_target_pairs={{0,0},{4,4},{16,1},{20,5},{8,2},{12,6},{24,3},{28,7},{9,8},{13,12}... | collective-permute-start | bytes 2752520 | tf_op jit(solution)/shard_map/ppermute | solution.py:1425
  303.5 0.9 copy-start
Sparse Core Ops, SparseCore 0:
  39.0 76.2 all-gather.2
  176.8 82.5 reduce-scatter.1

commit v4 on v3

--- a/solution.py
+++ b/solution.py
@@ -12,6 +12,7 @@
 EPSILON = 1e-05
 LANES = 128
 SPAN = 10
+NARROW = 8
 GROUP = 16
 MORE = 8
 SPARE = 8
@@ -66,17 +67,20 @@
     y_low, y_high = window(y_anchor, y_extent)
     x_low, x_high = window(x_anchor, x_extent)
     group_low, group_high = y_low >> rows_log, y_high >> rows_log
-    chunks = (group_high - group_low + SPAN) // SPAN
-    group = jnp.maximum(jnp.minimum(group_low, (side >> rows_log) - chunks * SPAN), 0)
     tile_x = x_low // LANES
     tiles_x = x_high // LANES - tile_x + 1
+    narrow = (group_high - group_low < NARROW) & (tiles_x == 1)
+    chunks = jnp.where(narrow, 1, (group_high - group_low + SPAN) // SPAN)
+    taken = jnp.where(narrow, NARROW, chunks * SPAN)
+    group = jnp.maximum(jnp.minimum(group_low, (side >> rows_log) - taken), 0)
     first_tile = by_level(list(FIRST)) + group * across + tile_x
     mask = jnp.minimum(side, LANES) - 1
     shift = 7 - rows_log
     rows_per = (1 << rows_log).astype(jnp.float32)
     nothing = jnp.zeros((SPARE,), jnp.int32)
     parts = chunks * tiles_x
-    key = 2 * (level > 0).astype(jnp.int32) + (parts > 1).astype(jnp.int32)
+    kind = jnp.where(narrow, 0, jnp.where(parts > 1, 2, 1))
+    key = jnp.where(level > 0, 3 + kind, 2 - kind)
     rois = level.shape[0]
     at = jnp.arange(rois, dtype=jnp.int32)
     before = (key[None, :] < key[:, None]) | (
@@ -85,7 +89,7 @@
     rank = jnp.sum(before.astype(jnp.int32), axis=1)
     order = jnp.sum(jnp.where(rank[None, :] == at[:, None], at[None, :], 0), axis=1)
     order = jnp.concatenate([order, jnp.full((GROUP,), rois, jnp.int32)])
-    ends = jnp.stack([jnp.sum((key <= last).astype(jnp.int32)) for last in range(4)])
+    ends = jnp.stack([jnp.sum((key <= last).astype(jnp.int32)) for last in range(6)])
     floats = jnp.stack(
         [
             x_anchor,
@@ -104,7 +108,7 @@
     return floats.reshape(-1), ints.reshape(-1), jnp.concatenate([order, ends])
 
 
-def window_weights(floats, ints, rois, region, chunk, tile_x):
+def window_weights(floats, ints, rois, region, chunk, tile_x, span=SPAN):
     rois = rois + SPARE
     x_anchor, x_extent, y_anchor, y_extent, x_origin, y_origin, rows_per = (
         floats[at * rois + region] for at in range(F32_FIELDS)
@@ -138,7 +142,7 @@
         for at in range(4)
     ]
     blocks = []
-    for at in range(SPAN):
+    for at in range(span):
         offset = rows_per * float(at)
         down = tent(near - offset) + tent(far - offset)
         both = jnp.concatenate([down, down], axis=0).astype(jnp.bfloat16)
@@ -154,7 +158,7 @@
     def step(at, carry):
         first = start + at * size
         inside = [first + index < stop for index in range(size)]
-        spare = order.shape[0] - 5
+        spare = order.shape[0] - 7
         places = [
             jnp.where(good, first + index, spare) for index, good in enumerate(inside)
         ]
@@ -191,14 +195,14 @@
 
 def ends_of(order):
     size = order.shape[0]
-    return [order[size - 4 + at] for at in range(4)]
+    return [order[size - 6 + at] for at in range(6)]
 
 
 def pool_kernel(
-    rois, floats, ints, order, mean, scale, shift, p2, p3, p4, p5,
+    rois, floats, ints, order, stats, shift, p2, p3, p4, p5,
     pooled_out, centred_out, weight_out, maps, values, sems,
 ):
-    channels = mean.shape[1] // 2
+    channels = stats.shape[1] // 2
     stride = rois + SPARE
     copies = []
     for level, plane in enumerate((p2, p3, p4, p5)):
@@ -227,15 +231,21 @@
     for copy in copies:
         copy.wait()
 
-    def item(region, chunk, tile_x):
-        kernel_w, first_tile, across = window_weights(floats, ints, rois, region, chunk, tile_x)
+    def item(region, chunk, tile_x, span=SPAN):
+        kernel_w, first_tile, across = window_weights(
+            floats, ints, rois, region, chunk, tile_x, span
+        )
         cells = jnp.concatenate(
-            [maps[:, tile_lanes(first_tile, across, at)] for at in range(SPAN)], axis=1
+            [maps[:, tile_lanes(first_tile, across, at)] for at in range(span)], axis=1
         )
         return contract_last(kernel_w, cells)
 
     def place(region):
         return pl.ds(region, 2 * SLOTS, stride=stride)
+
+    def narrow(regions):
+        for region in regions:
+            values[place(region), : channels + 16] = item(region, None, None, NARROW)
 
     def first(regions):
         for region in regions:
@@ -244,10 +254,12 @@
     def further(region, chunk, tile_x):
         values[place(region), : channels + 16] = values[place(region), : channels + 16] + item(region, chunk, tile_x)
 
-    low_end, low_multi, rest_end, all_end = ends_of(order)
-    for_groups(order, 0, all_end, GROUP, first)
-    for_parts(ints, order, rois, low_end, low_multi, MORE, further)
-    for_parts(ints, order, rois, rest_end, all_end, MORE, further)
+    ends = ends_of(order)
+    for_groups(order, 0, ends[1], MORE, first)
+    for_groups(order, ends[1], ends[3], GROUP, narrow)
+    for_groups(order, ends[3], ends[5], MORE, first)
+    for_parts(ints, order, rois, 0, ends[0], MORE, further)
+    for_parts(ints, order, rois, ends[4], ends[5], MORE, further)
     low_lane = lax.broadcasted_iota(jnp.int32, (rois, LANES), 1) < channels
     for at, slot in enumerate(USED):
         lanes = pl.ds(at * LANES, LANES)
@@ -255,15 +267,15 @@
         two = values[pl.ds((slot + SLOTS) * stride, rois), :]
         value = jnp.where(low_lane, one, pltpu.roll(two, channels, 1))
         total = jnp.where(low_lane, one[:, channels : channels + 1], two[:, channels : channels + 1])
-        centred = value - mean[...] * total
+        centred = value - stats[:1] * total
         centred_out[:, lanes] = centred.astype(jnp.bfloat16)
         weight_out[:, lanes] = total.astype(jnp.bfloat16)
-        pooled_out[:, lanes] = (centred * scale[...] + shift[...] * total).astype(jnp.bfloat16)
+        pooled_out[:, lanes] = (centred * stats[1:2] + shift[...] * total).astype(jnp.bfloat16)
 
 
 def unpool_kernel(
     rois, floats, ints, order, base, slope, grads, p2, p3, p4, p5,
-    o2, o3, o4, o5, maps, sums, slots, sems, out_sems,
+    o2, o3, o4, o5, maps, sums, slots, sems, out_sems, finish=None,
 ):
     channels = base.shape[0]
     stride = rois + SPARE
@@ -308,15 +320,21 @@
             (channels, extra * LANES), jnp.float32
         )
 
-    def item(region, chunk, tile_x):
-        kernel_w, first_tile, across = window_weights(floats, ints, rois, region, chunk, tile_x)
+    def item(region, chunk, tile_x, span=SPAN):
+        kernel_w, first_tile, across = window_weights(
+            floats, ints, rois, region, chunk, tile_x, span
+        )
         mine = slots[pl.ds(region, SLOTS, stride=stride), :]
         stacked = jnp.concatenate([mine[:, :channels], mine[:, channels:]], axis=0)
         turned = stacked.T.astype(jnp.bfloat16)
         result = jnp.dot(turned, kernel_w, preferred_element_type=jnp.float32)
-        for at in range(SPAN):
+        for at in range(span):
             lanes = tile_lanes(first_tile, across, at)
             sums[:, lanes] = sums[:, lanes] + result[:, at * LANES : (at + 1) * LANES]
+
+    def narrow(regions):
+        for region in regions:
+            item(region, None, None, NARROW)
 
     def first(regions):
         for region in regions:
@@ -328,12 +346,16 @@
             sums.at[:, pl.ds(FIRST[level] * LANES, cells)], outs[level].at[0], out_sems.at[level]
         )
 
-    low_end, low_multi, rest_end, all_end = ends_of(order)
-    for_groups(order, 0, low_multi, GROUP, first)
-    for_parts(ints, order, rois, low_end, low_multi, MORE, item)
+    ends = ends_of(order)
+    for_groups(order, 0, ends[1], MORE, first)
+    for_groups(order, ends[1], ends[2], GROUP, narrow)
+    for_parts(ints, order, rois, 0, ends[0], MORE, item)
     send(0).start()
-    for_groups(order, low_multi, all_end, GROUP, first)
-    for_parts(ints, order, rois, rest_end, all_end, MORE, item)
+    if finish is not None:
+        finish()
+    for_groups(order, ends[2], ends[3], GROUP, narrow)
+    for_groups(order, ends[3], ends[5], MORE, first)
+    for_parts(ints, order, rois, ends[4], ends[5], MORE, item)
     for level in range(1, 4):
         send(level).start()
     for level in range(4):
@@ -346,13 +368,13 @@
 LIMIT = 60 * 1024 * 1024
 
 
-def pool_maps(floats, ints, order, mean, scale, shift, planes, rois):
+def pool_maps(floats, ints, order, stats, shift, planes, rois):
     channels = planes[0].shape[1]
     flat = jax.ShapeDtypeStruct((rois, WIDE), jnp.bfloat16)
     return pl.pallas_call(
         functools.partial(pool_kernel, rois),
         out_shape=(flat, flat, flat),
-        in_specs=[SMEM, SMEM, SMEM, VMEM, VMEM, VMEM, ANY, ANY, ANY, ANY],
+        in_specs=[SMEM, SMEM, SMEM, VMEM, VMEM, ANY, ANY, ANY, ANY],
         out_specs=(VMEM, VMEM, VMEM),
         scratch_shapes=[
             pltpu.VMEM((channels + 16, PADDED * LANES), jnp.bfloat16),
@@ -361,7 +383,7 @@
         ],
         compiler_params=pltpu.CompilerParams(vmem_limit_bytes=LIMIT),
         name="pool",
-    )(floats, ints, order, mean, scale, shift, *planes)
+    )(floats, ints, order, stats, shift, *planes)
 
 
 def unpool_maps(floats, ints, order, base, slope, grads, planes, rois):
@@ -458,7 +480,9 @@
         return jnp.concatenate([vector, vector])[None]
 
     pooled, centred, weight = pool_maps(
-        floats, ints, order, twice(mean), twice(scale), twice(norm_bias), planes, rois
+        floats, ints, order,
+        jnp.concatenate([twice(mean), twice(scale), jnp.zeros((6, LANES), jnp.float32)]),
+        twice(norm_bias), planes, rois
     )
 
     partial_six = jnp.dot(pooled, wide, preferred_element_type=jnp.float32).astype(jnp.bfloat16)
@@ -626,13 +650,6 @@
     return list(range(0, rows, 2)) + list(range(rows - 1, 0, -2))
 
 
-def origin(kappa, rows, cols, position):
-    far = position >= rows // 2
-    plane = rows - 1 - position if far else position
-    code = lax.rem(plane + cols - kappa, cols)
-    return 2 * lax.rem(code, 2) + lax.div(code, 2), int(far)
-
-
 def position_of(kappa, rows, cols, block, half):
     plane = lax.rem(2 * (block % 2) + block // 2 + kappa, cols)
     return rows - 1 - plane if half else plane
@@ -705,8 +722,12 @@
 
 
 def stats_kernel(
-    rows, pixels, facts, p2, p3, p4, p5, out, maps, slots, sems, sends, recvs
+    rows, pixels, facts, small, p2, p3, p4, p5, out, small_out,
+    maps, slots, sems, sends, recvs, small_sends, small_recvs,
 ):
+    row = lax.axis_index("roi")
+    depth = rows // 2
+    plane, side = lax.div(row, 2), lax.rem(row, 2)
     channels = maps.shape[0]
     planes = (p2, p3, p4, p5)
     pieces = [(level, at) for level in range(4) for at in range(4 if level == 0 else 1)]
@@ -723,6 +744,23 @@
 
     for index in range(len(pieces)):
         fetch(index).start()
+    small_out[row] = small[...]
+    along = [
+        remote(small, small_out.at[row], small_sends, small_recvs, step - 1, "roi",
+               lax.rem(plane + step, depth) * 2 + side)
+        for step in range(1, depth)
+    ]
+    across = []
+    for step in range(depth):
+        block = small_out.at[lax.rem(plane + depth - step, depth) * 2 + side]
+        across.append(
+            remote(block, block, small_sends, small_recvs, depth - 1 + step, "roi",
+                   row + 1 - 2 * side)
+        )
+    met(rows - 1)
+    for copy in along:
+        copy.start()
+    across[0].start()
 
     def add(at, carry):
         one, two = carry
@@ -739,12 +777,14 @@
         fetch(index).wait()
         carry = lax.fori_loop(start // 4, (start + tiles) // 4, add, carry)
     sums = [jnp.sum(item.T, axis=0, keepdims=True) for item in carry]
-    me = lax.axis_index("roi")
-    slots[me] = jnp.concatenate(
+    slots[row] = jnp.concatenate(
         [jnp.concatenate(sums, axis=1), facts[1:2], jnp.zeros((6, LANES), jnp.float32)], axis=0
     )
-    met(rows - 1)
-    for copy in share(slots, "roi", rows, sends, recvs):
+    copies = share(slots, "roi", rows, sends, recvs)
+    for step in range(1, depth):
+        along[step - 1].wait_recv()
+        across[step].start()
+    for copy in copies:
         copy.wait()
     total = slots[0]
     for at in range(1, rows):
@@ -757,40 +797,20 @@
     out[...] = jnp.concatenate(
         [mean[:1], scale[:1], inv_std[:1], total[1:2], jnp.zeros((4, LANES), jnp.float32)], axis=0
     )
-
-
-def gather_small_kernel(rows, cols, mine, out, sends, recvs, col_sends, col_recvs, sem):
-    row, col = lax.axis_index("roi"), lax.axis_index("col")
-    depth = rows // 2
-    plane, side = lax.div(row, 2), lax.rem(row, 2)
-    partner = row + 1 - 2 * side
-    greet("roi", rows)
-    greet("col", cols)
-    own = pltpu.make_async_copy(mine, out.at[col, row], sem)
-    own.start()
-    own.wait()
-    met(rows + cols - 2)
-    along = [
-        remote(mine, out.at[col, row], sends, recvs, step - 1, "roi",
-               lax.rem(plane + step, depth) * 2 + side)
-        for step in range(1, depth)
-    ]
-    across = []
-    for step in range(depth):
-        source = lax.rem(plane + depth - step, depth) * 2 + side
-        block = out.at[col, source]
-        across.append(remote(block, block, sends, recvs, depth - 1 + step, "roi", partner))
-    for copy in along:
-        copy.start()
-    across[0].start()
-    for step in range(1, depth):
-        along[step - 1].wait_recv()
-        across[step].start()
     for copy in along:
         copy.wait_send()
     for copy in across:
         copy.wait()
-    relay = Relay(lambda at: out.at[at], col_sends, col_recvs, 0)
+
+
+def gather_small_kernel(cols, mine, out, sends, recvs, sem):
+    col = lax.axis_index("col")
+    greet("col", cols)
+    own = pltpu.make_async_copy(mine, out.at[col], sem)
+    own.start()
+    own.wait()
+    met(cols - 1)
+    relay = Relay(lambda at: out.at[at], sends, recvs, 0)
     relay.start()
     relay.forward()
     relay.wait()
@@ -799,49 +819,56 @@
 def place_wide(pieces, wide, sems, rows, cols):
     few, piece = pieces.shape[2], pieces.shape[3]
     kappa = lax.axis_index("col")
-    copies = []
-    for position in range(rows):
-        block, half = origin(kappa, rows, cols, position)
-        span = pl.ds(half * few, few)
-        lanes = pl.ds(pl.multiple_of(block * piece, piece), piece)
-        copies.append(
-            pltpu.make_async_copy(
-                pieces.at[position, pl.ds(0, LEADING)],
-                wide.at[pl.ds(0, LEADING), span, lanes],
-                sems.at[position, 0],
-            )
-        )
-        for at in range(LEADING, len(KEPT)):
+    blocks = []
+    for block in range(cols):
+        copies = []
+        for half in range(2):
+            position = position_of(kappa, rows, cols, block, half)
+            span, lanes = pl.ds(half * few, few), pl.ds(block * piece, piece)
+            place = 2 * block + half
             copies.append(
                 pltpu.make_async_copy(
-                    pieces.at[position, at],
-                    wide.at[KEPT[at], span, lanes],
-                    sems.at[position, at - LEADING + 1],
+                    pieces.at[position, pl.ds(0, LEADING)],
+                    wide.at[pl.ds(0, LEADING), span, lanes],
+                    sems.at[place, 0],
                 )
             )
-    for copy in copies:
-        copy.start()
+            for at in range(LEADING, len(KEPT)):
+                copies.append(
+                    pltpu.make_async_copy(
+                        pieces.at[position, at],
+                        wide.at[KEPT[at], span, lanes],
+                        sems.at[place, at - LEADING + 1],
+                    )
+                )
+        blocks.append(copies)
+    for copies in blocks:
+        for copy in copies:
+            copy.start()
     for at in SPARES:
         wide[at] = jnp.zeros(wide.shape[1:], wide.dtype)
-    return copies
+    return blocks
 
 
 def head_kernel(
-    rows, cols, classes, boxes, pooled, facts, score_bias, small, pieces,
+    rows, cols, classes, boxes, facts, score_bias, pooled_in, small_in, pieces,
     g6_all, g7_out, hid6_out, hid7_out, gs_out, scores_out, losses_out,
-    wide, mine, taken, sems, sends, recvs, relay_sends, relay_recvs,
+    pooled, small, wide, mine, taken, in_sems, sems, sends, recvs, relay_sends, relay_recvs,
 ):
     me = lax.axis_index("col")
     rois, hidden = g6_all.shape
     quarter, piece = rois // cols, hidden // cols
     greet("col", cols)
-    copies = place_wide(pieces, wide, sems, rows, cols)
+    pooled_copy = pltpu.make_async_copy(pooled_in, pooled, in_sems.at[0])
+    small_copy = pltpu.make_async_copy(small_in, small, in_sems.at[1])
+    pooled_copy.start()
+    blocks = place_wide(pieces, wide, sems, rows, cols)
+    small_copy.start()
+    pooled_copy.wait()
     met(cols - 1)
-    for copy in copies:
-        copy.wait()
 
     def sending(part, step):
-        lanes = pl.ds(pl.multiple_of(part * piece, piece), piece)
+        lanes = pl.ds(part * piece, piece)
         peer = lax.rem(me + step, cols)
         return pltpu.make_async_remote_copy(
             src_ref=mine.at[peer, :, lanes],
@@ -852,8 +879,10 @@
             device_id_type=MESH,
         )
 
-    def first_layer(part, carry):
-        lanes = pl.ds(pl.multiple_of(part * piece, piece), piece)
+    for part in range(cols):
+        for copy in blocks[part]:
+            copy.wait()
+        lanes = slice(part * piece, (part + 1) * piece)
         weights = wide[:, :, lanes].reshape(WIDE, piece)
         result = jnp.dot(pooled[...], weights, preferred_element_type=jnp.float32)
         result = result.astype(jnp.bfloat16)
@@ -861,9 +890,7 @@
             mine[at, :, lanes] = result[at * quarter : (at + 1) * quarter]
         for step in range(1, cols):
             sending(part, step).start()
-        return carry
-
-    lax.fori_loop(0, cols, first_layer, 0)
+    small_copy.wait()
     for part in range(cols):
         for step in range(1, cols):
             sending(part, step).wait()
@@ -927,25 +954,33 @@
     g7 = (contract_last(score_grads, head) * slope_seven).astype(jnp.bfloat16)
     g7_out[...] = g7
     place = pl.ds(pl.multiple_of(me * quarter, quarter), quarter)
+    relays = []
     for at in range(cols):
         lanes = slice(at * piece, (at + 1) * piece)
         back = jnp.dot(g7, deep[at], preferred_element_type=jnp.float32)
         sigma, value = sigma_six[:, lanes], pre_six[:, lanes]
         back = back * (sigma * (1.0 + value * (1.0 - sigma)))
         g6_all[place, lanes] = back.astype(jnp.bfloat16)
-    relay = Relay(
-        lambda at: g6_all.at[pl.ds(pl.multiple_of(at * quarter, quarter), quarter)],
-        relay_sends, relay_recvs, 0,
-    )
-    relay.start()
-    relay.forward()
-    relay.wait()
+        relays.append(
+            Relay(
+                lambda owner, at=at: g6_all.at[
+                    pl.ds(pl.multiple_of(owner * quarter, quarter), quarter),
+                    pl.ds(at * piece, piece),
+                ],
+                relay_sends, relay_recvs, 3 * at,
+            )
+        )
+        relays[-1].start()
+    for relay in relays:
+        relay.forward()
+    for relay in relays:
+        relay.wait()
 
 
 def wide_grad_kernel(
     rows, cols, pooled, g6_all, g7, hid6, hid7, gs, losses,
     terms, g7_all, losses_all,
-    hid6_own, buffers, extras, head_mine, head_taken, out_sems, sends, recvs,
+    hid6_own, buffers, last, extras, head_mine, head_taken, out_sems, sends, recvs,
 ):
     me = lax.axis_index("col")
     rois, hidden = g6_all.shape
@@ -991,6 +1026,17 @@
         span = pl.ds(pl.multiple_of(at * size, size), size)
         return pltpu.make_async_copy(buffers.at[slot], terms.at[:, span], out_sems.at[slot])
 
+    def put(result, target, row, parts):
+        for column in range(cols):
+            columns = slice(column * piece, (column + 1) * piece)
+            for half in range(2):
+                position = position_of(me, rows, cols, column, half)
+                for index, part in enumerate(parts):
+                    first = (part * 2 + half) * few
+                    target[position, row + index * few : row + (index + 1) * few, :] = result[
+                        first : first + few, columns
+                    ]
+
     def step(pair, carry):
         for slot in range(2):
             at = pair * 2 + slot
@@ -1001,22 +1047,23 @@
 
             lanes = pl.ds(pl.multiple_of(at * 2 * LANES, 2 * LANES), 2 * LANES)
             result = contract_first(pooled[:, lanes], g6_all[...]).astype(jnp.bfloat16)
-            for column in range(cols):
-                columns = slice(column * piece, (column + 1) * piece)
-                for half in range(2):
-                    position = position_of(me, rows, cols, column, half)
-                    for part in range(4):
-                        first = (part * 2 + half) * few
-                        buffers[slot, position, part * few : (part + 1) * few, :] = result[
-                            first : first + few, columns
-                        ]
+            put(result, buffers.at[slot], 0, range(4))
             leaving(slot, at).start()
         return carry
-
-    pairs = len(USED) // 4
-    lax.fori_loop(0, pairs - 3, step, 0)
+    pairs = LEADING // 8
+    lax.fori_loop(0, pairs - 1, step, 0)
     relay.forward()
-    lax.fori_loop(pairs - 3, pairs, step, 0)
+    lax.fori_loop(pairs - 1, pairs, step, 0)
+    row = 0
+    for at in range(2 * pairs, len(USED) // 2):
+        parts = [part for part in range(4) if 4 * at + part in KEPT]
+        lanes = slice(at * 2 * LANES, (at + 1) * 2 * LANES)
+        result = contract_first(pooled[:, lanes], g6_all[...]).astype(jnp.bfloat16)
+        put(result, last, row, parts)
+        row += len(parts) * few
+    first = 2 * pairs * 4 * few
+    rest = pltpu.make_async_copy(last, terms.at[:, pl.ds(first, row)], out_sems.at[2])
+    rest.start()
     relay.wait()
     for copy in copies:
         copy.wait()
@@ -1030,20 +1077,14 @@
         extras[position, owned : owned + per, :] = jnp.concatenate(
             [total.astype(jnp.bfloat16), nothing], axis=1
         )
+    more = pltpu.make_async_copy(
+        extras, terms.at[:, pl.ds(first + row, owned + per)], out_sems.at[3]
+    )
+    more.start()
     for slot in range(2):
         leaving(slot, 2 * pairs - 2 + slot).wait()
-    copies = [
-        pltpu.make_async_copy(
-            extras.at[:, pl.ds(at * few, few)],
-            terms.at[:, pl.ds(SPARES[at] * few, few)],
-            out_sems.at[2 + at],
-        )
-        for at in range((owned + per) // few)
-    ]
-    for copy in copies:
-        copy.start()
-    for copy in copies:
-        copy.wait()
+    rest.wait()
+    more.wait()
 
 
 def pool_grad_kernel(
@@ -1055,7 +1096,7 @@
     channels = base.shape[0]
     piece = hidden // cols
     greet("roi", rows)
-    copies = place_wide(pieces, wide, sems, rows, cols)
+    blocks = place_wide(pieces, wide, sems, rows, cols)
     own = pl.ds(pl.multiple_of(col * piece, piece), piece)
 
     def columns(values):
@@ -1070,8 +1111,9 @@
     losses = losses_all[0]
     for at in range(1, cols):
         losses = losses + losses_all[at]
-    for copy in copies:
-        copy.wait()
+    for copies in blocks:
+        for copy in copies:
+            copy.wait()
     scale = stats[1:2]
 
     def step(at, carry):
@@ -1115,14 +1157,174 @@
     base[...] = jnp.broadcast_to(base_row[:, :channels], (LANES, channels)).T
 
 
-def restore_kernel(few, term, out, half):
+def deliver_kernel(rows, cols, few, term, out, held, taken, half, sems, sends, recvs):
+    row, col = lax.axis_index("roi"), lax.axis_index("col")
+    plane, side = lax.div(row, 2), lax.rem(row, 2)
+    chip, core = lax.div(col, 2), lax.rem(col, 2)
+    near = {"roi": row, "col": cols - 1 - col}
+    crossing = lax.rem(lax.rem(plane + cols - col, cols), 2) != chip
+    kappa = jnp.where(crossing, cols - 1 - col, col)
+    core_there = lax.div(lax.rem(plane + cols - kappa, cols), 2)
+    target = {"roi": kappa * 2 + side, "col": 2 * chip + core_there}
+    alone = (kappa == plane) & (core_there == core)
+    plane_from = lax.rem(2 * core + chip + plane, cols)
+    core_from = jnp.where(lax.div(plane, 2) == chip, lax.rem(plane, 2), 1 - lax.rem(plane, 2))
+    source = {"roi": plane_from * 2 + side, "col": 2 * chip + core_from}
+    barrier = pltpu.get_barrier_semaphore()
+
+    @pl.when(crossing)
+    def _():
+        pl.semaphore_signal(barrier, inc=1, device_id=near, device_id_type=MESH)
+
+    @pl.when(jnp.logical_not(alone))
+    def _():
+        pl.semaphore_signal(barrier, inc=1, device_id=source, device_id_type=MESH)
+
+    @pl.when(crossing | jnp.logical_not(alone))
+    def _():
+        pl.semaphore_wait(barrier, crossing.astype(jnp.int32) + 1 - alone.astype(jnp.int32))
+
+    count = 7
+    size = len(KEPT) // count
+    spans = [pl.ds(at * size * few, size * few) for at in range(count)]
+
+    def over(at):
+        return pltpu.make_async_remote_copy(
+            src_ref=term.at[spans[at]], dst_ref=held.at[spans[at]],
+            send_sem=sends.at[0, at], recv_sem=recvs.at[0, at],
+            device_id=near, device_id_type=MESH,
+        )
+
+    def along(block, at):
+        return pltpu.make_async_remote_copy(
+            src_ref=block.at[spans[at]], dst_ref=taken.at[spans[at]],
+            send_sem=sends.at[1, at], recv_sem=recvs.at[1, at],
+            device_id=target, device_id_type=MESH,
+        )
+
+    def inside(block, at):
+        return pltpu.make_async_copy(block.at[spans[at]], taken.at[spans[at]], sems.at[at])
+
+    def pass_on(block, at):
+        @pl.when(alone)
+        def _():
+            inside(block, at).start()
+
+        @pl.when(jnp.logical_not(alone))
+        def _():
+            along(block, at).start()
+
+    @pl.when(crossing)
+    def _():
+        for at in range(count):
+            over(at).start()
+        for at in range(count):
+            over(at).wait_recv()
+            pass_on(held, at)
+
+    @pl.when(jnp.logical_not(crossing))
+    def _():
+        for at in range(count):
+            pass_on(term, at)
+
+    for chunk in range(count):
+        @pl.when(alone)
+        def _():
+            inside(held, chunk).wait()
+
+        @pl.when(jnp.logical_not(alone))
+        def _():
+            along(held, chunk).wait_recv()
+
+        for index in range(chunk * size, (chunk + 1) * size):
+            slot = KEPT[index]
+            place = pl.ds(slot // 2 % 7 * 7 + slot // 14 + 4 * (slot % 2), few, stride=49)
+            for part in range(out.shape[1] // LANES):
+                half[part, place, :] = taken[
+                    index * few : (index + 1) * few, part * LANES : (part + 1) * LANES
+                ].astype(jnp.float32)
     for part in range(out.shape[1] // LANES):
-        lanes = slice(part * LANES, (part + 1) * LANES)
-        for slot in range(len(KEPT)):
-            at = KEPT[slot]
-            place = pl.ds(at // 2 % 7 * 7 + at // 14 + 4 * (at % 2), few, stride=49)
-            half[part, place, :] = term[at * few : (at + 1) * few, lanes].astype(jnp.float32)
-        out[:, lanes] = half[part]
+        out[:, part * LANES : (part + 1) * LANES] = half[part]
+
+    @pl.when(crossing)
+    def _():
+        for at in range(count):
+            over(at).wait_send()
+
+    @pl.when(jnp.logical_not(alone))
+    def _():
+        for at in range(count):
+            along(held, at).wait_send()
+
+
+def unpool_all_kernel(
+    rois, rows, cols, classes, boxes, floats, ints, order, base, slope, totals, grads, *rest
+):
+    planes, outs, few, scratch = rest[:4], rest[4:8], rest[8:16], rest[16:]
+    gain, shift, bias_six, bias_seven, bias_cls, bias_box, cls_loss, box_loss = few
+    channels, per = gain.shape[0], bias_seven.shape[0]
+    row, col = lax.axis_index("roi"), lax.axis_index("col")
+
+    def finish():
+        head = totals[:8]
+        turned = pltpu.roll(head, channels, 1)
+        gain[...] = totals[8:][7, :channels]
+        shift[...] = turned[0, :channels]
+        wide_lines = bias_six.shape[0] // LANES
+        for at in range(wide_lines):
+            bias_six[at * LANES : (at + 1) * LANES] = head[1 + at]
+        place = (row * cols + col) * per
+        line = totals[pl.ds(1 + wide_lines + lax.div(place, LANES), 1), :]
+        line = pltpu.roll(
+            jnp.broadcast_to(line, (8, LANES)), lax.rem(LANES - lax.rem(place, LANES), LANES), 1
+        )
+        bias_seven[...] = line[0, :per]
+        first = 1 + (cols + 1) * wide_lines
+        scores = jnp.broadcast_to(totals[first : first + 1], (8, LANES))
+        bias_cls[...] = scores[0, :classes]
+        bias_box[...] = pltpu.roll(scores, LANES - classes, 1)[0, :boxes]
+        cls_loss[...] = totals[first + 1 : first + 2, :1] / (rois * rows)
+        box_loss[...] = jnp.sum(totals[first + 2 : first + 3], axis=1, keepdims=True) / (
+            rois * rows
+        )
+
+    unpool_kernel(
+        rois, floats, ints, order, base, slope, grads, *planes, *outs, *scratch, finish=finish
+    )
+
+
+def unpool_all(
+    floats, ints, order, base, slope, totals, grads, planes, rois, rows, cols, classes, boxes,
+    piece,
+):
+    channels = planes[0].shape[1]
+    f32 = jnp.float32
+    results = pl.pallas_call(
+        functools.partial(unpool_all_kernel, rois, rows, cols, classes, boxes),
+        out_shape=tuple(shaped(plane.shape, f32) for plane in planes)
+        + (
+            shaped((channels,), f32),
+            shaped((channels,), f32),
+            shaped((piece,), f32),
+            shaped((piece // rows,), f32),
+            shaped((classes,), f32),
+            shaped((boxes,), f32),
+            shaped((1, 1), f32),
+            shaped((1, 1), f32),
+        ),
+        in_specs=[SMEM] * 3 + [VMEM] * 4 + [ANY] * 4,
+        out_specs=(ANY,) * 4 + (VMEM,) * 8,
+        scratch_shapes=[
+            pltpu.VMEM((channels, ALL_TILES * LANES), jnp.bfloat16),
+            pltpu.VMEM((channels, PADDED * LANES), f32),
+            pltpu.VMEM((SLOTS * (rois + SPARE), LANES), f32),
+            pltpu.SemaphoreType.DMA((7,)),
+            pltpu.SemaphoreType.DMA((4,)),
+        ],
+        compiler_params=pltpu.CompilerParams(vmem_limit_bytes=LIMIT),
+        name="unpool",
+    )(floats, ints, order, base, slope, totals, grads, *planes)
+    return results[:4], results[4:]
 
 
 def comm_params(number):
@@ -1135,34 +1337,38 @@
     return jax.ShapeDtypeStruct(shape, dtype)
 
 
-def statistics(facts, planes, rows, pixels):
+def statistics(facts, small, planes, rows, pixels):
     channels = planes[0].shape[1]
+    moves = rows // 2 - 1 + rows // 2
     return pl.pallas_call(
         functools.partial(stats_kernel, rows, pixels),
-        out_shape=shaped((8, LANES), jnp.float32),
-        in_specs=[VMEM, ANY, ANY, ANY, ANY],
-        out_specs=VMEM,
+        out_shape=(
+            shaped((8, LANES), jnp.float32),
+            shaped((rows,) + small.shape, small.dtype),
+        ),
+        in_specs=[VMEM, VMEM, ANY, ANY, ANY, ANY],
+        out_specs=(VMEM, VMEM),
         scratch_shapes=[
             pltpu.VMEM((channels, ALL_TILES * LANES), jnp.bfloat16),
             pltpu.VMEM((rows, 8, LANES), jnp.float32),
             pltpu.SemaphoreType.DMA((7,)),
             pltpu.SemaphoreType.DMA((rows - 1,)),
             pltpu.SemaphoreType.DMA((rows - 1,)),
+            pltpu.SemaphoreType.DMA((moves,)),
+            pltpu.SemaphoreType.DMA((moves,)),
         ],
         compiler_params=comm_params(0),
         name="statistics",
-    )(facts, *planes)
-
-
-def gather_small(mine, rows, cols):
+    )(facts, small, *planes)
+
+
+def gather_small(mine, cols):
     return pl.pallas_call(
-        functools.partial(gather_small_kernel, rows, cols),
-        out_shape=shaped((cols, rows) + mine.shape, mine.dtype),
+        functools.partial(gather_small_kernel, cols),
+        out_shape=shaped((cols,) + mine.shape, mine.dtype),
         in_specs=[VMEM],
         out_specs=VMEM,
         scratch_shapes=[
-            pltpu.SemaphoreType.DMA((rows - 1,)),
-            pltpu.SemaphoreType.DMA((rows - 1,)),
             pltpu.SemaphoreType.DMA((3,)),
             pltpu.SemaphoreType.DMA((3,)),
             pltpu.SemaphoreType.DMA,
@@ -1187,21 +1393,24 @@
             shaped((quarter, LANES), f32),
             shaped((8, LANES), f32),
         ),
-        in_specs=[VMEM, VMEM, VMEM, VMEM, ANY],
+        in_specs=[VMEM, VMEM, ANY, ANY, ANY],
         out_specs=(VMEM,) * 7,
         scratch_shapes=[
+            pltpu.VMEM(pooled.shape, bf16),
+            pltpu.VMEM(small.shape, bf16),
             pltpu.VMEM((2 * len(USED), channels, hidden), bf16),
             pltpu.VMEM((cols, quarter, hidden), bf16),
             pltpu.VMEM((cols - 1, quarter, hidden), bf16),
+            pltpu.SemaphoreType.DMA((2,)),
             pltpu.SemaphoreType.DMA((rows, 8)),
             pltpu.SemaphoreType.DMA((cols - 1, cols)),
             pltpu.SemaphoreType.DMA((cols - 1, cols)),
-            pltpu.SemaphoreType.DMA((3,)),
-            pltpu.SemaphoreType.DMA((3,)),
+            pltpu.SemaphoreType.DMA((3 * cols,)),
+            pltpu.SemaphoreType.DMA((3 * cols,)),
         ],
         compiler_params=comm_params(2),
         name="head",
-    )(pooled, facts, score_bias, small, pieces)
+    )(facts, score_bias, pooled, small, pieces)
 
 
 def wide_grads(pooled, g6_all, g7, hid6, hid7, gs, losses, rows, cols):
@@ -1212,7 +1421,7 @@
     return pl.pallas_call(
         functools.partial(wide_grad_kernel, rows, cols),
         out_shape=(
-            shaped((rows, 2 * len(USED) * few, piece), bf16),
+            shaped((rows, len(KEPT) * few + owned + per, piece), bf16),
             shaped((rois, hidden), bf16),
             shaped((cols, 8, LANES), f32),
         ),
@@ -1221,10 +1430,11 @@
         scratch_shapes=[
             pltpu.VMEM((rois, piece), bf16),
             pltpu.VMEM((2, rows, 4 * few, piece), bf16),
+            pltpu.VMEM((rows, (len(KEPT) - LEADING // 8 * 8) * few, piece), bf16),
             pltpu.VMEM((rows, owned + per, piece), bf16),
             pltpu.VMEM((cols, rows, per, LANES), bf16),
             pltpu.VMEM((cols - 1, rows, per, LANES), bf16),
-            pltpu.SemaphoreType.DMA((2 + len(SPARES),)),
+            pltpu.SemaphoreType.DMA((4,)),
             pltpu.SemaphoreType.DMA((12,)),
             pltpu.SemaphoreType.DMA((12,)),
         ],
@@ -1259,15 +1469,23 @@
     )(g6_all, g7_all, losses_all, centred, weight, stats, pieces)
 
 
-def restore(term, few):
+def deliver(term, rows, cols, few):
+    piece, kept = term.shape[1], len(KEPT) * few
     return pl.pallas_call(
-        functools.partial(restore_kernel, few),
-        out_shape=shaped((49 * few, term.shape[1]), jnp.float32),
-        in_specs=[VMEM],
+        functools.partial(deliver_kernel, rows, cols, few),
+        out_shape=shaped((kept, piece), jnp.float32),
+        in_specs=[ANY],
         out_specs=VMEM,
-        scratch_shapes=[pltpu.VMEM((term.shape[1] // LANES, 49 * few, LANES), jnp.float32)],
-        compiler_params=pltpu.CompilerParams(vmem_limit_bytes=LIMIT),
-        name="restore",
+        scratch_shapes=[
+            pltpu.VMEM((kept, piece), term.dtype),
+            pltpu.VMEM((kept, piece), term.dtype),
+            pltpu.VMEM((piece // LANES, kept, LANES), jnp.float32),
+            pltpu.SemaphoreType.DMA((7,)),
+            pltpu.SemaphoreType.DMA((2, 7)),
+            pltpu.SemaphoreType.DMA((2, 7)),
+        ],
+        compiler_params=comm_params(5),
+        name="deliver",
     )(term)
 
 
@@ -1360,7 +1578,7 @@
     norm_facts = jnp.concatenate(
         [twice(norm_gain), jnp.full((1, LANES), count), jnp.zeros((6, LANES), f32)]
     )
-    stats = statistics(norm_facts, planes, rows, float(pixels))
+    stats, small = statistics(norm_facts, small, planes, rows, float(pixels))
     valid_total = stats[3, 0]
 
     picks = roi_image[None, :] == jnp.arange(4, dtype=jnp.int32)[:, None]
@@ -1376,9 +1594,8 @@
     block = lax.optimization_barrier((block, stats, floats, order))[0]
     pieces = lax.all_gather(block, "roi", axis=0, axis_index_groups=[ring])
     pooled, centred, weight = pool_maps(
-        floats, ints, order, stats[:1], stats[1:2], twice(norm_bias), planes, rois
-    )
-    small = gather_small(lax.optimization_barrier((small, pooled))[0], rows, cols)
+        floats, ints, order, stats, twice(norm_bias), planes, rois
+    )
 
     quarter = rois // cols
     first_row = lax.axis_index("col") * quarter
@@ -1403,6 +1620,8 @@
         ]
     )
     score_bias = jnp.pad(jnp.concatenate([cls_bias, box_bias]), (0, after))[None]
+    small, facts, score_bias, _ = lax.optimization_barrier((small, facts, score_bias, pooled))
+    small = gather_small(small, cols)
     g6_all, g7, hid6, hid7, gs, scores, losses = run_head(
         pooled, facts, score_bias, small, pieces, rows, cols, classes, boxes
     )
@@ -1420,38 +1639,39 @@
         g6_all, g7_all, losses_all, centred, weight, stats, pieces, rows, cols,
         float(pixels),
     )
-    input_grads = unpool_maps(floats, ints, order, base, slope, grads, planes, rois)
+    input_grads, few_grads = unpool_all(
+        floats, ints, order, base, slope, totals, grads, planes, rois, rows, cols, classes, boxes,
+        piece,
+    )
     term = lax.optimization_barrier((term, input_grads[3]))[0]
-    back = lax.ppermute(term, ("roi", "col"), [(there, here) for here, there in pairs])
-    fc6_weight_grad = restore(back, few)
-    extra = [
-        term[SPARES[at] * few : (SPARES[at] + 1) * few].astype(f32)
-        for at in range((fc7_weight.shape[0] + per) // few)
-    ]
-    fc7_weight_grad = jnp.concatenate(extra[:-1], axis=0)
-    cls_weight_grad = extra[-1][:, :classes]
-    box_weight_grad = extra[-1][:, classes : classes + boxes]
-
-    fc6_bias_grad = totals[1 : 1 + piece // LANES].reshape(-1)
-    seven = totals[1 + piece // LANES :][: cols * piece // LANES].reshape(-1)
-    place = (lax.axis_index("roi") * cols + lax.axis_index("col")) * per
-    fc7_bias_grad = lax.dynamic_slice_in_dim(seven, place, per)
-    line = 1 + (cols + 1) * piece // LANES
+    fc6_weight_grad = deliver(term, rows, cols, few)
+    kept = len(KEPT) * few
+    deep_rows = fc7_weight.shape[0]
+    extra = term[kept:].astype(f32)
+    fc7_weight_grad = extra[:deep_rows]
+    head_grad = extra[deep_rows:]
+    cls_weight_grad = head_grad[:, :classes]
+    box_weight_grad = head_grad[:, classes : classes + boxes]
+
+    (
+        norm_gain_grad, norm_bias_grad, fc6_bias_grad, fc7_bias_grad, class_bias_grad,
+        box_bias_grad, cls_loss, box_loss,
+    ) = few_grads
     return (
-        totals[line + 1, 0] / (rois * rows),
-        jnp.sum(totals[line + 2]) / (rois * rows),
+        cls_loss[0, 0],
+        box_loss[0, 0],
         decoded,
         *input_grads,
-        totals[15, :channels],
-        totals[0, channels:],
+        norm_gain_grad,
+        norm_bias_grad,
         fc6_weight_grad,
         fc6_bias_grad,
         fc7_weight_grad,
         fc7_bias_grad,
         cls_weight_grad,
-        totals[line, :classes],
+        class_bias_grad,
         box_weight_grad,
-        totals[line, classes : classes + boxes],
+        box_bias_grad,
     )
 
 

time: 317 us -> 284 us (0.90)
  waiting for transfers between devices: 35.1 us -> 3.78 us
  Pallas kernels: 230 us -> 236 us
  between operations: 18.8 us -> 15.2 us
    ppermute x1 -> x0, waiting for transfers between devices: 34 us -> none  [local_near(): lax.ppermute(term, ('roi', 'col'), [(there, here) for here, there in pairs])]
    pallas_call x4, Pallas kernels: 118 us -> 128 us  [the longest x1 54.3 us: unpool_all(): pl.pallas_call(functools.partial(unpool_all_kernel, rois, rows, cols, cla...]
  transfers between devices with their start and end apart: 4 -> 3, of which waited for: 2 -> 1; matrix products, arithmetic and copies ran while one was open for 7% -> 6% of each run, Pallas kernels for 58% -> 59%
where the time goes in v4:
time: 284 us
  Pallas kernels  236 us (83%)
  local copies, waits for them, and re-layouts  17 us (6%)
  between operations  15.2 us (5%)
  other arithmetic  8.73 us (3%)
  waiting for transfers between devices  3.78 us (1%)
  starting transfers between devices  2.95 us (1%)
    pallas_call x1, Pallas kernels, unpool_all(): pl.pallas_call(functools.partial(unpool_all_kernel, rois, rows, cols, cla...  54.3 us
    pallas_call x1, Pallas kernels, pool_maps(): pl.pallas_call(functools.partial(pool_kernel, rois), out_shape=(flat, fla...  44.6 us
    pallas_call x1, Pallas kernels, run_head(): pl.pallas_call(functools.partial(head_kernel, rows, cols, classes, boxes)...  25.9 us
    pallas_call x1, Pallas kernels, deliver(): pl.pallas_call(functools.partial(deliver_kernel, rows, cols, few), out_sh...  25.9 us
    pallas_call x1, Pallas kernels, statistics(): pl.pallas_call(functools.partial(stats_kernel, rows, pixels), out_shape=(...  25.5 us
    pallas_call x1, Pallas kernels, pool_grads(): pl.pallas_call(functools.partial(pool_grad_kernel, rows, cols, pixels), o...  22.4 us
    pallas_call x1, Pallas kernels, gather_small(): pl.pallas_call(functools.partial(gather_small_kernel, cols), out_shape=sh...  21.9 us
    pallas_call x1, Pallas kernels, wide_grads(): pl.pallas_call(functools.partial(wide_grad_kernel, rows, cols), out_shape...  15.5 us
  transfers between devices with their start and end apart: 3, of which 1 were waited for; matrix products, arithmetic and copies ran while one was open for 6% of the time, Pallas kernels for 59%

profile of v4, /device:TPU:12, one launch (start us, length us, event | category | flops | bytes accessed | tf_op | source)
XLA Modules:
  0.0 283.6 jit_solution(9952592368980587852)
XLA Ops:
  7.2 1.4 reshape.451
  8.6 0.2 pad.26
  8.8 0.2 reshape.452
  9.1 0.2 copy.81
  9.3 0.2 copy.80
  9.6 2.9 %collective-permute-start = (bf16[49,32,256]{2,1,0:T(8,128)(2,1)S(1)}, bf16[49,32,256]{2,1,0:T(8,128)(2,1)S(1)}, u32[]{:S(2)}, u32[]{:S(2)}) collective-permute-start(bf16[49,32,256]{2,1,0:T(8,128)(2,1)S(1)} %pad_maximum_fusion), channel_id=1, source_target_pairs={{0,0},{4,4},{1,16},{5,20},{2,8},{6,12},{3,24},{7,28},{8,9},{12,13}... | collective-permute-start | bytes 2408456 | tf_op jit(solution)/shard_map/ppermute | solution.py:1561
  12.5 0.6 convert_reduce_fusion.1
  13.1 0.7 pad.54.clone
  13.9 0.1 copy.78
  14.0 0.1 copy.77
  14.2 0.1 select_reduce_fusion.1
  14.3 0.7 convert_reduce_fusion.2
  15.2 0.7 reshape.445.floats
  16.0 0.1 fusion.10
  16.0 0.6 maximum_maximum_fusion
  16.7 0.7 maximum_maximum_fusion.1.facts
  17.3 25.5 %statistics.1 = (f32[8,128]{1,0:T(8,128)}, bf16[8,5,32,256]{3,2,1,0:T(8,128)(2,1)}) custom-call(f32[8,128]{1,0:T(8,128)} %maximum_maximum_fusion.1.facts, bf16[5,32,256]{2,1,0:T(8,128)(2,1)} %bitcast.133, bf16[1,64,65536]{2,1,0:T(8,128)(2,1)} %rest_0_.1, bf16[1,64,16384]{2,1,0:T(8,128)(2,1)} %rest_1_.1, bf16[1,64,4096]{2,1,0:T(8,128)(2,1)} %rest_2_.1, ...), custom_call_target="tpu_custom_call" | custom-call | tf_op jit(solution)/shard_map/statistics/pallas_call | solution.py:1343
  42.8 0.2 convert_reduce_fusion
  43.0 0.2 select_reduce_fusion
  43.2 4.5 %concatenate.38.order = s32[406]{0:T(512)} concatenate(s32[384]{0:T(512)S(1)} %select_reduce_fusion, s32[16]{0:T(128)S(1)} %broadcast.310, s32[1]{0:T(128)} %bitcast.2, s32[1]{0:T(128)} %bitcast.3, s32[1]{0:T(128)} %bitcast.4, s32[1]{0:T(128)} %bitcast.5, s32[1]{0:T(128)} %bitcast.6, s32[1]{0:T(128)} %bitcast.7), dimensions={0} | concatenate | bytes 3248 | tf_op jit(solution)/shard_map/concatenate | solution.py:108
  47.8 0.9 copy-done
  48.7 1.2 slice.114
  50.0 0.7 reshape.446.ints
  50.7 0.8 dynamic-slice_convert_fusion
  51.5 0.1 copy.79
  52.3 0.6 maximum_bitcast_fusion.1.shift
  52.9 44.6 %pool.1 = (bf16[384,3584]{1,0:T(8,128)(2,1)}, bf16[384,3584]{1,0:T(8,128)(2,1)}, bf16[384,3584]{1,0:T(8,128)(2,1)}) custom-call(f32[2744]{0:T(1024)} %reshape.445.floats, s32[2352]{0:T(1024)} %reshape.446.ints, s32[406]{0:T(512)} %concatenate.38.order, f32[8,128]{1,0:T(8,128)} %get-tuple-element.54.stats, f32[1,128]{1,0:T(1,128)} %maximum_bitcast_fusion.1.shift, ...), custom_call_target="tpu_custom_call" | custom-call | tf_op jit(solution)/shard_map/pool/pallas_call | solution.py:374
  97.5 0.6 fusion.38.score_bias
  98.1 0.8 compare_select_fusion
  98.9 0.1 pad_bitcast_fusion
  98.9 0.1 fusion.2
  99.0 0.1 select_multiply_fusion
  99.1 0.7 pad_maximum_fusion.1.facts
  99.8 21.9 %gather_small.1.small_in = bf16[4,8,5,32,256]{4,3,2,1,0:T(8,128)(2,1)} custom-call(bf16[8,5,32,256]{3,2,1,0:T(8,128)(2,1)} %get-tuple-element.58.mine), custom_call_target="tpu_custom_call" | custom-call | tf_op jit(solution)/shard_map/gather_small/pallas_call | solution.py:1366
  121.8 25.9 %head.1 = (bf16[384,1024]{1,0:T(8,128)(2,1)}, bf16[96,1024]{1,0:T(8,128)(2,1)}, bf16[96,1024]{1,0:T(8,128)(2,1)}, bf16[96,1024]{1,0:T(8,128)(2,1)}, bf16[96,128]...) custom-call(f32[3,96,128]{2,1,0:T(8,128)} %pad_maximum_fusion.1.facts, f32[1,128]{1,0:T(1,128)} %fusion.38.score_bias, ...), custom_call_target="tpu_custom_call" | custom-call | tf_op jit(solution)/shard_map/head/pallas_call | solution.py:1385
  147.7 15.5 %wide_grads.1 = (bf16[8,1728,256]{2,1,0:T(8,128)(2,1)}, bf16[384,1024]{1,0:T(8,128)(2,1)}, f32[4,8,128]{2,1,0:T(8,128)}) custom-call(bf16[384,3584]{1,0:T(8,128)(2,1)} %get-tuple-element.55.pooled_in.pooled, bf16[384,1024]{1,0:T(8,128)(2,1)} %get-tuple-element.60.g6_all, bf16[96,1024]{1,0:T(8,128)(2,1)} %get-tuple-element.61.g7, ...), custom_call_target="tpu_custom_call" | custom-call | tf_op jit(solution)/shard_map/wide_grads/pallas_call | solution.py:1421
  163.2 0.8 copy-done.1
  164.0 0.2 exponential_reduce_fusion.1
  164.3 22.4 %pool_grads.1 = (bf16[384,3584]{1,0:T(8,128)(2,1)}, f32[16,128]{1,0:T(8,128)}, f32[64,128]{1,0:T(8,128)}, f32[64,128]{1,0:T(8,128)}) custom-call(bf16[384,1024]{1,0:T(8,128)(2,1)} %get-tuple-element.60.g6_all, bf16[384,1024]{1,0:T(8,128)(2,1)} %get-tuple-element.66.g7_all, f32[4,8,128]{2,1,0:T(8,128)} %get-tuple-element.67.losses_all, ...), custom_call_target="tpu_custom_call" | custom-call | tf_op jit(solution)/shard_map/pool_grads/pallas_call | solution.py:1450
  186.7 54.3 %unpool.1 = (f32[1,64,65536]{2,1,0:T(8,128)}, f32[1,64,16384]{2,1,0:T(8,128)}, f32[1,64,4096]{2,1,0:T(8,128)}, f32[1,64,1024]{2,1,0:T(8,128)}, f32[64]{0:T(128)}...) custom-call(f32[2744]{0:T(1024)} %reshape.445.floats, ...), custom_call_target="tpu_custom_call" | custom-call | tf_op jit(solution)/shard_map/unpool/pallas_call | solution.py:1302
  241.0 0.6 maximum_multiply_fusion
  241.6 3.7 %reduce-scatter.2.cloned.1.call-done.term = bf16[1728,256]{1,0:T(8,128)(2,1)} async-done(((bf16[13824,256]{1,0:T(8,128)(2,1)}), bf16[1728,256]{1,0:T(8,128)(2,1)}) %reduce-scatter.2.cloned.1.call-update) | async-done | bytes 884752 | tf_op jit(solution)/shard_map/reduce_scatter | solution.py:1634
  245.3 0.9 slice_convert_fusion
  246.3 0.6 slice.128
  246.9 0.7 slice.127
  247.5 25.9 %deliver.1 = f32[1568,256]{1,0:T(8,128)} custom-call(bf16[1728,256]{1,0:T(8,128)(2,1)} %reduce-scatter.2.cloned.1.call-done.term), custom_call_target="tpu_custom_call" | custom-call | tf_op jit(solution)/shard_map/deliver/pallas_call | solution.py:1474
  273.4 0.7 copy.82
  274.1 2.7 copy.84
  (71 shorter events, 0.8 us)
Async XLA Ops:
  7.2 114.6 %all-gather.3.cloned.1.call-start = ((), (), s32[]{:S(2)}) async-start(), calls=%async_computation.2 | async-start | bytes 7225344 | tf_op jit(solution)/shard_map/all_gather | solution.py:1595
  9.0 3.5 %copy-start.5 = (s32[384]{0:T(512)S(1)}, s32[384]{0:T(512)}, u32[]{:S(2)}) copy-start(s32[384]{0:T(512)} %param.41) | copy-start | bytes 4612
  9.0 4.9 %copy-start.9 = (s32[2,4]{1,0:T(2,128)S(1)}, s32[2,4]{1,0:T(2,128)}, u32[]{:S(2)}) copy-start(s32[2,4]{1,0:T(2,128)} %param.38) | copy-start | bytes 100
  9.0 4.9 %copy-start.10 = (f32[256]{0:T(256)S(1)}, f32[256]{0:T(256)}, u32[]{:S(2)}) copy-start(f32[256]{0:T(256)} %param.28) | copy-start | bytes 3076
  9.0 4.9 %copy-start.11 = (bf16[32]{0:T(256)(128)(2,1)S(1)}, bf16[32]{0:T(256)(128)(2,1)}, u32[]{:S(2)}) copy-start(bf16[32]{0:T(256)(128)(2,1)} %param.30) | copy-start | bytes 196
  9.0 5.0 %copy-start.8 = (bf16[32,4]{0,1:T(4,128)(2,1)S(1)}, bf16[32,4]{0,1:T(4,128)(2,1)}, u32[]{:S(2)}) copy-start(bf16[32,4]{0,1:T(4,128)(2,1)} %param.33) | copy-start | bytes 772
  9.1 5.1 %copy-start.3 = (s32[4,384]{1,0:T(4,128)S(1)}, s32[4,384]{1,0:T(4,128)}, u32[]{:S(2)}) copy-start(s32[4,384]{1,0:T(4,128)} %param.35) | copy-start | bytes 18436
  9.1 5.1 %copy-start.6 = (s32[384]{0:T(512)S(1)}, s32[384]{0:T(512)}, u32[]{:S(2)}) copy-start(s32[384]{0:T(512)} %param.37) | copy-start | bytes 4612
  9.1 5.2 %copy-start.7 = (s32[384]{0:T(512)S(1)}, s32[384]{0:T(512)}, u32[]{:S(2)}) copy-start(s32[384]{0:T(512)} %param.36) | copy-start | bytes 4612
  9.1 6.8 %copy-start.12 = (f32[64]{0:T(128)S(1)}, f32[64]{0:T(128)}, u32[]{:S(2)}) copy-start(f32[64]{0:T(128)} %param.25) | copy-start | bytes 772
  9.1 6.8 %copy-start.4 = (bf16[32,81]{1,0:T(8,128)(2,1)S(1)}, bf16[32,81]{1,0:T(8,128)(2,1)}, u32[]{:S(2)}) copy-start(bf16[32,81]{1,0:T(8,128)(2,1)} %param.31) | copy-start | bytes 15556
  9.1 6.9 %copy-start.2 = (bf16[128,256]{1,0:T(8,128)(2,1)S(1)}, bf16[128,256]{1,0:T(8,128)(2,1)}, u32[]{:S(2)}) copy-start(bf16[128,256]{1,0:T(8,128)(2,1)} %param.29) | copy-start | bytes 196612
  9.6 38.1 %collective-permute-start = (bf16[49,32,256]{2,1,0:T(8,128)(2,1)S(1)}, bf16[49,32,256]{2,1,0:T(8,128)(2,1)S(1)}, u32[]{:S(2)}, u32[]{:S(2)}) collective-permute-start(bf16[49,32,256]{2,1,0:T(8,128)(2,1)S(1)} %pad_maximum_fusion), channel_id=1, source_target_pairs={{0,0},{4,4},{1,16},{5,20},{2,8},{6,12},{3,24},{7,28},{8,9},{12,13}... | collective-permute-start | bytes 2408456 | tf_op jit(solution)/shard_map/ppermute | solution.py:1561
  17.3 34.9 %copy-start.13 = (f32[64]{0:T(128)S(1)}, f32[64]{0:T(128)}, u32[]{:S(2)}) copy-start(f32[64]{0:T(128)} %param.26) | copy-start | bytes 772
  47.8 0.9 copy-start
  48.7 196.6 %reduce-scatter.2.cloned.1.call-start = ((), (), s32[]{:S(2)}) async-start(), calls=%async_computation.1 | async-start | bytes 7962624 | tf_op jit(solution)/shard_map/reduce_scatter | solution.py:1634
  52.9 44.6 %copy-start.14 = (f32[4]{0:T(128)S(1)}, f32[4]{0:T(128)}, u32[]{:S(2)}) copy-start(f32[4]{0:T(128)} %param.34) | copy-start | bytes 52
  52.9 44.6 %copy-start.15 = (f32[81]{0:T(128)S(1)}, f32[81]{0:T(128)}, u32[]{:S(2)}) copy-start(f32[81]{0:T(128)} %param.32) | copy-start | bytes 976
  163.2 0.8 copy-start.1
Sparse Core Ops, SparseCore 0:
  48.8 71.2 all-gather.2
  163.4 81.8 reduce-scatter.1

commit v5 on v4

--- a/solution.py
+++ b/solution.py
@@ -14,7 +14,7 @@
 SPAN = 10
 NARROW = 8
 GROUP = 16
-MORE = 8
+MORE = 16
 SPARE = 8
 SIDES = tuple(CANVAS // (4 * 2**level) for level in range(4))
 TILES = tuple(side * side // LANES for side in SIDES)
@@ -199,10 +199,10 @@
 
 
 def pool_kernel(
-    rois, floats, ints, order, stats, shift, p2, p3, p4, p5,
-    pooled_out, centred_out, weight_out, maps, values, sems,
+    rois, floats, ints, order, p2, p3, p4, p5,
+    centred_out, weight_out, local_out, maps, values, sems,
 ):
-    channels = stats.shape[1] // 2
+    channels = p2.shape[1]
     stride = rois + SPARE
     copies = []
     for level, plane in enumerate((p2, p3, p4, p5)):
@@ -214,7 +214,8 @@
                 sems.at[level],
             )
         )
-        copies[-1].start()
+    for copy in copies[::-1]:
+        copy.start()
     ones = jnp.ones((16, 8 * LANES), jnp.bfloat16)
 
     def fill(at, carry):
@@ -228,7 +229,7 @@
         maps[:, pl.ds(ALL_TILES * LANES, extra * LANES)] = jnp.zeros(
             (channels + 16, extra * LANES), jnp.bfloat16
         )
-    for copy in copies:
+    for copy in copies[1:]:
         copy.wait()
 
     def item(region, chunk, tile_x, span=SPAN):
@@ -255,11 +256,35 @@
         values[place(region), : channels + 16] = values[place(region), : channels + 16] + item(region, chunk, tile_x)
 
     ends = ends_of(order)
+    for_groups(order, ends[3], ends[5], MORE, first)
+    for_parts(ints, order, rois, ends[4], ends[5], MORE, further)
+    copies[0].wait()
     for_groups(order, 0, ends[1], MORE, first)
+    for_parts(ints, order, rois, 0, ends[0], MORE, further)
     for_groups(order, ends[1], ends[3], GROUP, narrow)
-    for_groups(order, ends[3], ends[5], MORE, first)
-    for_parts(ints, order, rois, 0, ends[0], MORE, further)
-    for_parts(ints, order, rois, ends[4], ends[5], MORE, further)
+
+    def add(at, carry):
+        one, two = carry
+        for part in range(4):
+            lanes = pl.ds(pl.multiple_of((at * 4 + part) * LANES, LANES), LANES)
+            value = maps[pl.ds(0, channels), lanes].astype(jnp.float32)
+            one, two = one + value, two + value * value
+        return one, two
+
+    sums = lax.fori_loop(
+        0, ALL_TILES // 4, add, (jnp.zeros((channels, LANES), jnp.float32),) * 2
+    )
+    sums = [jnp.sum(item.T, axis=0, keepdims=True) for item in sums]
+    sums = jnp.broadcast_to(jnp.concatenate(sums, axis=1), (8, LANES))
+    low = lax.broadcasted_iota(jnp.int32, (8, LANES), 1) < channels
+    turned = pltpu.roll(sums, channels, 1)
+    cells = float(ALL_TILES * LANES)
+    mean = (jnp.where(low, sums, turned) / cells)[:1]
+    square = (jnp.where(low, turned, sums) / cells)[:1]
+    inverse = lax.rsqrt(jnp.maximum(square - mean * mean, 0.0) + EPSILON)
+    local_out[...] = jnp.concatenate(
+        [sums[:1], mean, inverse, jnp.zeros((5, LANES), jnp.float32)], axis=0
+    )
     low_lane = lax.broadcasted_iota(jnp.int32, (rois, LANES), 1) < channels
     for at, slot in enumerate(USED):
         lanes = pl.ds(at * LANES, LANES)
@@ -267,10 +292,8 @@
         two = values[pl.ds((slot + SLOTS) * stride, rois), :]
         value = jnp.where(low_lane, one, pltpu.roll(two, channels, 1))
         total = jnp.where(low_lane, one[:, channels : channels + 1], two[:, channels : channels + 1])
-        centred = value - stats[:1] * total
-        centred_out[:, lanes] = centred.astype(jnp.bfloat16)
+        centred_out[:, lanes] = ((value - mean * total) * inverse).astype(jnp.bfloat16)
         weight_out[:, lanes] = total.astype(jnp.bfloat16)
-        pooled_out[:, lanes] = (centred * stats[1:2] + shift[...] * total).astype(jnp.bfloat16)
 
 
 def unpool_kernel(
@@ -368,13 +391,13 @@
 LIMIT = 60 * 1024 * 1024
 
 
-def pool_maps(floats, ints, order, stats, shift, planes, rois):
+def pool_maps(floats, ints, order, planes, rois):
     channels = planes[0].shape[1]
     flat = jax.ShapeDtypeStruct((rois, WIDE), jnp.bfloat16)
     return pl.pallas_call(
         functools.partial(pool_kernel, rois),
-        out_shape=(flat, flat, flat),
-        in_specs=[SMEM, SMEM, SMEM, VMEM, VMEM, ANY, ANY, ANY, ANY],
+        out_shape=(flat, flat, jax.ShapeDtypeStruct((8, LANES), jnp.float32)),
+        in_specs=[SMEM, SMEM, SMEM, ANY, ANY, ANY, ANY],
         out_specs=(VMEM, VMEM, VMEM),
         scratch_shapes=[
             pltpu.VMEM((channels + 16, PADDED * LANES), jnp.bfloat16),
@@ -383,7 +406,7 @@
         ],
         compiler_params=pltpu.CompilerParams(vmem_limit_bytes=LIMIT),
         name="pool",
-    )(floats, ints, order, stats, shift, *planes)
+    )(floats, ints, order, *planes)
 
 
 def unpool_maps(floats, ints, order, base, slope, grads, planes, rois):
@@ -476,14 +499,13 @@
         roi_level,
     )
 
-    def twice(vector):
-        return jnp.concatenate([vector, vector])[None]
-
-    pooled, centred, weight = pool_maps(
-        floats, ints, order,
-        jnp.concatenate([twice(mean), twice(scale), jnp.zeros((6, LANES), jnp.float32)]),
-        twice(norm_bias), planes, rois
-    )
+    centred, weight, at_home = pool_maps(floats, ints, order, planes, rois)
+    times = WIDE // channels
+    weight = weight.astype(jnp.float32)
+    centred = centred.astype(jnp.float32) / jnp.tile(at_home[2, :channels], times)
+    centred = centred + weight * jnp.tile(at_home[1, :channels] - mean, times)
+    pooled = centred * jnp.tile(scale, times) + weight * jnp.tile(norm_bias, times)
+    pooled = pooled.astype(jnp.bfloat16)
 
     partial_six = jnp.dot(pooled, wide, preferred_element_type=jnp.float32).astype(jnp.bfloat16)
     pre_six = lax.psum_scatter(partial_six, "col", scatter_dimension=0, tiled=True)
@@ -721,99 +743,70 @@
         self.passed.wait()
 
 
-def stats_kernel(
-    rows, pixels, facts, small, p2, p3, p4, p5, out, small_out,
-    maps, slots, sems, sends, recvs, small_sends, small_recvs,
+def gather_small_kernel(
+    rows, cols, pixels, mine, norms, at_home, out, stats,
+    slots, sends, recvs, x_sends, x_recvs, s_sends, s_recvs, sem,
 ):
-    row = lax.axis_index("roi")
-    depth = rows // 2
+    row, col = lax.axis_index("roi"), lax.axis_index("col")
+    depth, channels = rows // 2, LANES // 2
     plane, side = lax.div(row, 2), lax.rem(row, 2)
-    channels = maps.shape[0]
-    planes = (p2, p3, p4, p5)
-    pieces = [(level, at) for level in range(4) for at in range(4 if level == 0 else 1)]
     greet("roi", rows)
-
-    def fetch(index):
-        level, at = pieces[index]
-        cells = TILES[level] * LANES // (4 if level == 0 else 1)
-        return pltpu.make_async_copy(
-            planes[level].at[0, :, pl.ds(at * cells, cells)],
-            maps.at[:, pl.ds(FIRST[level] * LANES + at * cells, cells)],
-            sems.at[index],
-        )
-
-    for index in range(len(pieces)):
-        fetch(index).start()
-    small_out[row] = small[...]
+    greet("col", cols)
+    slots[row] = jnp.concatenate([at_home[:1], norms[1:2], at_home[2:]], axis=0)
+    own = pltpu.make_async_copy(mine, out.at[col, plane, side], sem)
+    own.start()
+    own.wait()
+    met(rows + cols - 2)
+    sums = share(slots, "roi", rows, s_sends, s_recvs)
     along = [
-        remote(small, small_out.at[row], small_sends, small_recvs, step - 1, "roi",
+        remote(mine, out.at[col, plane, side], x_sends, x_recvs, step - 1, "roi",
                lax.rem(plane + step, depth) * 2 + side)
         for step in range(1, depth)
     ]
     across = []
     for step in range(depth):
-        block = small_out.at[lax.rem(plane + depth - step, depth) * 2 + side]
+        block = out.at[col, lax.rem(plane + depth - step, depth), side]
         across.append(
-            remote(block, block, small_sends, small_recvs, depth - 1 + step, "roi",
-                   row + 1 - 2 * side)
-        )
-    met(rows - 1)
+            remote(block, block, x_sends, x_recvs, depth - 1 + step, "roi", row + 1 - 2 * side)
+        )
     for copy in along:
         copy.start()
     across[0].start()
-
-    def add(at, carry):
-        one, two = carry
-        for part in range(4):
-            lanes = pl.ds(pl.multiple_of((at * 4 + part) * LANES, LANES), LANES)
-            value = maps[:, lanes].astype(jnp.float32)
-            one, two = one + value, two + value * value
-        return one, two
-
-    carry = (jnp.zeros((channels, LANES), jnp.float32),) * 2
-    for index, (level, at) in enumerate(pieces):
-        tiles = TILES[level] // (4 if level == 0 else 1)
-        start = FIRST[level] + at * tiles
-        fetch(index).wait()
-        carry = lax.fori_loop(start // 4, (start + tiles) // 4, add, carry)
-    sums = [jnp.sum(item.T, axis=0, keepdims=True) for item in carry]
-    slots[row] = jnp.concatenate(
-        [jnp.concatenate(sums, axis=1), facts[1:2], jnp.zeros((6, LANES), jnp.float32)], axis=0
-    )
-    copies = share(slots, "roi", rows, sends, recvs)
     for step in range(1, depth):
         along[step - 1].wait_recv()
         across[step].start()
-    for copy in copies:
+    relays = [
+        Relay(lambda at: out.at[at, :, side], sends, recvs, 0),
+        Relay(lambda at: out.at[at, :, 1 - side], sends, recvs, 3),
+    ]
+    relays[0].start()
+    for copy in across:
+        copy.wait_recv()
+    relays[1].start()
+    for copy in sums:
         copy.wait()
     total = slots[0]
     for at in range(1, rows):
         total = total + slots[at]
     turned = pltpu.roll(total, channels, 1)
     low = lax.broadcasted_iota(jnp.int32, total.shape, 1) < channels
-    mean = jnp.where(low, total, turned) / pixels
-    inv_std = lax.rsqrt(jnp.where(low, turned, total) / pixels - mean * mean + EPSILON)
-    scale = facts[...] * inv_std
-    out[...] = jnp.concatenate(
-        [mean[:1], scale[:1], inv_std[:1], total[1:2], jnp.zeros((4, LANES), jnp.float32)], axis=0
-    )
-    for copy in along:
+    mean = (jnp.where(low, total, turned) / pixels)[:1]
+    square = (jnp.where(low, turned, total) / pixels)[:1]
+    inv_std = lax.rsqrt(square - mean * mean + EPSILON)
+    scale = norms[:1] * inv_std
+    spread = 1.0 / at_home[2:3]
+    offset = at_home[1:2] - mean
+    stats[...] = jnp.concatenate(
+        [mean, scale, inv_std, total[1:2], scale * spread, scale * offset + norms[2:3],
+         spread, offset],
+        axis=0,
+    )
+    for relay in relays:
+        relay.forward()
+    for relay in relays:
+        relay.wait()
+    for copy in along + across:
         copy.wait_send()
-    for copy in across:
-        copy.wait()
-
-
-def gather_small_kernel(cols, mine, out, sends, recvs, sem):
-    col = lax.axis_index("col")
-    greet("col", cols)
-    own = pltpu.make_async_copy(mine, out.at[col], sem)
-    own.start()
-    own.wait()
-    met(cols - 1)
-    relay = Relay(lambda at: out.at[at], sends, recvs, 0)
-    relay.start()
-    relay.forward()
-    relay.wait()
 
 
 def place_wide(pieces, wide, sems, rows, cols):
@@ -851,20 +844,28 @@
 
 
 def head_kernel(
-    rows, cols, classes, boxes, facts, score_bias, pooled_in, small_in, pieces,
-    g6_all, g7_out, hid6_out, hid7_out, gs_out, scores_out, losses_out,
-    pooled, small, wide, mine, taken, in_sems, sems, sends, recvs, relay_sends, relay_recvs,
+    rows, cols, classes, boxes, facts, score_bias, stats, centred_in, weight_in, small_in, pieces,
+    pooled, g6_all, g7_out, hid6_out, hid7_out, gs_out, scores_out, losses_out,
+    centred, weight, small, wide, mine, taken, in_sems, sems, sends, recvs, relay_sends, relay_recvs,
 ):
     me = lax.axis_index("col")
     rois, hidden = g6_all.shape
     quarter, piece = rois // cols, hidden // cols
     greet("col", cols)
-    pooled_copy = pltpu.make_async_copy(pooled_in, pooled, in_sems.at[0])
-    small_copy = pltpu.make_async_copy(small_in, small, in_sems.at[1])
-    pooled_copy.start()
+    centred_copy = pltpu.make_async_copy(centred_in, centred, in_sems.at[0])
+    weight_copy = pltpu.make_async_copy(weight_in, weight, in_sems.at[1])
+    small_copy = pltpu.make_async_copy(small_in, small, in_sems.at[2])
+    centred_copy.start()
+    weight_copy.start()
     blocks = place_wide(pieces, wide, sems, rows, cols)
     small_copy.start()
-    pooled_copy.wait()
+    centred_copy.wait()
+    weight_copy.wait()
+    for at in range(len(USED)):
+        lanes = slice(at * LANES, (at + 1) * LANES)
+        value = centred[:, lanes].astype(jnp.float32) * stats[4:5]
+        value = value + weight[:, lanes].astype(jnp.float32) * stats[5:6]
+        pooled[:, lanes] = value.astype(jnp.bfloat16)
     met(cols - 1)
 
     def sending(part, step):
@@ -926,7 +927,8 @@
     hid7_out[...] = hidden_seven
     scores = jnp.dot(hidden_seven, head, preferred_element_type=jnp.float32) + score_bias[...]
     scores_out[...] = scores
-    targets, onehot, weights = facts[0], facts[1], facts[2]
+    loss_scale = float(rois * rows) / stats[3:4, :1]
+    targets, onehot, weights = facts[0], facts[1], facts[2] * loss_scale
     is_class = lane < classes
     top = jnp.max(jnp.where(is_class, scores, -jnp.inf), axis=1, keepdims=True)
     powers = jnp.where(is_class, jnp.exp(jnp.where(is_class, scores - top, 0.0)), 0.0)
@@ -1134,10 +1136,9 @@
     nothing = jnp.zeros((8, LANES), jnp.float32)
     gain, shift = lax.fori_loop(0, len(USED) // 2, step, (nothing, nothing))
     low = lax.broadcasted_iota(jnp.int32, (8, LANES), 1) < channels
-    both = jnp.where(
-        low, gain + pltpu.roll(gain, channels, 1), shift + pltpu.roll(shift, channels, 1)
-    )
-    both = jnp.sum(both, axis=0, keepdims=True)
+    gain = jnp.sum(gain + pltpu.roll(gain, channels, 1), axis=0, keepdims=True)
+    shift = jnp.sum(shift + pltpu.roll(shift, channels, 1), axis=0, keepdims=True)
+    both = jnp.where(low[:1], stats[6:7] * gain + stats[7:8] * shift, shift)
     lines = [both] + bias_rows + [losses[2:3], losses[:2]]
     count = 1 + len(bias_rows) + 3
     lines.append(jnp.zeros((16 - count, LANES), jnp.float32))
@@ -1157,7 +1158,7 @@
     base[...] = jnp.broadcast_to(base_row[:, :channels], (LANES, channels)).T
 
 
-def deliver_kernel(rows, cols, few, term, out, held, taken, half, sems, sends, recvs):
+def deliver_kernel(rows, cols, few, term, taken, held, sems, sends, recvs):
     row, col = lax.axis_index("roi"), lax.axis_index("col")
     plane, side = lax.div(row, 2), lax.rem(row, 2)
     chip, core = lax.div(col, 2), lax.rem(col, 2)
@@ -1236,15 +1237,6 @@
         def _():
             along(held, chunk).wait_recv()
 
-        for index in range(chunk * size, (chunk + 1) * size):
-            slot = KEPT[index]
-            place = pl.ds(slot // 2 % 7 * 7 + slot // 14 + 4 * (slot % 2), few, stride=49)
-            for part in range(out.shape[1] // LANES):
-                half[part, place, :] = taken[
-                    index * few : (index + 1) * few, part * LANES : (part + 1) * LANES
-                ].astype(jnp.float32)
-    for part in range(out.shape[1] // LANES):
-        out[:, part * LANES : (part + 1) * LANES] = half[part]
 
     @pl.when(crossing)
     def _():
@@ -1255,6 +1247,23 @@
     def _():
         for at in range(count):
             along(held, at).wait_send()
+
+
+def restore_kernel(few, classes, boxes, taken, term, out, deep, scores, deltas, half):
+    for part in range(out.shape[1] // LANES):
+        lanes = slice(part * LANES, (part + 1) * LANES)
+        for index, slot in enumerate(KEPT):
+            place = pl.ds(slot // 2 % 7 * 7 + slot // 14 + 4 * (slot % 2), few, stride=49)
+            half[part, place, :] = taken[index * few : (index + 1) * few, lanes].astype(
+                jnp.float32
+            )
+        out[:, lanes] = half[part]
+    rows = deep.shape[0]
+    kept = out.shape[0]
+    deep[...] = term[kept : kept + rows, :].astype(jnp.float32)
+    head = term[kept + rows :, :LANES].astype(jnp.float32)
+    scores[...] = head[:, :classes]
+    deltas[...] = pltpu.roll(head, LANES - classes, 1)[:, :boxes]
 
 
 def unpool_all_kernel(
@@ -1337,54 +1346,39 @@
     return jax.ShapeDtypeStruct(shape, dtype)
 
 
-def statistics(facts, small, planes, rows, pixels):
-    channels = planes[0].shape[1]
-    moves = rows // 2 - 1 + rows // 2
-    return pl.pallas_call(
-        functools.partial(stats_kernel, rows, pixels),
+def gather_small(mine, norms, at_home, rows, cols, pixels):
+    out, stats = pl.pallas_call(
+        functools.partial(gather_small_kernel, rows, cols, pixels),
         out_shape=(
+            shaped((cols, rows // 2, 2) + mine.shape, mine.dtype),
             shaped((8, LANES), jnp.float32),
-            shaped((rows,) + small.shape, small.dtype),
         ),
-        in_specs=[VMEM, VMEM, ANY, ANY, ANY, ANY],
+        in_specs=[VMEM] * 3,
         out_specs=(VMEM, VMEM),
         scratch_shapes=[
-            pltpu.VMEM((channels, ALL_TILES * LANES), jnp.bfloat16),
             pltpu.VMEM((rows, 8, LANES), jnp.float32),
-            pltpu.SemaphoreType.DMA((7,)),
+            pltpu.SemaphoreType.DMA((6,)),
+            pltpu.SemaphoreType.DMA((6,)),
             pltpu.SemaphoreType.DMA((rows - 1,)),
             pltpu.SemaphoreType.DMA((rows - 1,)),
-            pltpu.SemaphoreType.DMA((moves,)),
-            pltpu.SemaphoreType.DMA((moves,)),
-        ],
-        compiler_params=comm_params(0),
-        name="statistics",
-    )(facts, small, *planes)
-
-
-def gather_small(mine, cols):
-    return pl.pallas_call(
-        functools.partial(gather_small_kernel, cols),
-        out_shape=shaped((cols,) + mine.shape, mine.dtype),
-        in_specs=[VMEM],
-        out_specs=VMEM,
-        scratch_shapes=[
-            pltpu.SemaphoreType.DMA((3,)),
-            pltpu.SemaphoreType.DMA((3,)),
+            pltpu.SemaphoreType.DMA((rows - 1,)),
+            pltpu.SemaphoreType.DMA((rows - 1,)),
             pltpu.SemaphoreType.DMA,
         ],
         compiler_params=comm_params(1),
         name="gather_small",
-    )(mine)
-
-
-def run_head(pooled, facts, score_bias, small, pieces, rows, cols, classes, boxes):
-    rois, channels = pooled.shape[0], LANES // 2
+    )(mine, norms, at_home)
+    return out.reshape((cols, rows) + mine.shape), stats
+
+
+def run_head(centred, weight, stats, facts, score_bias, small, pieces, rows, cols, classes, boxes):
+    rois, channels = centred.shape[0], LANES // 2
     quarter, hidden = rois // cols, pieces.shape[3] * cols
     bf16, f32 = jnp.bfloat16, jnp.float32
     return pl.pallas_call(
         functools.partial(head_kernel, rows, cols, classes, boxes),
         out_shape=(
+            shaped(centred.shape, bf16),
             shaped((rois, hidden), bf16),
             shaped((quarter, hidden), bf16),
             shaped((quarter, hidden), bf16),
@@ -1393,15 +1387,16 @@
             shaped((quarter, LANES), f32),
             shaped((8, LANES), f32),
         ),
-        in_specs=[VMEM, VMEM, ANY, ANY, ANY],
-        out_specs=(VMEM,) * 7,
+        in_specs=[VMEM, VMEM, VMEM, ANY, ANY, ANY, ANY],
+        out_specs=(VMEM,) * 8,
         scratch_shapes=[
-            pltpu.VMEM(pooled.shape, bf16),
+            pltpu.VMEM(centred.shape, bf16),
+            pltpu.VMEM(centred.shape, bf16),
             pltpu.VMEM(small.shape, bf16),
             pltpu.VMEM((2 * len(USED), channels, hidden), bf16),
             pltpu.VMEM((cols, quarter, hidden), bf16),
             pltpu.VMEM((cols - 1, quarter, hidden), bf16),
-            pltpu.SemaphoreType.DMA((2,)),
+            pltpu.SemaphoreType.DMA((3,)),
             pltpu.SemaphoreType.DMA((rows, 8)),
             pltpu.SemaphoreType.DMA((cols - 1, cols)),
             pltpu.SemaphoreType.DMA((cols - 1, cols)),
@@ -1410,7 +1405,7 @@
         ],
         compiler_params=comm_params(2),
         name="head",
-    )(facts, score_bias, pooled, small, pieces)
+    )(facts, score_bias, stats, centred, weight, small, pieces)
 
 
 def wide_grads(pooled, g6_all, g7, hid6, hid7, gs, losses, rows, cols):
@@ -1473,13 +1468,11 @@
     piece, kept = term.shape[1], len(KEPT) * few
     return pl.pallas_call(
         functools.partial(deliver_kernel, rows, cols, few),
-        out_shape=shaped((kept, piece), jnp.float32),
+        out_shape=shaped((kept, piece), term.dtype),
         in_specs=[ANY],
         out_specs=VMEM,
         scratch_shapes=[
             pltpu.VMEM((kept, piece), term.dtype),
-            pltpu.VMEM((kept, piece), term.dtype),
-            pltpu.VMEM((piece // LANES, kept, LANES), jnp.float32),
             pltpu.SemaphoreType.DMA((7,)),
             pltpu.SemaphoreType.DMA((2, 7)),
             pltpu.SemaphoreType.DMA((2, 7)),
@@ -1487,6 +1480,25 @@
         compiler_params=comm_params(5),
         name="deliver",
     )(term)
+
+
+def restore(taken, term, few, deep_rows, per, classes, boxes):
+    kept, piece = taken.shape
+    f32 = jnp.float32
+    return pl.pallas_call(
+        functools.partial(restore_kernel, few, classes, boxes),
+        out_shape=(
+            shaped((kept, piece), f32),
+            shaped((deep_rows, piece), f32),
+            shaped((per, classes), f32),
+            shaped((per, boxes), f32),
+        ),
+        in_specs=[VMEM, VMEM],
+        out_specs=(VMEM,) * 4,
+        scratch_shapes=[pltpu.VMEM((piece // LANES, kept, LANES), f32)],
+        compiler_params=pltpu.CompilerParams(vmem_limit_bytes=LIMIT),
+        name="restore",
+    )(taken, term)
 
 
 def targets_of(mine_boxes, mine_goals):
@@ -1575,11 +1587,9 @@
         return jnp.concatenate([vector, vector])[None]
 
     count = jnp.sum(valid.astype(f32))
-    norm_facts = jnp.concatenate(
-        [twice(norm_gain), jnp.full((1, LANES), count), jnp.zeros((6, LANES), f32)]
-    )
-    stats, small = statistics(norm_facts, small, planes, rows, float(pixels))
-    valid_total = stats[3, 0]
+    norms = jnp.concatenate(
+        [twice(norm_gain), jnp.full((1, LANES), count), twice(norm_bias), jnp.zeros((5, LANES), f32)]
+    )
 
     picks = roi_image[None, :] == jnp.arange(4, dtype=jnp.int32)[:, None]
     shift_x = jnp.sum(jnp.where(picks, canvas_offsets[0][:, None], 0), axis=0)
@@ -1591,11 +1601,9 @@
         (roi_boxes[3] + shift_y).astype(f32),
         roi_level,
     )
-    block = lax.optimization_barrier((block, stats, floats, order))[0]
+    block = lax.optimization_barrier((block, floats, order))[0]
     pieces = lax.all_gather(block, "roi", axis=0, axis_index_groups=[ring])
-    pooled, centred, weight = pool_maps(
-        floats, ints, order, stats, twice(norm_bias), planes, rois
-    )
+    centred, weight, at_home = pool_maps(floats, ints, order, planes, rois)
 
     quarter = rois // cols
     first_row = lax.axis_index("col") * quarter
@@ -1604,15 +1612,13 @@
     mine_boxes = lax.dynamic_slice_in_dim(roi_boxes, first_row, quarter, axis=1).astype(f32)
     mine_goals = lax.dynamic_slice_in_dim(target_boxes, first_row, quarter, axis=1).astype(f32)
     foreground = mine_valid * (mine_labels > 0).astype(f32)
-    loss_scale = rois * rows / valid_total
     lane = jnp.arange(LANES, dtype=jnp.int32)[None, :]
     after = LANES - classes - boxes
     facts = jnp.stack(
         [
             jnp.pad(targets_of(mine_boxes, mine_goals), ((0, 0), (classes, after))),
             (mine_labels[:, None] == lane).astype(f32),
-            loss_scale
-            * jnp.where(
+            jnp.where(
                 lane < classes,
                 mine_valid[:, None],
                 jnp.where(lane < classes + boxes, foreground[:, None], 0.0),
@@ -1620,10 +1626,10 @@
         ]
     )
     score_bias = jnp.pad(jnp.concatenate([cls_bias, box_bias]), (0, after))[None]
-    small, facts, score_bias, _ = lax.optimization_barrier((small, facts, score_bias, pooled))
-    small = gather_small(small, cols)
-    g6_all, g7, hid6, hid7, gs, scores, losses = run_head(
-        pooled, facts, score_bias, small, pieces, rows, cols, classes, boxes
+    small, facts, score_bias, _ = lax.optimization_barrier((small, facts, score_bias, at_home))
+    small, stats = gather_small(small, norms, at_home, rows, cols, float(pixels))
+    pooled, g6_all, g7, hid6, hid7, gs, scores, losses = run_head(
+        centred, weight, stats, facts, score_bias, small, pieces, rows, cols, classes, boxes
     )
     decoded = decode(mine_boxes, scores[:, classes : classes + boxes])
 
@@ -1644,15 +1650,9 @@
         piece,
     )
     term = lax.optimization_barrier((term, input_grads[3]))[0]
-    fc6_weight_grad = deliver(term, rows, cols, few)
-    kept = len(KEPT) * few
-    deep_rows = fc7_weight.shape[0]
-    extra = term[kept:].astype(f32)
-    fc7_weight_grad = extra[:deep_rows]
-    head_grad = extra[deep_rows:]
-    cls_weight_grad = head_grad[:, :classes]
-    box_weight_grad = head_grad[:, classes : classes + boxes]
-
+    fc6_weight_grad, fc7_weight_grad, cls_weight_grad, box_weight_grad = restore(
+        deliver(term, rows, cols, few), term, few, fc7_weight.shape[0], per, classes, boxes
+    )
     (
         norm_gain_grad, norm_bias_grad, fc6_bias_grad, fc7_bias_grad, class_bias_grad,
         box_bias_grad, cls_loss, box_loss,

time: 284 us -> 281 us (0.989)
  waiting for transfers between devices: 3.78 us -> 13.9 us
  Pallas kernels: 236 us -> 230 us
  local copies, waits for them, and re-layouts: 17 us -> 12.5 us
    ppermute x1, waiting for transfers between devices: 0.01 us -> 11.4 us  [local_near(): block = lax.ppermute(block, ('roi', 'col'), pairs)]
    pallas_call x2, Pallas kernels: 47.4 us -> 41.2 us  [the longest x1 38.4 us: gather_small(): pl.pallas_call(functools.partial(gather_small_kernel, rows, cols, pixels)...]
  transfers between devices with their start and end apart: 3 -> 3, of which waited for: 1 -> 2; matrix products, arithmetic and copies ran while one was open for 6% -> 5% of each run, Pallas kernels for 59% -> 56%
where the time goes in v5:
time: 281 us
  Pallas kernels  230 us (82%)
  between operations  14.5 us (5%)
  waiting for transfers between devices  13.9 us (5%)
  local copies, waits for them, and re-layouts  12.5 us (4%)
  other arithmetic  7.23 us (3%)
  starting transfers between devices  2.95 us (1%)
    pallas_call x1, Pallas kernels, unpool_all(): pl.pallas_call(functools.partial(unpool_all_kernel, rois, rows, cols, cla...  54.9 us
    pallas_call x1, Pallas kernels, pool_maps(): pl.pallas_call(functools.partial(pool_kernel, rois), out_shape=(flat, fla...  45.1 us
    pallas_call x1, Pallas kernels, gather_small(): pl.pallas_call(functools.partial(gather_small_kernel, rows, cols, pixels)...  38.4 us
    pallas_call x1, Pallas kernels, run_head(): pl.pallas_call(functools.partial(head_kernel, rows, cols, classes, boxes)...  28.2 us
    pallas_call x1, Pallas kernels, deliver(): pl.pallas_call(functools.partial(deliver_kernel, rows, cols, few), out_sh...  25.4 us
    pallas_call x1, Pallas kernels, pool_grads(): pl.pallas_call(functools.partial(pool_grad_kernel, rows, cols, pixels), o...  20.2 us
    pallas_call x1, Pallas kernels, wide_grads(): pl.pallas_call(functools.partial(wide_grad_kernel, rows, cols), out_shape...  15 us
    ppermute x1, waiting for transfers between devices, local_near(): block = lax.ppermute(block, ('roi', 'col'), pairs)  11.4 us
  transfers between devices with their start and end apart: 3, of which 2 were waited for; matrix products, arithmetic and copies ran while one was open for 5% of the time, Pallas kernels for 56%

profile of v5, /device:TPU:12, one launch (start us, length us, event | category | flops | bytes accessed | tf_op | source)
XLA Modules:
  0.0 281.2 jit_solution(3127489862603096254)
XLA Ops:
  7.2 0.0 all-gather.3.cloned.1.call-start
  7.2 1.4 reshape.450
  8.6 0.2 pad.26
  8.8 0.2 reshape.451
  9.1 0.2 copy.81
  9.3 0.2 copy.80
  9.5 0.1 pad_maximum_fusion
  9.6 2.9 %collective-permute-start = (bf16[49,32,256]{2,1,0:T(8,128)(2,1)S(1)}, bf16[49,32,256]{2,1,0:T(8,128)(2,1)S(1)}, u32[]{:S(2)}, u32[]{:S(2)}) collective-permute-start(bf16[49,32,256]{2,1,0:T(8,128)(2,1)S(1)} %pad_maximum_fusion), channel_id=1, source_target_pairs={{0,0},{4,4},{1,16},{5,20},{2,8},{6,12},{3,24},{7,28},{8,9},{12,13}... | collective-permute-start | bytes 2408456 | tf_op jit(solution)/shard_map/ppermute | solution.py:1573
  12.5 0.1 select_reduce_fusion.1
  12.6 0.7 convert_reduce_fusion.2
  13.5 0.7 reshape.443.floats
  14.2 0.2 convert_reduce_fusion
  14.4 0.2 select_reduce_fusion
  14.6 4.5 %concatenate.38.order = s32[406]{0:T(512)} concatenate(s32[384]{0:T(512)S(1)} %select_reduce_fusion, s32[16]{0:T(128)S(1)} %broadcast.303, s32[1]{0:T(128)} %bitcast.2, s32[1]{0:T(128)} %bitcast.3, s32[1]{0:T(128)} %bitcast.4, s32[1]{0:T(128)} %bitcast.5, s32[1]{0:T(128)} %bitcast.6, s32[1]{0:T(128)} %bitcast.7), dimensions={0} | concatenate | bytes 3248 | tf_op jit(solution)/shard_map/concatenate | solution.py:108
  19.2 11.4 %collective-permute-done = bf16[49,32,256]{2,1,0:T(8,128)(2,1)S(1)} collective-permute-done((bf16[49,32,256]{2,1,0:T(8,128)(2,1)S(1)}, bf16[49,32,256]{2,1,0:T(8,128)(2,1)S(1)}, u32[]{:S(2)}, u32[]{:S(2)}) %collective-permute-start) | collective-permute-done | bytes 802848 | tf_op jit(solution)/shard_map/ppermute | solution.py:1573
  30.6 0.9 copy-done
  31.5 0.0 reduce-scatter.2.cloned.1.call-start
  31.5 0.6 convert_reduce_fusion.1
  32.1 0.7 pad.34.clone
  32.9 0.1 pad.36.clone
  32.9 0.1 copy.78
  33.0 0.1 copy.77
  33.2 0.7 reshape.444.ints
  33.9 0.8 dynamic-slice_convert_fusion
  34.7 0.1 copy.79
  34.9 45.1 %pool.1 = (bf16[384,3584]{1,0:T(8,128)(2,1)}, bf16[384,3584]{1,0:T(8,128)(2,1)}, f32[8,128]{1,0:T(8,128)}) custom-call(f32[2744]{0:T(1024)} %reshape.443.floats, s32[2352]{0:T(1024)} %reshape.444.ints, s32[406]{0:T(512)} %concatenate.38.order, bf16[1,64,65536]{2,1,0:T(8,128)(2,1)} %rest_0_.1, bf16[1,64,16384]{2,1,0:T(8,128)(2,1)} %rest_1_.1, ...), custom_call_target="tpu_custom_call" | custom-call | tf_op jit(solution)/shard_map/pool/pallas_call | solution.py:397
  80.1 0.6 fusion.38.score_bias
  80.7 0.8 compare_select_fusion
  81.4 0.1 fusion.10
  81.5 0.1 pad_bitcast_fusion
  81.6 0.6 maximum_maximum_fusion
  82.2 0.1 fusion.2
  82.3 0.1 select_select_fusion
  82.4 0.7 pad_maximum_fusion.1.facts
  83.1 0.1 maximum_bitcast_fusion
  83.2 0.7 maximum_maximum_fusion.1.norms
  83.8 38.4 %gather_small.1 = (bf16[4,4,2,5,32,256]{5,4,3,2,1,0:T(8,128)(2,1)}, f32[8,128]{1,0:T(8,128)}) custom-call(bf16[5,32,256]{2,1,0:T(8,128)(2,1)} %bitcast.134, f32[8,128]{1,0:T(8,128)} %maximum_maximum_fusion.1.norms, f32[8,128]{1,0:T(8,128)} %get-tuple-element.58.at_home), custom_call_target="tpu_custom_call" | custom-call | tf_op jit(solution)/shard_map/gather_small/pallas_call | solution.py:1350
  122.3 28.2 %head.1 = (bf16[384,3584]{1,0:T(8,128)(2,1)}, bf16[384,1024]{1,0:T(8,128)(2,1)}, bf16[96,1024]{1,0:T(8,128)(2,1)}, bf16[96,1024]{1,0:T(8,128)(2,1)}, bf16[96,102...) custom-call(f32[3,96,128]{2,1,0:T(8,128)} %pad_maximum_fusion.1.facts, ...), custom_call_target="tpu_custom_call" | custom-call | tf_op jit(solution)/shard_map/head/pallas_call | solution.py:1378
  150.5 15.0 %wide_grads.1 = (bf16[8,1728,256]{2,1,0:T(8,128)(2,1)}, bf16[384,1024]{1,0:T(8,128)(2,1)}, f32[4,8,128]{2,1,0:T(8,128)}) custom-call(bf16[384,3584]{1,0:T(8,128)(2,1)} %get-tuple-element.68.pooled, bf16[384,1024]{1,0:T(8,128)(2,1)} %get-tuple-element.67.g6_all, bf16[96,1024]{1,0:T(8,128)(2,1)} %get-tuple-element.69.g7, ...), custom_call_target="tpu_custom_call" | custom-call | tf_op jit(solution)/shard_map/wide_grads/pallas_call | solution.py:1416
  165.6 0.8 copy-done.1
  166.3 0.2 exponential_reduce_fusion.1
  166.6 20.2 %pool_grads.1 = (bf16[384,3584]{1,0:T(8,128)(2,1)}, f32[16,128]{1,0:T(8,128)}, f32[64,128]{1,0:T(8,128)}, f32[64,128]{1,0:T(8,128)}) custom-call(bf16[384,1024]{1,0:T(8,128)(2,1)} %get-tuple-element.67.g6_all, bf16[384,1024]{1,0:T(8,128)(2,1)} %get-tuple-element.74.g7_all, f32[4,8,128]{2,1,0:T(8,128)} %get-tuple-element.75.losses_all, ...), custom_call_target="tpu_custom_call" | custom-call | tf_op jit(solution)/shard_map/pool_grads/pallas_call | solution.py:1445
  186.8 54.9 %unpool.1 = (f32[1,64,65536]{2,1,0:T(8,128)}, f32[1,64,16384]{2,1,0:T(8,128)}, f32[1,64,4096]{2,1,0:T(8,128)}, f32[1,64,1024]{2,1,0:T(8,128)}, f32[64]{0:T(128)}...) custom-call(f32[2744]{0:T(1024)} %reshape.443.floats, ...), custom_call_target="tpu_custom_call" | custom-call | tf_op jit(solution)/shard_map/unpool/pallas_call | solution.py:1311
  241.8 0.6 maximum_multiply_fusion
  242.3 2.4 reduce-scatter.2.cloned.1.call-done.term
  244.8 25.4 %deliver.1.taken = bf16[1568,256]{1,0:T(8,128)(2,1)} custom-call(bf16[1728,256]{1,0:T(8,128)(2,1)} %reduce-scatter.2.cloned.1.call-done.term), custom_call_target="tpu_custom_call" | custom-call | tf_op jit(solution)/shard_map/deliver/pallas_call | solution.py:1469
  270.2 2.8 restore.1
  273.0 1.4 copy.82
  (64 shorter events, 0.4 us)
Async XLA Ops:
  7.2 115.1 %all-gather.3.cloned.1.call-start = ((), (), s32[]{:S(2)}) async-start(), calls=%async_computation.2 | async-start | bytes 7225344 | tf_op jit(solution)/shard_map/all_gather | solution.py:1605
  9.0 3.5 %copy-start.9 = (s32[2,4]{1,0:T(2,128)S(1)}, s32[2,4]{1,0:T(2,128)}, u32[]{:S(2)}) copy-start(s32[2,4]{1,0:T(2,128)} %param.38) | copy-start | bytes 100
  9.0 3.5 %copy-start.3 = (s32[4,384]{1,0:T(4,128)S(1)}, s32[4,384]{1,0:T(4,128)}, u32[]{:S(2)}) copy-start(s32[4,384]{1,0:T(4,128)} %param.35) | copy-start | bytes 18436
  9.0 3.5 %copy-start.6 = (s32[384]{0:T(512)S(1)}, s32[384]{0:T(512)}, u32[]{:S(2)}) copy-start(s32[384]{0:T(512)} %param.37) | copy-start | bytes 4612
  9.0 3.6 %copy-start.7 = (s32[384]{0:T(512)S(1)}, s32[384]{0:T(512)}, u32[]{:S(2)}) copy-start(s32[384]{0:T(512)} %param.36) | copy-start | bytes 4612
  9.0 22.5 %copy-start.5 = (s32[384]{0:T(512)S(1)}, s32[384]{0:T(512)}, u32[]{:S(2)}) copy-start(s32[384]{0:T(512)} %param.41) | copy-start | bytes 4612
  9.1 23.9 %copy-start.11 = (bf16[32]{0:T(256)(128)(2,1)S(1)}, bf16[32]{0:T(256)(128)(2,1)}, u32[]{:S(2)}) copy-start(bf16[32]{0:T(256)(128)(2,1)} %param.30) | copy-start | bytes 196
  9.1 24.0 %copy-start.8 = (bf16[32,4]{0,1:T(4,128)(2,1)S(1)}, bf16[32,4]{0,1:T(4,128)(2,1)}, u32[]{:S(2)}) copy-start(bf16[32,4]{0,1:T(4,128)(2,1)} %param.33) | copy-start | bytes 772
  9.6 21.0 %collective-permute-start = (bf16[49,32,256]{2,1,0:T(8,128)(2,1)S(1)}, bf16[49,32,256]{2,1,0:T(8,128)(2,1)S(1)}, u32[]{:S(2)}, u32[]{:S(2)}) collective-permute-start(bf16[49,32,256]{2,1,0:T(8,128)(2,1)S(1)} %pad_maximum_fusion), channel_id=1, source_target_pairs={{0,0},{4,4},{1,16},{5,20},{2,8},{6,12},{3,24},{7,28},{8,9},{12,13}... | collective-permute-start | bytes 2408456 | tf_op jit(solution)/shard_map/ppermute | solution.py:1573
  30.6 0.9 copy-start
  31.5 213.3 %reduce-scatter.2.cloned.1.call-start = ((), (), s32[]{:S(2)}) async-start(), calls=%async_computation.1 | async-start | bytes 7962624 | tf_op jit(solution)/shard_map/reduce_scatter | solution.py:1640
  34.8 45.2 %copy-start.14 = (f32[4]{0:T(128)S(1)}, f32[4]{0:T(128)}, u32[]{:S(2)}) copy-start(f32[4]{0:T(128)} %param.34) | copy-start | bytes 52
  34.8 45.2 %copy-start.15 = (f32[81]{0:T(128)S(1)}, f32[81]{0:T(128)}, u32[]{:S(2)}) copy-start(f32[81]{0:T(128)} %param.32) | copy-start | bytes 976
  34.8 46.6 %copy-start.10 = (f32[256]{0:T(256)S(1)}, f32[256]{0:T(256)}, u32[]{:S(2)}) copy-start(f32[256]{0:T(256)} %param.28) | copy-start | bytes 3076
  34.8 46.6 %copy-start.4 = (bf16[32,81]{1,0:T(8,128)(2,1)S(1)}, bf16[32,81]{1,0:T(8,128)(2,1)}, u32[]{:S(2)}) copy-start(bf16[32,81]{1,0:T(8,128)(2,1)} %param.31) | copy-start | bytes 15556
  34.9 46.7 %copy-start.2 = (bf16[128,256]{1,0:T(8,128)(2,1)S(1)}, bf16[128,256]{1,0:T(8,128)(2,1)}, u32[]{:S(2)}) copy-start(bf16[128,256]{1,0:T(8,128)(2,1)} %param.29) | copy-start | bytes 196612
  34.9 48.2 %copy-start.12 = (f32[64]{0:T(128)S(1)}, f32[64]{0:T(128)}, u32[]{:S(2)}) copy-start(f32[64]{0:T(128)} %param.25) | copy-start | bytes 772
  34.9 48.2 %copy-start.13 = (f32[64]{0:T(128)S(1)}, f32[64]{0:T(128)}, u32[]{:S(2)}) copy-start(f32[64]{0:T(128)} %param.26) | copy-start | bytes 772
  165.5 0.8 copy-start.1
Sparse Core Ops, SparseCore 0:
  31.6 79.2 all-gather.2
  165.7 79.0 reduce-scatter.1

commit v6 on v5

--- a/solution.py
+++ b/solution.py
@@ -980,9 +980,9 @@
 
 
 def wide_grad_kernel(
-    rows, cols, pooled, g6_all, g7, hid6, hid7, gs, losses,
+    rows, cols, pooled_in, g6_all, g7, hid6, hid7, gs, losses,
     terms, g7_all, losses_all,
-    hid6_own, buffers, last, extras, head_mine, head_taken, out_sems, sends, recvs,
+    pooled, hid6_own, buffers, last, extras, head_mine, head_taken, in_sem, out_sems, sends, recvs,
 ):
     me = lax.axis_index("col")
     rois, hidden = g6_all.shape
@@ -991,6 +991,8 @@
     few = buffers.shape[2] // 4
     ring = ring_of(rows)
     greet("col", cols)
+    fetch = pltpu.make_async_copy(pooled_in, pooled, in_sem)
+    fetch.start()
 
     def block(at):
         return pl.ds(pl.multiple_of(at * quarter, quarter), quarter)
@@ -1052,6 +1054,7 @@
             put(result, buffers.at[slot], 0, range(4))
             leaving(slot, at).start()
         return carry
+    fetch.wait()
     pairs = LEADING // 8
     lax.fori_loop(0, pairs - 1, step, 0)
     relay.forward()
@@ -1420,15 +1423,17 @@
             shaped((rois, hidden), bf16),
             shaped((cols, 8, LANES), f32),
         ),
-        in_specs=[VMEM] * 7,
+        in_specs=[ANY] + [VMEM] * 6,
         out_specs=(ANY, VMEM, VMEM),
         scratch_shapes=[
+            pltpu.VMEM(pooled.shape, bf16),
             pltpu.VMEM((rois, piece), bf16),
             pltpu.VMEM((2, rows, 4 * few, piece), bf16),
             pltpu.VMEM((rows, (len(KEPT) - LEADING // 8 * 8) * few, piece), bf16),
             pltpu.VMEM((rows, owned + per, piece), bf16),
             pltpu.VMEM((cols, rows, per, LANES), bf16),
             pltpu.VMEM((cols - 1, rows, per, LANES), bf16),
+            pltpu.SemaphoreType.DMA,
             pltpu.SemaphoreType.DMA((4,)),
             pltpu.SemaphoreType.DMA((12,)),
             pltpu.SemaphoreType.DMA((12,)),

time: 281 us -> 281 us (level)
  Pallas kernels: 230 us -> 226 us
  transfers between devices with their start and end apart: 3 -> 3, of which waited for: 2 -> 2; matrix products, arithmetic and copies ran while one was open for 5% -> 5% of each run, Pallas kernels for 56% -> 55%
where the time goes in v6:
time: 281 us; the launch traced here: 279 us
  Pallas kernels  226 us (80%)
  waiting for transfers between devices  16.5 us (6%)
  between operations  14.5 us (5%)
  local copies, waits for them, and re-layouts  12.5 us (4%)
  other arithmetic  7.23 us (3%)
  starting transfers between devices  2.95 us (1%)
    pallas_call x1, Pallas kernels, unpool_all(): pl.pallas_call(functools.partial(unpool_all_kernel, rois, rows, cols, cla...  52.8 us
    pallas_call x1, Pallas kernels, pool_maps(): pl.pallas_call(functools.partial(pool_kernel, rois), out_shape=(flat, fla...  43.7 us
    pallas_call x1, Pallas kernels, gather_small(): pl.pallas_call(functools.partial(gather_small_kernel, rows, cols, pixels)...  37.7 us
    pallas_call x1, Pallas kernels, run_head(): pl.pallas_call(functools.partial(head_kernel, rows, cols, classes, boxes)...  28.3 us
    pallas_call x1, Pallas kernels, deliver(): pl.pallas_call(functools.partial(deliver_kernel, rows, cols, few), out_sh...  25.4 us
    pallas_call x1, Pallas kernels, pool_grads(): pl.pallas_call(functools.partial(pool_grad_kernel, rows, cols, pixels), o...  18.6 us
    pallas_call x1, Pallas kernels, wide_grads(): pl.pallas_call(functools.partial(wide_grad_kernel, rows, cols), out_shape...  16.3 us
    ppermute x1, waiting for transfers between devices, local_near(): block = lax.ppermute(block, ('roi', 'col'), pairs)  11.4 us
  transfers between devices with their start and end apart: 3, of which 2 were waited for; matrix products, arithmetic and copies ran while one was open for 5% of the time, Pallas kernels for 55%

profile of v6, /device:TPU:12, one launch (start us, length us, event | category | flops | bytes accessed | tf_op | source)
XLA Modules:
  0.0 279.3 jit_solution(9422882320297265190)
XLA Ops:
  7.2 0.0 all-gather.3.cloned.1.call-start
  7.2 1.4 reshape.450
  8.6 0.2 pad.26
  8.8 0.2 reshape.451
  9.1 0.2 copy.81
  9.3 0.2 copy.80
  9.5 0.1 pad_maximum_fusion
  9.6 2.9 %collective-permute-start = (bf16[49,32,256]{2,1,0:T(8,128)(2,1)S(1)}, bf16[49,32,256]{2,1,0:T(8,128)(2,1)S(1)}, u32[]{:S(2)}, u32[]{:S(2)}) collective-permute-start(bf16[49,32,256]{2,1,0:T(8,128)(2,1)S(1)} %pad_maximum_fusion), channel_id=1, source_target_pairs={{0,0},{4,4},{1,16},{5,20},{2,8},{6,12},{3,24},{7,28},{8,9},{12,13}... | collective-permute-start | bytes 2408456 | tf_op jit(solution)/shard_map/ppermute | solution.py:1578
  12.5 0.1 select_reduce_fusion.1
  12.6 0.7 convert_reduce_fusion.2
  13.5 0.7 reshape.443.floats
  14.2 0.2 convert_reduce_fusion
  14.4 0.2 select_reduce_fusion
  14.6 4.5 %concatenate.38.order = s32[406]{0:T(512)} concatenate(s32[384]{0:T(512)S(1)} %select_reduce_fusion, s32[16]{0:T(128)S(1)} %broadcast.303, s32[1]{0:T(128)} %bitcast.2, s32[1]{0:T(128)} %bitcast.3, s32[1]{0:T(128)} %bitcast.4, s32[1]{0:T(128)} %bitcast.5, s32[1]{0:T(128)} %bitcast.6, s32[1]{0:T(128)} %bitcast.7), dimensions={0} | concatenate | bytes 3248 | tf_op jit(solution)/shard_map/concatenate | solution.py:108
  19.2 11.4 %collective-permute-done = bf16[49,32,256]{2,1,0:T(8,128)(2,1)S(1)} collective-permute-done((bf16[49,32,256]{2,1,0:T(8,128)(2,1)S(1)}, bf16[49,32,256]{2,1,0:T(8,128)(2,1)S(1)}, u32[]{:S(2)}, u32[]{:S(2)}) %collective-permute-start) | collective-permute-done | bytes 802848 | tf_op jit(solution)/shard_map/ppermute | solution.py:1578
  30.6 0.9 copy-done
  31.5 0.0 reduce-scatter.2.cloned.1.call-start
  31.5 0.6 convert_reduce_fusion.1
  32.1 0.7 pad.34.clone
  32.9 0.1 pad.36.clone
  32.9 0.1 copy.78
  33.0 0.1 copy.77
  33.2 0.7 reshape.444.ints
  33.9 0.8 dynamic-slice_convert_fusion
  34.7 0.1 copy.79
  34.9 43.7 %pool.1 = (bf16[384,3584]{1,0:T(8,128)(2,1)}, bf16[384,3584]{1,0:T(8,128)(2,1)}, f32[8,128]{1,0:T(8,128)}) custom-call(f32[2744]{0:T(1024)} %reshape.443.floats, s32[2352]{0:T(1024)} %reshape.444.ints, s32[406]{0:T(512)} %concatenate.38.order, bf16[1,64,65536]{2,1,0:T(8,128)(2,1)} %rest_0_.1, bf16[1,64,16384]{2,1,0:T(8,128)(2,1)} %rest_1_.1, ...), custom_call_target="tpu_custom_call" | custom-call | tf_op jit(solution)/shard_map/pool/pallas_call | solution.py:397
  78.6 0.6 fusion.38.score_bias
  79.2 0.8 compare_select_fusion
  80.0 0.1 fusion.10
  80.1 0.1 pad_bitcast_fusion
  80.2 0.6 maximum_maximum_fusion
  80.8 0.1 fusion.2
  80.9 0.1 select_select_fusion
  81.0 0.7 pad_maximum_fusion.1.facts
  81.7 0.1 maximum_bitcast_fusion
  81.7 0.7 maximum_maximum_fusion.1.norms
  82.4 37.7 %gather_small.1 = (bf16[4,4,2,5,32,256]{5,4,3,2,1,0:T(8,128)(2,1)}, f32[8,128]{1,0:T(8,128)}) custom-call(bf16[5,32,256]{2,1,0:T(8,128)(2,1)} %bitcast.134, f32[8,128]{1,0:T(8,128)} %maximum_maximum_fusion.1.norms, f32[8,128]{1,0:T(8,128)} %get-tuple-element.58.at_home), custom_call_target="tpu_custom_call" | custom-call | tf_op jit(solution)/shard_map/gather_small/pallas_call | solution.py:1353
  120.1 28.3 %head.1 = (bf16[384,3584]{1,0:T(8,128)(2,1)}, bf16[384,1024]{1,0:T(8,128)(2,1)}, bf16[96,1024]{1,0:T(8,128)(2,1)}, bf16[96,1024]{1,0:T(8,128)(2,1)}, bf16[96,102...) custom-call(f32[3,96,128]{2,1,0:T(8,128)} %pad_maximum_fusion.1.facts, ...), custom_call_target="tpu_custom_call" | custom-call | tf_op jit(solution)/shard_map/head/pallas_call | solution.py:1381
  148.4 16.3 %wide_grads.1 = (bf16[8,1728,256]{2,1,0:T(8,128)(2,1)}, bf16[384,1024]{1,0:T(8,128)(2,1)}, f32[4,8,128]{2,1,0:T(8,128)}) custom-call(bf16[384,3584]{1,0:T(8,128)(2,1)} %get-tuple-element.68.pooled_in, bf16[384,1024]{1,0:T(8,128)(2,1)} %get-tuple-element.67.g6_all, bf16[96,1024]{1,0:T(8,128)(2,1)} %get-tuple-element.69.g7, ...), custom_call_target="tpu_custom_call" | custom-call | tf_op jit(solution)/shard_map/wide_grads/pallas_call | solution.py:1419
  164.7 0.8 copy-done.1
  165.5 0.2 exponential_reduce_fusion.1
  165.8 18.6 %pool_grads.1 = (bf16[384,3584]{1,0:T(8,128)(2,1)}, f32[16,128]{1,0:T(8,128)}, f32[64,128]{1,0:T(8,128)}, f32[64,128]{1,0:T(8,128)}) custom-call(bf16[384,1024]{1,0:T(8,128)(2,1)} %get-tuple-element.67.g6_all, bf16[384,1024]{1,0:T(8,128)(2,1)} %get-tuple-element.74.g7_all, f32[4,8,128]{2,1,0:T(8,128)} %get-tuple-element.75.losses_all, ...), custom_call_target="tpu_custom_call" | custom-call | tf_op jit(solution)/shard_map/pool_grads/pallas_call | solution.py:1450
  184.3 52.8 %unpool.1 = (f32[1,64,65536]{2,1,0:T(8,128)}, f32[1,64,16384]{2,1,0:T(8,128)}, f32[1,64,4096]{2,1,0:T(8,128)}, f32[1,64,1024]{2,1,0:T(8,128)}, f32[64]{0:T(128)}...) custom-call(f32[2744]{0:T(1024)} %reshape.443.floats, ...), custom_call_target="tpu_custom_call" | custom-call | tf_op jit(solution)/shard_map/unpool/pallas_call | solution.py:1314
  237.2 0.6 maximum_multiply_fusion
  237.8 5.1 %reduce-scatter.2.cloned.1.call-done.term = bf16[1728,256]{1,0:T(8,128)(2,1)} async-done(((bf16[13824,256]{1,0:T(8,128)(2,1)}), bf16[1728,256]{1,0:T(8,128)(2,1)}) %reduce-scatter.2.cloned.1.call-update) | async-done | bytes 884752 | tf_op jit(solution)/shard_map/reduce_scatter | solution.py:1645
  242.8 25.4 %deliver.1.taken = bf16[1568,256]{1,0:T(8,128)(2,1)} custom-call(bf16[1728,256]{1,0:T(8,128)(2,1)} %reduce-scatter.2.cloned.1.call-done.term), custom_call_target="tpu_custom_call" | custom-call | tf_op jit(solution)/shard_map/deliver/pallas_call | solution.py:1474
  268.3 2.8 %restore.1 = (f32[1568,256]{1,0:T(8,128)}, f32[128,256]{1,0:T(8,128)}, f32[32,81]{1,0:T(8,128)}, f32[32,4]{1,0:T(8,128)}) custom-call(bf16[1568,256]{1,0:T(8,128)(2,1)} %deliver.1.taken, bf16[1728,256]{1,0:T(8,128)(2,1)} %reduce-scatter.2.cloned.1.call-done.term), custom_call_target="tpu_custom_call" | custom-call | tf_op jit(solution)/shard_map/restore/pallas_call | solution.py:1493
  271.1 1.4 copy.82
  (64 shorter events, 0.4 us)
Async XLA Ops:
  7.2 112.9 %all-gather.3.cloned.1.call-start = ((), (), s32[]{:S(2)}) async-start(), calls=%async_computation.2 | async-start | bytes 7225344 | tf_op jit(solution)/shard_map/all_gather | solution.py:1610
  9.0 3.5 %copy-start.9 = (s32[2,4]{1,0:T(2,128)S(1)}, s32[2,4]{1,0:T(2,128)}, u32[]{:S(2)}) copy-start(s32[2,4]{1,0:T(2,128)} %param.38) | copy-start | bytes 100
  9.0 3.5 %copy-start.3 = (s32[4,384]{1,0:T(4,128)S(1)}, s32[4,384]{1,0:T(4,128)}, u32[]{:S(2)}) copy-start(s32[4,384]{1,0:T(4,128)} %param.35) | copy-start | bytes 18436
  9.0 3.5 %copy-start.6 = (s32[384]{0:T(512)S(1)}, s32[384]{0:T(512)}, u32[]{:S(2)}) copy-start(s32[384]{0:T(512)} %param.37) | copy-start | bytes 4612
  9.0 3.6 %copy-start.7 = (s32[384]{0:T(512)S(1)}, s32[384]{0:T(512)}, u32[]{:S(2)}) copy-start(s32[384]{0:T(512)} %param.36) | copy-start | bytes 4612
  9.0 22.5 %copy-start.5 = (s32[384]{0:T(512)S(1)}, s32[384]{0:T(512)}, u32[]{:S(2)}) copy-start(s32[384]{0:T(512)} %param.41) | copy-start | bytes 4612
  9.1 23.9 %copy-start.11 = (bf16[32]{0:T(256)(128)(2,1)S(1)}, bf16[32]{0:T(256)(128)(2,1)}, u32[]{:S(2)}) copy-start(bf16[32]{0:T(256)(128)(2,1)} %param.30) | copy-start | bytes 196
  9.1 24.0 %copy-start.8 = (bf16[32,4]{0,1:T(4,128)(2,1)S(1)}, bf16[32,4]{0,1:T(4,128)(2,1)}, u32[]{:S(2)}) copy-start(bf16[32,4]{0,1:T(4,128)(2,1)} %param.33) | copy-start | bytes 772
  9.6 21.0 %collective-permute-start = (bf16[49,32,256]{2,1,0:T(8,128)(2,1)S(1)}, bf16[49,32,256]{2,1,0:T(8,128)(2,1)S(1)}, u32[]{:S(2)}, u32[]{:S(2)}) collective-permute-start(bf16[49,32,256]{2,1,0:T(8,128)(2,1)S(1)} %pad_maximum_fusion), channel_id=1, source_target_pairs={{0,0},{4,4},{1,16},{5,20},{2,8},{6,12},{3,24},{7,28},{8,9},{12,13}... | collective-permute-start | bytes 2408456 | tf_op jit(solution)/shard_map/ppermute | solution.py:1578
  30.6 0.9 copy-start
  31.5 211.4 %reduce-scatter.2.cloned.1.call-start = ((), (), s32[]{:S(2)}) async-start(), calls=%async_computation.1 | async-start | bytes 7962624 | tf_op jit(solution)/shard_map/reduce_scatter | solution.py:1645
  34.8 43.8 %copy-start.14 = (f32[4]{0:T(128)S(1)}, f32[4]{0:T(128)}, u32[]{:S(2)}) copy-start(f32[4]{0:T(128)} %param.34) | copy-start | bytes 52
  34.8 43.8 %copy-start.15 = (f32[81]{0:T(128)S(1)}, f32[81]{0:T(128)}, u32[]{:S(2)}) copy-start(f32[81]{0:T(128)} %param.32) | copy-start | bytes 976
  34.8 45.1 %copy-start.10 = (f32[256]{0:T(256)S(1)}, f32[256]{0:T(256)}, u32[]{:S(2)}) copy-start(f32[256]{0:T(256)} %param.28) | copy-start | bytes 3076
  34.8 45.1 %copy-start.4 = (bf16[32,81]{1,0:T(8,128)(2,1)S(1)}, bf16[32,81]{1,0:T(8,128)(2,1)}, u32[]{:S(2)}) copy-start(bf16[32,81]{1,0:T(8,128)(2,1)} %param.31) | copy-start | bytes 15556
  34.9 45.3 %copy-start.2 = (bf16[128,256]{1,0:T(8,128)(2,1)S(1)}, bf16[128,256]{1,0:T(8,128)(2,1)}, u32[]{:S(2)}) copy-start(bf16[128,256]{1,0:T(8,128)(2,1)} %param.29) | copy-start | bytes 196612
  34.9 46.8 %copy-start.12 = (f32[64]{0:T(128)S(1)}, f32[64]{0:T(128)}, u32[]{:S(2)}) copy-start(f32[64]{0:T(128)} %param.25) | copy-start | bytes 772
  34.9 46.8 %copy-start.13 = (f32[64]{0:T(128)S(1)}, f32[64]{0:T(128)}, u32[]{:S(2)}) copy-start(f32[64]{0:T(128)} %param.26) | copy-start | bytes 772
  164.7 0.8 copy-start.1
Sparse Core Ops, SparseCore 0:
  31.6 79.2 all-gather.2
  164.8 77.9 reduce-scatter.1
